TPU v7x, 256 devices: a whole 4x4x8 slice. The times are simulated.
256 devices in a mesh: dp: 8 (over z), seq: 32 (over y, x, core).
Axes of the slice: x: 4, y: 4, z: 8, core: 2. Of those that a mesh axis runs over, the one named last changes fastest.
Arguments:
- events: bfloat16 [8, 32, 256, 1024], P('dp', 'seq'), may hold values from -6 to 6
- lengths: int32 [8, 4], P('dp'), may hold values from 1 to 32, 64 in all within a row
- weight_in: bfloat16 [1024, 4096], replicated, may hold values from -0.1875 to 0.1875
- weight_out: bfloat16 [1024, 1024], replicated, may hold values from -0.1875 to 0.1875
- cotangent: bfloat16 [8, 32, 256, 1024], P('dp', 'seq'), may hold values from -6 to 6
Outputs:
- layer_out: bfloat16 [8, 32, 256, 1024], P('dp', 'seq')
- event_grads: bfloat16 [8, 32, 256, 1024], P('dp', 'seq')
- weight_key_grad: float32 [1024, 1024], P(('dp', 'seq'))
Inputs may be any that keep to these rules, and one draw needn't show every extreme that they name: lengths[g, u] counts tiles of 128 events; each group's lengths sum to 64 and one of them equals 32.
All inputs are finite; a program needn't handle non-finite values.
Results may differ from a plain program's by a relative error of at most 0.015.
Values may be sent and summed in bfloat16 or wider, within the bound.
No kernel may reach another device: no remote copies, remote signals or barrier semaphores. Data moves between devices by JAX's collectives and lax.ppermute only.
A program may use at most 128 MiB of HBM per device.

v0:
```python
import jax
import jax.numpy as jnp
from jax import lax
from jax.sharding import PartitionSpec as P

HEADS = 8
HEAD = 128
TILE = 128
MOST = 4


EPSILON = 1e-06


def shifted(block, axis, distance):
    devices = range(lax.axis_size(axis))
    route = [(i - distance, i) for i in devices if i - distance in devices]
    return lax.ppermute(block, axis, route)


def for_sending(array):

    def short(part):
        return part.astype(jnp.bfloat16) if part.dtype == jnp.float32 else part

    return jax.tree.map(short, array)


def layer_norm(values):
    centre = jnp.mean(values, axis=-1, keepdims=True)
    centred = values - centre
    spread = jnp.mean(centred * centred, axis=-1, keepdims=True)
    recip = lax.rsqrt(spread + EPSILON)
    return (centred * recip, recip)


def norm_back(upstream, normed_f, recip):
    first = jnp.mean(upstream, axis=-1, keepdims=True)
    second = jnp.mean(upstream * normed_f, axis=-1, keepdims=True)
    return recip * (upstream - first - normed_f * second)


def silu_slope(values):
    sigmoid = jax.nn.sigmoid(values)
    return sigmoid * (1.0 + values * (1.0 - sigmoid))


def tile_history(tile_pos, history_ends):
    return jnp.sum((tile_pos[..., None] >= history_ends).astype(jnp.int32), axis=-1)


def tile_scale(history, group_lengths):
    labels = jnp.arange(group_lengths.shape[0], dtype=jnp.int32)
    picked = jnp.sum(jnp.where(history[..., None] == labels, group_lengths, 0), axis=-1)
    return 1.0 / (picked * TILE).astype(jnp.float32)


def contract_rows(left, right):
    return lax.dot_general(
        left, right, (((0,), (0,)), ((), ())), preferred_element_type=jnp.float32
    )


def contract_cols(left, right):
    return lax.dot_general(
        left, right, (((1,), (1,)), ((), ())), preferred_element_type=jnp.float32
    )


def shards(events, lengths, weight_in, weight_out, cotangent):
    pair_count = lax.axis_size("seq")
    pair_index = lax.axis_index("seq")
    tile_rows = events.shape[2] // 2
    model_width = events.shape[3]
    scale = HEAD ** (-0.5)
    group_lengths = lengths[0]
    history_ends = jnp.cumsum(group_lengths)
    positions = jnp.stack([pair_index, 2 * pair_count - 1 - pair_index])
    offsets = jnp.arange(MOST, dtype=jnp.int32)
    own_history = tile_history(positions, history_ends)
    inverse = tile_scale(own_history, group_lengths)
    key_pos = positions[:, None] - offsets[None, :]
    tile_live = (key_pos >= 0) & (
        tile_history(jnp.maximum(key_pos, 0), history_ends) == own_history[:, None]
    )
    row_ids = jnp.arange(tile_rows, dtype=jnp.int32)
    causal = row_ids[None, :] <= row_ids[:, None]
    row_live = (offsets[:, None, None] > 0) | causal[None]
    live_mask = tile_live[:, None, None, :, None] & jnp.transpose(row_live, (1, 0, 2))[None, None]
    scale_rows = inverse[:, None, None, None, None]
    events_f = events.reshape(2 * tile_rows, model_width).astype(jnp.float32)
    normed_f, recip = layer_norm(events_f)
    normed = normed_f.astype(jnp.bfloat16)
    pre_act = jnp.dot(normed, weight_in, preferred_element_type=jnp.float32)
    projected = jax.nn.silu(pre_act).astype(jnp.bfloat16)
    gate_part = projected[:, :model_width]
    value_part = projected[:, model_width : 2 * model_width]
    query_part = projected[:, 2 * model_width : 3 * model_width]
    key_part = projected[:, 3 * model_width :]
    key_value = jnp.concatenate([key_part, value_part], axis=1).reshape(
        2, tile_rows, 2 * model_width
    )
    windows = [key_value]
    for step in range(1, MOST):
        earlier_block = windows[-1]
        earlier_lower_half = shifted(earlier_block[0], "seq", 1)
        earlier_upper_half = shifted(earlier_block[1], "seq", -1)
        earlier_upper_half = jnp.where(
            pair_index == pair_count - 1, earlier_block[0], earlier_upper_half
        )
        windows.append(jnp.stack([earlier_lower_half, earlier_upper_half]))
    window = jnp.stack(windows)
    key_tiles = window[..., :model_width].reshape(MOST, 2, tile_rows, HEADS, HEAD)
    value_tiles = window[..., model_width:].reshape(MOST, 2, tile_rows, HEADS, HEAD)
    queries = query_part.reshape(2, tile_rows, HEADS, HEAD)
    scores = (
        jnp.einsum("arhd,machd->ahrmc", queries, key_tiles, preferred_element_type=jnp.float32)
        * scale
    )
    attention = (jnp.where(live_mask, jax.nn.silu(scores), 0.0) * scale_rows).astype(jnp.bfloat16)
    attended = jnp.einsum(
        "ahrmc,machd->arhd", attention, value_tiles, preferred_element_type=jnp.float32
    )
    attended = attended.reshape(2 * tile_rows, model_width)
    attended_n, attended_recip = layer_norm(attended)
    gated = (attended_n * gate_part.astype(jnp.float32)).astype(jnp.bfloat16)
    layer_out = (events_f + jnp.dot(gated, weight_out, preferred_element_type=jnp.float32)).astype(
        jnp.bfloat16
    )
    layer_out = layer_out.reshape(events.shape)
    back = cotangent.reshape(2 * tile_rows, model_width)
    d_gated = contract_cols(back, weight_out)
    d_gate = d_gated * attended_n
    d_attended = norm_back(
        d_gated * gate_part.astype(jnp.float32), attended_n, attended_recip
    ).astype(jnp.bfloat16)
    upstream = d_attended.reshape(2, tile_rows, HEADS, HEAD)
    d_weights = jnp.einsum(
        "arhd,machd->ahrmc", upstream, value_tiles, preferred_element_type=jnp.float32
    )
    d_scores = (jnp.where(live_mask, d_weights * silu_slope(scores), 0.0) * scale_rows).astype(
        jnp.bfloat16
    )
    d_query = (
        jnp.einsum("ahrmc,machd->arhd", d_scores, key_tiles, preferred_element_type=jnp.float32)
        * scale
    )
    d_query = d_query.reshape(2 * tile_rows, model_width)
    part_key = (
        jnp.einsum("ahrmc,arhd->machd", d_scores, queries, preferred_element_type=jnp.float32)
        * scale
    )
    part_value = jnp.einsum(
        "ahrmc,arhd->machd", attention, upstream, preferred_element_type=jnp.float32
    )
    partials = jnp.concatenate(
        [
            part_key.reshape(MOST, 2, tile_rows, model_width),
            part_value.reshape(MOST, 2, tile_rows, model_width),
        ],
        axis=3,
    )
    carried = partials[MOST - 1]
    for step in range(MOST - 1, 0, -1):
        lower_half = shifted(for_sending(carried[0]), "seq", -1)
        lower_half = jnp.where(pair_index == pair_count - 1, carried[1], lower_half)
        upper_half = shifted(for_sending(carried[1]), "seq", 1)
        carried = jnp.stack([lower_half, upper_half]) + partials[step - 1]
    d_key = carried[..., :model_width].reshape(2 * tile_rows, model_width)
    d_value = carried[..., model_width:].reshape(2 * tile_rows, model_width)
    d_pre = (
        jnp.concatenate([d_gate, d_value, d_query, d_key], axis=1) * silu_slope(pre_act)
    ).astype(jnp.bfloat16)
    d_normed = contract_cols(d_pre, weight_in)
    event_grads = (back.astype(jnp.float32) + norm_back(d_normed, normed_f, recip)).astype(
        jnp.bfloat16
    )
    event_grads = event_grads.reshape(events.shape)
    key_pre = d_pre[:, 3 * model_width :]
    summed = lax.psum_scatter(
        contract_rows(normed, key_pre), ("dp", "seq"), scatter_dimension=0, tiled=True
    )
    return (layer_out, event_grads, summed)


def solution(mesh):
    return jax.shard_map(
        shards,
        mesh=mesh,
        in_specs=(P("dp", "seq", None, None), P("dp", None), P(), P(), P("dp", "seq", None, None)),
        out_specs=(P("dp", "seq", None, None), P("dp", "seq", None, None), P(("dp", "seq"), None)),
        check_vma=False,
    )
```

profile of v0, /device:TPU:32, one launch (start us, length us, event | category | flops | bytes accessed | tf_op | source)
XLA Modules:
  0.0 463.4 jit_solution(13410020452459424315)
XLA Ops:
  9.9 8.1 %multiply_convert_fusion.2 = (bf16[256,4096]{1,0:T(8,128)(2,1)S(1)}, f32[256,4096]{1,0:T(8,128)}) fusion(bf16[1024,4096]{1,0:T(8,128)(2,1)} %param.7, bf16[1,1,256,1024]{3,2,1,0:T(8,128)(2,1)} %param.5, f32[256]{0:T(256)S(1)} %add_rsqrt_fusion, f32[256]{0:T(256)S(1)} %broadcast_multiply_fusion.5), kind=kOutput, calls=%fused_computation.7 | convolution fusion | flops 2153775104 | bytes 15206400 | tf_op jit(solution)/shard_map/dot_general | solution.py:94
  23.4 1.8 collective-permute-done.1
  26.4 9.3 %collective-permute-start = (bf16[128,2048]{1,0:T(8,128)(2,1)S(1)}, bf16[128,2048]{1,0:T(8,128)(2,1)}, u32[]{:S(2)}, u32[]{:S(2)}) collective-permute-start(bf16[128,2048]{1,0:T(8,128)(2,1)S(1)} %get-tuple-element.8), channel_id=1, source_target_pairs={{0,1},{1,2},{2,3},{3,4},{4,5},{5,6},{6,7},{7,8},{8,9},{9,10},{10,1... | collective-permute-start | bytes 1572872 | tf_op jit(solution)/shard_map/ppermute | solution.py:18
  39.5 3.4 collective-permute-start.2
  46.2 1.4 maximum_bitcast_fusion
  47.6 6.4 %collective-permute-start.4 = (bf16[128,2048]{1,0:T(8,128)(2,1)S(1)}, bf16[128,2048]{1,0:T(8,128)(2,1)S(1)}, u32[]{:S(2)}, u32[]{:S(2)}) collective-permute-start(bf16[128,2048]{1,0:T(8,128)(2,1)S(1)} %collective-permute-done.2), channel_id=1, source_target_pairs={{0,1},{1,2},{2,3},{3,4},{4,5},{5,6},{6,7},{7,8},{8,9},{9,10},{10,1... | collective-permute-start | bytes 1572872 | tf_op jit(solution)/shard_map/ppermute | solution.py:18
  57.6 2.0 copy.58
  59.6 1.9 copy.60
  61.5 4.3 copy.42
  65.9 5.7 %multiply_convert_fusion.1 = (bf16[2,8,128,4,128]{4,2,3,1,0:T(8,128)(2,1)S(1)}, f32[2,8,128,4,128]{4,2,3,1,0:T(8,128)}) fusion(f32[2]{0:T(128)S(1)} %convert_divide_fusion, pred[2,128,4,128]{3,1,2,0:T(8,128)(4,1)S(1)} %broadcast_and_fusion, bf16[2,128,8,128,1]{1,3,4,2,0:T(8,128)(2,1)S(1)} %copy-done.19, bf16[4,2,128,8,128]{2,4,0,3,1:T(8,128)(2,1)} %copy.42), kind=kOutput, calls=%fused_computation.5 | convolution fusion | flops 276824064 | bytes 9043976 | tf_op jit(solution)/shard_map/arhd,machd->ahrmc/dot_general | solution.py:117
  74.4 2.7 fusion.44
  77.0 2.6 fusion.52
  80.2 4.4 convolution_bitcast_fusion
  84.6 2.6 multiply_convert_fusion
  88.5 2.7 multiply_bitcast_fusion
  91.2 5.3 %copy.39 = f32[4,2,128,8,128]{4,3,2,1,0:T(8,128)} copy(f32[4,2,128,8,128]{2,4,0,3,1:T(8,128)} %multiply_bitcast_fusion) | data formatting | bytes 8388608 | tf_op jit(solution)/shard_map/mul | solution.py:150
  96.5 4.9 %reshape.242 = f32[4,2,128,1024]{3,2,1,0:T(8,128)} reshape(f32[4,2,128,8,128]{4,3,2,1,0:T(8,128)} %copy.39) | data formatting | bytes 8388608 | tf_op jit(solution)/shard_map/reshape | solution.py:158
  101.4 5.3 %copy.41 = f32[4,2,128,8,128]{4,3,2,1,0:T(8,128)} copy(f32[4,2,128,8,128]{2,4,0,3,1:T(8,128)} %convolution_bitcast_fusion) | data formatting | bytes 8388608 | tf_op jit(solution)/shard_map/ahrmc,arhd->machd/transpose | solution.py:153
  106.7 4.9 %reshape.243 = f32[4,2,128,1024]{3,2,1,0:T(8,128)} reshape(f32[4,2,128,8,128]{4,3,2,1,0:T(8,128)} %copy.41) | data formatting | bytes 8388608 | tf_op jit(solution)/shard_map/reshape | solution.py:159
  111.6 2.7 constant_dynamic-update-slice_fusion.1
  117.1 8.8 %collective-permute-start.7 = (bf16[128,2048]{1,0:T(8,128)(2,1)S(1)}, bf16[128,2048]{1,0:T(8,128)(2,1)S(1)}, u32[]{:S(2)}, u32[]{:S(2)}) collective-permute-start(bf16[128,2048]{1,0:T(8,128)(2,1)S(1)} %get-tuple-element.10), channel_id=1, source_target_pairs={{0,1},{1,2},{2,3},{3,4},{4,5},{5,6},{6,7},{7,8},{8,9},{9,10},{10,1... | collective-permute-start | bytes 1572872 | tf_op jit(solution)/shard_map/ppermute | solution.py:18
  128.9 9.6 %collective-permute-start.9 = (bf16[128,2048]{1,0:T(8,128)(2,1)S(1)}, bf16[128,2048]{1,0:T(8,128)(2,1)S(1)}, u32[]{:S(2)}, u32[]{:S(2)}) collective-permute-start(bf16[128,2048]{1,0:T(8,128)(2,1)S(1)} %get-tuple-element.20), channel_id=1, source_target_pairs={{0,1},{1,2},{2,3},{3,4},{4,5},{5,6},{6,7},{7,8},{8,9},{9,10},{10,1... | collective-permute-start | bytes 1572872 | tf_op jit(solution)/shard_map/ppermute | solution.py:18
  144.2 10.4 %collective-permute-start.11 = (bf16[128,2048]{1,0:T(8,128)(2,1)}, bf16[128,2048]{1,0:T(8,128)(2,1)}, u32[]{:S(2)}, u32[]{:S(2)}) collective-permute-start(bf16[128,2048]{1,0:T(8,128)(2,1)} %get-tuple-element.18), channel_id=1, source_target_pairs={{0,1},{1,2},{2,3},{3,4},{4,5},{5,6},{6,7},{7,8},{8,9},{9,10},{10,1... | collective-permute-start | bytes 1572872 | tf_op jit(solution)/shard_map/ppermute | solution.py:18
  156.7 1.4 copy.83
  158.1 1.5 select_bitcast_fusion
  160.8 2.0 fusion.1
  163.9 1.4 fusion
  166.8 2.8 fusion.39
  169.7 3.1 fusion.19
  172.8 6.0 %fusion.54 = (f32[256]{0:T(256)S(1)}, f32[256]{0:T(256)S(1)}, f32[256,1024]{1,0:T(8,128)S(1)}) fusion(f32[256]{0:T(256)S(1)} %add_rsqrt_fusion, f32[256]{0:T(256)S(1)} %broadcast_multiply_fusion.5, bf16[1,1,256,1024]{3,2,1,0:T(8,128)(2,1)S(1)} %copy-done.4, bf16[256,4096]{1,0:T(8,128)(2,1)S(1)} %copy-done.16, bf16[1024,4096]{1,0:T(8,128)(2,1)} %param.7), kind=kOutput, calls=%fused_computation.119 | convolution fusion | flops 2149056000 | bytes 12062720 | tf_op jit(solution)/shard_map/dot_general | solution.py:65
  180.0 275.2 %all-reduce.3.cloned.1.call-done = f32[1024,1024]{1,0:T(8,128)} async-done(((f32[1024,1024]{1,0:T(8,128)}), f32[1024,1024]{1,0:T(8,128)}) %all-reduce.3.cloned.1.call-update) | async-done | bytes 4194320
  455.2 1.4 constant_dynamic-slice_fusion
  (121 shorter events, 42.8 us)
Async XLA Ops:
  7.2 67.2 %copy-start = (bf16[1024,1024]{1,0:T(8,128)(2,1)S(1)}, bf16[1024,1024]{1,0:T(8,128)(2,1)}, u32[]{:S(2)}) copy-start(bf16[1024,1024]{1,0:T(8,128)(2,1)} %param.8) | copy-start | bytes 6291460
  7.2 448.0 %all-reduce.3.cloned.1.call-start = ((), (), s32[]{:S(2)}) async-start(), calls=%async_computation | async-start | bytes 8388608
  18.0 4.5 copy-start.22
  21.1 4.1 collective-permute-start.1
  26.4 13.0 %copy-start.18 = (bf16[128,2048]{1,0:T(8,128)(2,1)}, bf16[128,2048]{1,0:T(8,128)(2,1)S(1)}, u32[]{:S(2)}) copy-start(bf16[128,2048]{1,0:T(8,128)(2,1)S(1)} %get-tuple-element.7) | copy-start | bytes 1572868
  26.4 13.1 %collective-permute-start = (bf16[128,2048]{1,0:T(8,128)(2,1)S(1)}, bf16[128,2048]{1,0:T(8,128)(2,1)}, u32[]{:S(2)}, u32[]{:S(2)}) collective-permute-start(bf16[128,2048]{1,0:T(8,128)(2,1)S(1)} %get-tuple-element.8), channel_id=1, source_target_pairs={{0,1},{1,2},{2,3},{3,4},{4,5},{5,6},{6,7},{7,8},{8,9},{9,10},{10,1... | collective-permute-start | bytes 1572872 | tf_op jit(solution)/shard_map/ppermute | solution.py:18
  35.7 7.3 %collective-permute-start.3 = (bf16[128,2048]{1,0:T(8,128)(2,1)S(1)}, bf16[128,2048]{1,0:T(8,128)(2,1)S(1)}, u32[]{:S(2)}, u32[]{:S(2)}) collective-permute-start(bf16[128,2048]{1,0:T(8,128)(2,1)S(1)} %get-tuple-element.7), channel_id=1, source_target_pairs={{1,0},{2,1},{3,2},{4,3},{5,4},{6,5},{7,6},{8,7},{9,8},{10,9},{11,1... | collective-permute-start | bytes 1572872 | tf_op jit(solution)/shard_map/ppermute | solution.py:18
  39.5 8.1 %collective-permute-start.2 = (bf16[128,2048]{1,0:T(8,128)(2,1)}, bf16[128,2048]{1,0:T(8,128)(2,1)S(1)}, u32[]{:S(2)}, u32[]{:S(2)}) collective-permute-start(bf16[128,2048]{1,0:T(8,128)(2,1)} %collective-permute-done), channel_id=1, source_target_pairs={{0,1},{1,2},{2,3},{3,4},{4,5},{5,6},{6,7},{7,8},{8,9},{9,10},{10,1... | collective-permute-start | bytes 1572872 | tf_op jit(solution)/shard_map/ppermute | solution.py:18
  43.8 11.4 %collective-permute-start.5 = (bf16[128,2048]{1,0:T(8,128)(2,1)}, bf16[128,2048]{1,0:T(8,128)(2,1)}, u32[]{:S(2)}, u32[]{:S(2)}) collective-permute-start(bf16[128,2048]{1,0:T(8,128)(2,1)} %broadcast_select_fusion), channel_id=1, source_target_pairs={{1,0},{2,1},{3,2},{4,3},{5,4},{6,5},{7,6},{8,7},{9,8},{10,9},{11,1... | collective-permute-start | bytes 1572872 | tf_op jit(solution)/shard_map/ppermute | solution.py:18
  46.2 10.2 %copy-start.14 = (bf16[256,2048]{1,0:T(8,128)(2,1)S(1)}, bf16[256,2048]{1,0:T(8,128)(2,1)}, u32[]{:S(2)}) copy-start(bf16[256,2048]{1,0:T(8,128)(2,1)} %pad_maximum_fusion.1) | copy-start | bytes 3145732
  47.6 8.7 %collective-permute-start.4 = (bf16[128,2048]{1,0:T(8,128)(2,1)S(1)}, bf16[128,2048]{1,0:T(8,128)(2,1)S(1)}, u32[]{:S(2)}, u32[]{:S(2)}) collective-permute-start(bf16[128,2048]{1,0:T(8,128)(2,1)S(1)} %collective-permute-done.2), channel_id=1, source_target_pairs={{0,1},{1,2},{2,3},{3,4},{4,5},{5,6},{6,7},{7,8},{8,9},{9,10},{10,1... | collective-permute-start | bytes 1572872 | tf_op jit(solution)/shard_map/ppermute | solution.py:18
  59.6 6.3 %copy-start.19 = (bf16[2,128,8,128,1]{1,3,4,2,0:T(8,128)(2,1)S(1)}, bf16[2,128,8,128,1]{1,3,4,2,0:T(8,128)(2,1)}, u32[]{:S(2)}) copy-start(bf16[2,128,8,128,1]{1,3,4,2,0:T(8,128)(2,1)} %copy.47) | copy-start | bytes 1572868
  65.9 5.7 %copy-start.8 = (bf16[128,8,8,128]{3,2,1,0:T(8,128)(2,1)S(1)}, bf16[128,8,8,128]{3,2,1,0:T(8,128)(2,1)}, u32[]{:S(2)}) copy-start(bf16[128,8,8,128]{3,2,1,0:T(8,128)(2,1)} %copy.58) | copy-start | bytes 6291460
  74.2 2.9 copy-start.12
  80.1 4.4 copy-start.9
  80.1 4.4 copy-start.23
  84.6 4.0 copy-start.20
  111.6 3.4 copy-start.2
  115.6 24.6 %copy-start.1 = (f32[4,2,128,2048]{3,2,1,0:T(8,128)}, f32[4,2,128,2048]{3,2,1,0:T(8,128)S(1)}, u32[]{:S(2)}) copy-start(f32[4,2,128,2048]{3,2,1,0:T(8,128)S(1)} %constant_dynamic-update-slice_fusion) | copy-start | bytes 25165828
  115.8 10.1 %collective-permute-start.6 = (bf16[128,2048]{1,0:T(8,128)(2,1)S(1)}, bf16[128,2048]{1,0:T(8,128)(2,1)S(1)}, u32[]{:S(2)}, u32[]{:S(2)}) collective-permute-start(bf16[128,2048]{1,0:T(8,128)(2,1)S(1)} %get-tuple-element.9), channel_id=1, source_target_pairs={{1,0},{2,1},{3,2},{4,3},{5,4},{6,5},{7,6},{8,7},{9,8},{10,9},{11,1... | collective-permute-start | bytes 1572872 | tf_op jit(solution)/shard_map/ppermute | solution.py:18
  117.1 10.0 %collective-permute-start.7 = (bf16[128,2048]{1,0:T(8,128)(2,1)S(1)}, bf16[128,2048]{1,0:T(8,128)(2,1)S(1)}, u32[]{:S(2)}, u32[]{:S(2)}) collective-permute-start(bf16[128,2048]{1,0:T(8,128)(2,1)S(1)} %get-tuple-element.10), channel_id=1, source_target_pairs={{0,1},{1,2},{2,3},{3,4},{4,5},{5,6},{6,7},{7,8},{8,9},{9,10},{10,1... | collective-permute-start | bytes 1572872 | tf_op jit(solution)/shard_map/ppermute | solution.py:18
  127.6 11.0 %collective-permute-start.8 = (bf16[128,2048]{1,0:T(8,128)(2,1)S(1)}, bf16[128,2048]{1,0:T(8,128)(2,1)S(1)}, u32[]{:S(2)}, u32[]{:S(2)}) collective-permute-start(bf16[128,2048]{1,0:T(8,128)(2,1)S(1)} %get-tuple-element.19), channel_id=1, source_target_pairs={{1,0},{2,1},{3,2},{4,3},{5,4},{6,5},{7,6},{8,7},{9,8},{10,9},{11,1... | collective-permute-start | bytes 1572872 | tf_op jit(solution)/shard_map/ppermute | solution.py:18
  128.9 11.1 %collective-permute-start.9 = (bf16[128,2048]{1,0:T(8,128)(2,1)S(1)}, bf16[128,2048]{1,0:T(8,128)(2,1)S(1)}, u32[]{:S(2)}, u32[]{:S(2)}) collective-permute-start(bf16[128,2048]{1,0:T(8,128)(2,1)S(1)} %get-tuple-element.20), channel_id=1, source_target_pairs={{0,1},{1,2},{2,3},{3,4},{4,5},{5,6},{6,7},{7,8},{8,9},{9,10},{10,1... | collective-permute-start | bytes 1572872 | tf_op jit(solution)/shard_map/ppermute | solution.py:18
  140.2 14.5 %copy-start.5 = (bf16[4,2,128,8,128]{2,4,0,3,1:T(8,128)(2,1)S(1)}, bf16[4,2,128,8,128]{2,4,0,3,1:T(8,128)(2,1)}, u32[]{:S(2)}) copy-start(bf16[4,2,128,8,128]{2,4,0,3,1:T(8,128)(2,1)} %copy.42) | copy-start | bytes 6291460
  140.2 14.4 %copy-start.7 = (bf16[2,8,128,4,128]{4,2,3,1,0:T(8,128)(2,1)S(1)}, bf16[2,8,128,4,128]{4,2,3,1,0:T(8,128)(2,1)}, u32[]{:S(2)}) copy-start(bf16[2,8,128,4,128]{4,2,3,1,0:T(8,128)(2,1)} %copy-done.6) | copy-start | bytes 6291460
  142.9 15.2 %collective-permute-start.10 = (bf16[128,2048]{1,0:T(8,128)(2,1)}, bf16[128,2048]{1,0:T(8,128)(2,1)}, u32[]{:S(2)}, u32[]{:S(2)}) collective-permute-start(bf16[128,2048]{1,0:T(8,128)(2,1)} %get-tuple-element.17), channel_id=1, source_target_pairs={{1,0},{2,1},{3,2},{4,3},{5,4},{6,5},{7,6},{8,7},{9,8},{10,9},{11,1... | collective-permute-start | bytes 1572872 | tf_op jit(solution)/shard_map/ppermute | solution.py:18
  144.2 15.4 %collective-permute-start.11 = (bf16[128,2048]{1,0:T(8,128)(2,1)}, bf16[128,2048]{1,0:T(8,128)(2,1)}, u32[]{:S(2)}, u32[]{:S(2)}) collective-permute-start(bf16[128,2048]{1,0:T(8,128)(2,1)} %get-tuple-element.18), channel_id=1, source_target_pairs={{0,1},{1,2},{2,3},{3,4},{4,5},{5,6},{6,7},{7,8},{8,9},{9,10},{10,1... | collective-permute-start | bytes 1572872 | tf_op jit(solution)/shard_map/ppermute | solution.py:18
  160.8 2.2 copy-start.11
  160.8 3.1 copy-start.13
  163.9 2.8 copy-start.4
  169.6 3.1 copy-start.16
  172.8 6.0 %copy-start.21 = (bf16[1,1,256,1024]{3,2,1,0:T(8,128)(2,1)S(1)}, bf16[1,1,256,1024]{3,2,1,0:T(8,128)(2,1)}, u32[]{:S(2)}) copy-start(bf16[1,1,256,1024]{3,2,1,0:T(8,128)(2,1)} %param.9) | copy-start | bytes 1572868
  (5 other events, 6.7 us)
Sparse Core Ops, SparseCore 0:
  169.8 285.4 all-reduce.2
where the time goes:
time: 467 us; the launch traced here: 463 us
  waiting for transfers between devices  280 us (60%)
  starting transfers between devices  55.7 us (12%)
  local copies, waits for them, and re-layouts  50.9 us (11%)
  matrix products  39.5 us (8%)
  other arithmetic  23.2 us (5%)
  between operations  14.6 us (3%)
    unnamed x2, waiting for transfers between devices  275 us
    ppermute x12, starting transfers between devices, shifted(): return lax.ppermute(block, axis, route)  55.6 us
    unnamed x55, local copies, waits for them, and re-layouts  18.3 us
  transfers between devices with their start and end apart: 13, of which 4 were waited for; matrix products, arithmetic and copies ran while one was open for 5% of the time, Pallas kernels for 0%

commit v1 on v0

v1 whole, which is shorter than its diff:
```python
import jax
import jax.numpy as jnp
from jax import lax
from jax.experimental import pallas as pl
from jax.experimental.pallas import tpu as pltpu
from jax.sharding import Mesh, PartitionSpec as P

HEADS = 8
HEAD = 128
TILE = 128
MOST = 4
EPSILON = 1e-06
SCALE = HEAD ** (-0.5)
SEQ = ("y", "x", "core")
MIB = 1024 * 1024

F32 = jnp.float32
BF16 = jnp.bfloat16


def chain_device(block, chips):
    return 2 * block if block < chips else 2 * (2 * chips - 1 - block) + 1


def tile_owner(tile, pairs):
    return tile if tile < pairs else 2 * pairs - 1 - tile


def routes(pairs):
    chips = pairs // 2
    place = [chain_device(block, chips) for block in range(pairs)]
    near_odd = [(tile_owner(2 * b - 1, pairs), place[b]) for b in range(1, pairs)]
    near_even = [(tile_owner(2 * b - 2, pairs), place[b]) for b in range(1, pairs)]
    onward = [(place[b - 1], place[b]) for b in range(2, pairs)]
    far_odd = [(tile_owner(2 * b - 3, pairs), place[b]) for b in range(2, pairs)]
    return near_odd, near_even, onward, far_odd


def reverse(route):
    return [(b, a) for a, b in route]


def move(block, route):
    return lax.ppermute(block, SEQ, route)


def normalize(values):
    centre = jnp.mean(values, axis=-1, keepdims=True)
    centred = values - centre
    spread = jnp.mean(centred * centred, axis=-1, keepdims=True)
    recip = lax.rsqrt(spread + EPSILON)
    return centred * recip, recip


def norm_back(upstream, normed_f, recip):
    first = jnp.mean(upstream, axis=-1, keepdims=True)
    second = jnp.mean(upstream * normed_f, axis=-1, keepdims=True)
    return recip * (upstream - first - normed_f * second)


def silu_pair(half):
    bend = jnp.tanh(half)
    silu = half + half * bend
    sigmoid = 0.5 + 0.5 * bend
    return silu, sigmoid + silu * (1.0 - sigmoid)


def dot_nn(left, right):
    return lax.dot_general(left, right, (((1,), (0,)), ((), ())), preferred_element_type=F32)


def dot_nt(left, right):
    return lax.dot_general(left, right, (((1,), (1,)), ((), ())), preferred_element_type=F32)


def dot_tn(left, right):
    return lax.dot_general(left, right, (((0,), (0,)), ((), ())), preferred_element_type=F32)


def whole():
    return pl.BlockSpec(memory_space=pltpu.VMEM)


def project_kernel(*refs):
    tiles, (weight, normed, proj, slope) = refs[:-4], refs[-4:]

    @pl.when(pl.program_id(0) == 0)
    def _():
        for n, tile in enumerate(tiles):
            rows = tile.shape[0]
            normed[n * rows : (n + 1) * rows, :] = normalize(tile[...].astype(F32))[0].astype(BF16)

    pre = dot_nn(normed[...], weight[...])
    silu, bent = silu_pair(0.5 * pre)
    proj[...] = silu.astype(BF16)
    slope[...] = bent.astype(BF16)


def project(tiles, weight, columns, pick):
    rows = sum(t.shape[0] for t in tiles)
    width = tiles[0].shape[1]
    step = 512
    return pl.pallas_call(
        project_kernel,
        grid=(columns // step,),
        in_specs=[pl.BlockSpec(t.shape, lambda i: (0, 0)) for t in tiles]
        + [pl.BlockSpec((width, step), lambda i: (0, pick(i)))],
        out_specs=[
            pl.BlockSpec((rows, width), lambda i: (0, 0)),
            pl.BlockSpec((rows, step), lambda i: (0, i)),
            pl.BlockSpec((rows, step), lambda i: (0, i)),
        ],
        out_shape=[
            jax.ShapeDtypeStruct((rows, width), BF16),
            jax.ShapeDtypeStruct((rows, columns), BF16),
            jax.ShapeDtypeStruct((rows, columns), BF16),
        ],
        compiler_params=pltpu.CompilerParams(vmem_limit_bytes=40 * MIB),
        cost_estimate=pl.CostEstimate(
            flops=2 * rows * width * columns,
            bytes_accessed=2 * (width * columns + 2 * rows * columns),
            transcendentals=rows * columns,
        ),
    )(*tiles, weight)


def attention_kernel(
    info, proj, slope, normed, near, near_slope, near_normed, d_gated,
    gated, d_pre, near_d_pre, send, keep,
    factor, att_all, bent_all, attended, d_attended,
):
    width = normed.shape[1]
    halo = near.shape[0]
    block, core = info[0], info[1]
    ends = [info[2]]
    for user in range(1, 4):
        ends.append(ends[-1] + info[2 + user])
    columns = MOST * TILE
    lane = lax.broadcasted_iota(jnp.int32, (TILE, columns), 1)
    row = lax.broadcasted_iota(jnp.int32, (TILE, columns), 0)
    causal = lane - (columns - TILE) <= row
    for r in range(2):
        tile = 2 * block + r
        start, end = jnp.int32(0), ends[-1]
        for stop in ends:
            start = jnp.maximum(start, jnp.where(stop <= tile, stop, 0))
            end = jnp.minimum(end, jnp.where(stop > tile, stop, ends[-1]))
        live = (lane // TILE + (tile - (MOST - 1)) >= start) & causal
        events = jnp.full((TILE, columns), (end - start) * TILE, jnp.int32).astype(F32)
        factor[r] = jnp.where(live, 1.0 / events, 0.0)

    def head_slices(h):
        at = pl.multiple_of(h * HEAD, HEAD)
        return [pl.ds(part * width + at, HEAD) for part in range(4)]

    def forward(h, carry):
        _, at_v, at_q, at_k = head_slices(h)
        near_v, near_k = pl.ds(pl.multiple_of(h * HEAD, HEAD), HEAD), head_slices(h)[1]
        keys = jnp.concatenate([near[:, near_k], proj[:, at_k]], axis=0)
        values = jnp.concatenate([near[:, near_v], proj[:, at_v]], axis=0)
        for r in range(2):
            rows = slice(r * TILE, (r + 1) * TILE)
            window = slice(r * TILE, r * TILE + columns)
            scores = dot_nt(proj[rows, at_q], keys[window])
            silu, bent = silu_pair(scores * (0.5 * SCALE))
            att = (silu * factor[r]).astype(BF16)
            att_all[h, r] = att
            bent_all[h, r] = (bent * factor[r]).astype(BF16)
            attended[rows, near_v] = dot_nn(att, values[window])
        return carry

    lax.fori_loop(0, HEADS, forward, 0, unroll=2)

    for r in range(2):
        rows = slice(r * TILE, (r + 1) * TILE)
        gate = proj[rows, 0:width].astype(F32)
        normal, recip = normalize(attended[rows, :])
        gated[rows, :] = (normal * gate).astype(BF16)
        upstream = d_gated[rows, :]
        d_attended[rows, :] = norm_back(upstream * gate, normal, recip).astype(BF16)
        d_pre[rows, 0:width] = (upstream * normal * slope[rows, 0:width].astype(F32)).astype(BF16)

    def backward(h, carry):
        _, at_v, at_q, at_k = head_slices(h)
        near_v, near_k = pl.ds(pl.multiple_of(h * HEAD, HEAD), HEAD), head_slices(h)[1]
        keys = jnp.concatenate([near[:, near_k], proj[:, at_k]], axis=0)
        values = jnp.concatenate([near[:, near_v], proj[:, at_v]], axis=0)
        d_keys, d_values = [], []
        for r in range(2):
            rows = slice(r * TILE, (r + 1) * TILE)
            window = slice(r * TILE, r * TILE + columns)
            upstream = d_attended[rows, near_v]
            d_att = dot_nt(upstream, values[window])
            d_scores = (d_att * bent_all[h, r].astype(F32)).astype(BF16)
            d_query = dot_nn(d_scores, keys[window]) * SCALE
            d_pre[rows, at_q] = (d_query * slope[rows, at_q].astype(F32)).astype(BF16)
            d_keys.append(dot_tn(d_scores, proj[rows, at_q]))
            d_values.append(dot_tn(att_all[h, r], upstream))
        for (first, second), own_at, near_at, scaled in (
            (d_keys, at_k, near_k, SCALE),
            (d_values, at_v, near_v, 1.0),
        ):
            both = first[TILE:] + second[:-TILE]
            total = jnp.concatenate([first[:TILE], both, second[-TILE:]], axis=0) * scaled
            near_d_pre[:, near_at] = (
                total[:halo] * near_slope[:, near_at].astype(F32)
            ).astype(BF16)
            d_pre[:, own_at] = (total[halo:] * slope[:, own_at].astype(F32)).astype(BF16)
        return carry

    lax.fori_loop(0, HEADS, backward, 0, unroll=2)

    half = width // 2
    for out, side in ((send, 1 - core), (keep, core)):
        at = pl.multiple_of(side * half, half)
        d_key = jnp.concatenate(
            [near_d_pre[:, pl.ds(width + at, half)], d_pre[:, pl.ds(3 * width + at, half)]], axis=0
        )
        for n in range(0, width, 256):
            part = jnp.concatenate([near_normed[:, n : n + 256], normed[:, n : n + 256]], axis=0)
            out[n : n + 256, :] = dot_tn(part, d_key).astype(BF16)


def attention(info, proj, slope, normed, near, near_slope, near_normed, d_gated):
    rows, width = normed.shape
    halo = near.shape[0]
    shapes = [
        ((rows, width), BF16),
        ((rows, 4 * width), BF16),
        ((halo, 2 * width), BF16),
        ((width, width // 2), BF16),
        ((width, width // 2), BF16),
    ]
    return pl.pallas_call(
        attention_kernel,
        in_specs=[pl.BlockSpec(memory_space=pltpu.SMEM)] + [whole()] * 7,
        out_specs=[whole()] * 5,
        out_shape=[jax.ShapeDtypeStruct(*s) for s in shapes],
        scratch_shapes=[
            pltpu.VMEM((2, TILE, MOST * TILE), F32),
            pltpu.VMEM((HEADS, 2, TILE, MOST * TILE), BF16),
            pltpu.VMEM((HEADS, 2, TILE, MOST * TILE), BF16),
            pltpu.VMEM((rows, width), F32),
            pltpu.VMEM((rows, width), BF16),
        ],
        compiler_params=pltpu.CompilerParams(vmem_limit_bytes=40 * MIB),
        cost_estimate=pl.CostEstimate(
            flops=2 * 1500 * MIB, bytes_accessed=16 * MIB, transcendentals=MIB
        ),
    )(info, proj, slope, normed, near, near_slope, near_normed, d_gated)


def through_kernel(d_pre, near_d_pre, weight, own, other, far, odd, even, total, near_total):
    i = pl.program_id(0)

    @pl.when(i == 0)
    def _():
        total[...] = jnp.zeros_like(total)
        near_total[...] = jnp.zeros_like(near_total)

    total[...] += dot_nt(d_pre[...], weight[...])

    @pl.when((i // 2) % 2 == 1)
    def _():
        near_total[...] += dot_nt(near_d_pre[...], weight[...])

    @pl.when(i == pl.num_programs(0) - 1)
    def _():
        own[...] = total[:TILE, :]
        other[...] = total[TILE:, :].astype(BF16)
        far[...] = near_total[:TILE, :].astype(BF16)
        even[...] = near_total[TILE : 2 * TILE, :].astype(BF16)
        odd[...] = near_total[2 * TILE :, :].astype(BF16)


def through(d_pre, near_d_pre, weight):
    rows, halo, width = d_pre.shape[0], near_d_pre.shape[0], weight.shape[0]
    step = width // 2
    shape = (TILE, width)
    return pl.pallas_call(
        through_kernel,
        grid=(8,),
        in_specs=[
            pl.BlockSpec((rows, step), lambda i: (0, i)),
            pl.BlockSpec((halo, step), lambda i: (0, 2 * (i // 4) + jnp.where((i // 2) % 2 == 1, i % 2, 0))),
            pl.BlockSpec((width, step), lambda i: (0, i)),
        ],
        out_specs=[pl.BlockSpec(shape, lambda i: (0, 0))] * 5,
        out_shape=[jax.ShapeDtypeStruct(shape, F32)] + [jax.ShapeDtypeStruct(shape, BF16)] * 4,
        scratch_shapes=[pltpu.VMEM((rows, width), F32), pltpu.VMEM((halo, width), F32)],
        compiler_params=pltpu.CompilerParams(vmem_limit_bytes=32 * MIB),
        cost_estimate=pl.CostEstimate(
            flops=2 * width * width * (4 * rows + 2 * halo),
            bytes_accessed=8 * width * width + 8 * rows * width,
            transcendentals=0,
        ),
    )(d_pre, near_d_pre, weight)


def finish_kernel(info, events, back, own, even, other, odd, far, out):
    core = info[1]
    own_rows = pl.ds(pl.multiple_of(core * TILE, TILE), TILE)
    other_rows = pl.ds(pl.multiple_of((1 - core) * TILE, TILE), TILE)
    sums = (
        (own_rows, own[...] + even[...].astype(F32)),
        (other_rows, other[...].astype(F32) + odd[...].astype(F32) + far[...].astype(F32)),
    )
    for rows, d_normed in sums:
        normed_f, recip = normalize(events[rows, :].astype(F32))
        out[rows, :] = (back[rows, :].astype(F32) + norm_back(d_normed, normed_f, recip)).astype(BF16)


def finish(info, *arrays):
    return pl.pallas_call(
        finish_kernel,
        in_specs=[pl.BlockSpec(memory_space=pltpu.SMEM)] + [whole()] * 7,
        out_specs=whole(),
        out_shape=jax.ShapeDtypeStruct(arrays[0].shape, BF16),
        compiler_params=pltpu.CompilerParams(vmem_limit_bytes=24 * MIB),
        cost_estimate=pl.CostEstimate(flops=4 * MIB, bytes_accessed=4 * MIB, transcendentals=0),
    )(info, *arrays)


def shards(events, lengths, weight_in, weight_out, cotangent):
    pairs = lax.axis_size(SEQ)
    chips = pairs // 2
    pair = lax.axis_index(SEQ)
    core = lax.axis_index("core")
    block = jnp.where(core == 0, pair // 2, pairs - 1 - pair // 2)
    info = jnp.concatenate([jnp.stack([block, core]).astype(jnp.int32), lengths[0]])
    near_odd, near_even, onward, far_odd = routes(pairs)
    swap = [(i, i ^ 1) for i in range(pairs)]

    local = events.reshape(2 * TILE, -1)
    back = cotangent.reshape(2 * TILE, -1)
    width = local.shape[1]

    def split(array):
        mine = lax.dynamic_slice_in_dim(array, core * TILE, TILE, 0)
        other = lax.dynamic_slice_in_dim(array, (1 - core) * TILE, TILE, 0)
        return mine, other

    mine, other = split(local)
    tile_1 = move(other, near_odd)
    tile_2 = move(mine, near_even)
    second = move(other, swap)
    tile_3 = move(tile_1, onward)
    back_mine, back_other = split(back)
    back_second = move(back_other, swap)

    normed, proj, slope = project([mine, second], weight_in, 4 * width, lambda i: i)
    d_gated = dot_nt(jnp.concatenate([back_mine, back_second], axis=0), weight_out)
    near_normed, near, near_slope = project(
        [tile_3, tile_2, tile_1], weight_in, 2 * width, lambda i: 2 + i + 4 * (i // 2) - 2 * (i // 2)
    )
    gated, d_pre, near_d_pre, send, keep = attention(
        info, proj, slope, normed, near, near_slope, near_normed, d_gated
    )

    total = keep.astype(F32) + move(send, swap).astype(F32)
    pieces = lax.all_to_all(
        total.astype(BF16), ("dp", "y", "x"), split_axis=0, concat_axis=0, tiled=True
    )
    count = lax.axis_size(("dp", "y", "x"))
    share = jnp.sum(pieces.reshape(count, width // count, width // 2).astype(F32), axis=0)
    rows = width // count // 2
    kept = lax.dynamic_slice_in_dim(share, core * rows, rows, 0)
    given = lax.dynamic_slice_in_dim(share, (1 - core) * rows, rows, 0)
    taken = move(given, swap)
    summed = jnp.where(
        core == 0,
        jnp.concatenate([kept, taken], axis=1),
        jnp.concatenate([taken, kept], axis=1),
    )

    own_d, other_d, far_d, odd_d, even_d = through(d_pre, near_d_pre, weight_in)
    other_in = move(other_d, swap)
    odd_in = move(odd_d, reverse(near_odd))
    even_in = move(even_d, reverse(near_even))
    far_in = move(far_d, reverse(far_odd))
    event_grads = finish(info, local, back, own_d, even_in, other_in, odd_in, far_in)

    contexts = jnp.concatenate([mine, second], axis=0).astype(F32)
    outs = (contexts + dot_nn(gated, weight_out)).astype(BF16)
    out_mine, out_second = outs[:TILE], outs[TILE:]
    out_other = move(out_second, swap)
    layer_out = jnp.where(
        core == 0,
        jnp.concatenate([out_mine, out_other], axis=0),
        jnp.concatenate([out_other, out_mine], axis=0),
    )
    return (layer_out.reshape(events.shape), event_grads.reshape(events.shape), summed)


def solution(mesh):
    devices = mesh.devices
    fine = Mesh(devices.reshape(devices.shape[0], 4, 4, 2), ("dp",) + SEQ)
    every = P("dp", SEQ, None, None)
    return jax.shard_map(
        shards,
        mesh=fine,
        in_specs=(every, P("dp", None), P(), P(), every),
        out_specs=(every, every, P(("dp",) + SEQ, None)),
        check_vma=False,
    )
```

time: 467 us -> 112 us (0.24)
  the two profiles are of different devices: /device:TPU:32 before, /device:TPU:1 now
where the time goes in v1:
time: 112 us
  starting transfers between devices  42.6 us (38%)
  Pallas kernels  36.3 us (32%)
  local copies, waits for them, and re-layouts  18 us (16%)
  other arithmetic  5.67 us (5%)
  waiting for transfers between devices  5.57 us (5%)
  matrix products  2.64 us (2%)
    ppermute x12, starting transfers between devices, move(): return lax.ppermute(block, SEQ, route)  24 us
    all_to_all x1, starting transfers between devices, shards(): lax.all_to_all(total.astype(BF16), ('dp', 'y', 'x'), split_axis=0, concat...  18.5 us
    pallas_call x1, Pallas kernels, attention(): pl.pallas_call(attention_kernel, in_specs=[pl.BlockSpec(memory_space=pltp...  14.7 us
    unnamed x28, local copies, waits for them, and re-layouts  13.5 us
    pallas_call x2, Pallas kernels, project(): pl.pallas_call(project_kernel, grid=(columns // step,), in_specs=[pl.Bloc...  10.2 us
    pallas_call x1, Pallas kernels, through(): pl.pallas_call(through_kernel, grid=(8,), in_specs=[pl.BlockSpec((rows, s...  8.79 us
    all_to_all x1, waiting for transfers between devices, shards(): lax.all_to_all(total.astype(BF16), ('dp', 'y', 'x'), split_axis=0, concat...  2.88 us
    pallas_call x1, Pallas kernels, finish(): pl.pallas_call(finish_kernel, in_specs=[pl.BlockSpec(memory_space=pltpu.S...  2.7 us
  transfers between devices with their start and end apart: 13, of which 2 were waited for; matrix products, arithmetic and copies ran while one was open for 8% of the time, Pallas kernels for 16%

profile of v1, /device:TPU:1, one launch (start us, length us, event | category | flops | bytes accessed | tf_op | source)
XLA Modules:
  0.0 111.6 jit_solution(10364460631193193780)
XLA Ops:
  0.7 1.9 %dynamic-slice_bitcast_fusion.2 = (bf16[128,1024]{1,0:T(8,128)(2,1)}, bf16[128,1024]{1,0:T(8,128)(2,1)S(1)}) fusion(bf16[1,1,256,1024]{3,2,1,0:T(8,128)(2,1)} %param.5, s32[]{:T(128)S(6)} %select_n.48, s32[]{:T(128)S(6)} %select_n.47), kind=kLoop, calls=%fused_computation.13 | loop fusion | bytes 1048584 | tf_op jit(solution)/shard_map/dynamic_slice | solution.py:340
  2.6 4.5 %collective-permute-start.1 = (bf16[128,1024]{1,0:T(8,128)(2,1)}, bf16[128,1024]{1,0:T(8,128)(2,1)S(1)}, u32[]{:S(2)}, u32[]{:S(2)}) collective-permute-start(bf16[128,1024]{1,0:T(8,128)(2,1)} %get-tuple-element.39), channel_id=1, source_target_pairs={{1,2},{3,4},{5,6},{7,8},{9,10},{11,12},{13,14},{15,16},{17,18},{19... | collective-permute-start | bytes 786440 | tf_op jit(solution)/shard_map/ppermute | solution.py:44
  7.2 1.3 %collective-permute-start.3 = (bf16[128,1024]{1,0:T(8,128)(2,1)S(1)}, bf16[128,1024]{1,0:T(8,128)(2,1)S(1)}, u32[]{:S(2)}, u32[]{:S(2)}) collective-permute-start(bf16[128,1024]{1,0:T(8,128)(2,1)S(1)} %get-tuple-element.40.refs_0_), channel_id=1, source_target_pairs={{0,2},{2,4},{4,6},{6,8},{8,10},{10,12},{12,14},{14,16},{16,18},{18... | collective-permute-start | bytes 786440 | tf_op jit(solution)/shard_map/ppermute | solution.py:44
  8.5 1.8 %dynamic-slice_bitcast_fusion.1 = (bf16[128,1024]{1,0:T(8,128)(2,1)S(1)}, bf16[128,1024]{1,0:T(8,128)(2,1)}) fusion(bf16[1,1,256,1024]{3,2,1,0:T(8,128)(2,1)} %param.9, s32[]{:T(128)S(6)} %select_n.47, s32[]{:T(128)S(6)} %select_n.48), kind=kLoop, calls=%fused_computation.12 | loop fusion | bytes 1048584 | tf_op jit(solution)/shard_map/dynamic_slice | solution.py:339
  10.3 2.6 %collective-permute-start.4 = (bf16[128,1024]{1,0:T(8,128)(2,1)}, bf16[128,1024]{1,0:T(8,128)(2,1)}, u32[]{:S(2)}, u32[]{:S(2)}) collective-permute-start(bf16[128,1024]{1,0:T(8,128)(2,1)} %get-tuple-element.38), channel_id=1, source_target_pairs={{0,1},{1,0},{2,3},{3,2},{4,5},{5,4},{6,7},{7,6},{8,9},{9,8},{10,11... | collective-permute-start | bytes 786440 | tf_op jit(solution)/shard_map/ppermute | solution.py:44
  12.9 1.3 %collective-permute-start.2 = (bf16[128,1024]{1,0:T(8,128)(2,1)S(1)}, bf16[128,1024]{1,0:T(8,128)(2,1)S(1)}, u32[]{:S(2)}, u32[]{:S(2)}) collective-permute-start(bf16[128,1024]{1,0:T(8,128)(2,1)S(1)} %collective-permute-done.1.refs_2_), channel_id=1, source_target_pairs={{2,4},{4,6},{6,8},{8,10},{10,12},{12,14},{14,16},{16,18},{18,20},{... | collective-permute-start | bytes 786440 | tf_op jit(solution)/shard_map/ppermute | solution.py:44
  14.3 3.4 %copy-done.1 = bf16[1024,4096]{1,0:T(8,128)(2,1)S(1)} copy-done((bf16[1024,4096]{1,0:T(8,128)(2,1)S(1)}, bf16[1024,4096]{1,0:T(8,128)(2,1)}, u32[]{:S(2)}) %copy-start.1) | copy-done | bytes 8388632
  17.6 5.9 %shard_map.76 = (bf16[256,1024]{1,0:T(8,128)(2,1)S(1)}, bf16[256,4096]{1,0:T(8,128)(2,1)S(1)}, bf16[256,4096]{1,0:T(8,128)(2,1)S(1)}) custom-call(bf16[128,1024]{1,0:T(8,128)(2,1)S(1)} %get-tuple-element.40.refs_0_, bf16[128,1024]{1,0:T(8,128)(2,1)S(1)} %collective-permute-done.refs_1_, bf16[1024,4096]{1,0:T(8,128)(2,1)S(1)} %copy-done.1), custom_call_target="tpu_custom_call" | custom-call | flops 2147483648 | bytes 12582912 | tf_op jit(solution)/shard_map/pallas_call | solution.py:103
  23.6 1.9 %fusion.2.d_gated = f32[256,1024]{1,0:T(8,128)S(1)} fusion(bf16[1024,1024]{1,0:T(8,128)(2,1)S(1)} %copy-done, bf16[128,1024]{1,0:T(8,128)(2,1)} %collective-permute-done.4, bf16[128,1024]{1,0:T(8,128)(2,1)S(1)} %get-tuple-element.37), kind=kOutput, calls=%fused_computation.5 | convolution fusion | flops 537919488 | bytes 3670016 | tf_op jit(solution)/shard_map/dot_general | solution.py:73
  25.6 3.4 %copy-done.2 = bf16[1024,4096]{1,0:T(8,128)(2,1)S(1)} copy-done((bf16[1024,4096]{1,0:T(8,128)(2,1)S(1)}, bf16[1024,4096]{1,0:T(8,128)(2,1)}, u32[]{:S(2)}) %copy-start.2) | copy-done | bytes 8388632
  28.9 4.2 %shard_map.77 = (bf16[384,1024]{1,0:T(8,128)(2,1)S(1)}, bf16[384,2048]{1,0:T(8,128)(2,1)S(1)}, bf16[384,2048]{1,0:T(8,128)(2,1)S(1)}) custom-call(bf16[128,1024]{1,0:T(8,128)(2,1)S(1)} %collective-permute-done.2.refs_0_, bf16[128,1024]{1,0:T(8,128)(2,1)S(1)} %collective-permute-done.3.refs_1_, bf16[128,1024]{1,0:T(8,128)(2,1)S(1)} %collective-permute-done.1.refs_2_, ...), custom_call_target="tpu_custom_call" | custom-call | flops 1610612736 | bytes 7340032 | tf_op jit(solution)/shard_map/pallas_call | solution.py:103
  33.2 14.7 %shard_map.78 = (bf16[256,1024]{1,0:T(8,128)(2,1)S(1)}, bf16[256,4096]{1,0:T(8,128)(2,1)S(1)}, bf16[384,2048]{1,0:T(8,128)(2,1)S(1)}, bf16[1024,512]{1,0:T(8,128)(2,1)S(1)}, bf16[1024,512]{1,0:T(8,128)(2,1)S(1)}) custom-call(s32[6]{0:T(128)S(1)} %pad_add_fusion.info, bf16[256,4096]{1,0:T(8,128)(2,1)S(1)} %get-tuple-element.19.proj, ...), custom_call_target="tpu_custom_call" | custom-call | flops 3145728000 | bytes 16777216 | tf_op jit(solution)/shard_map/pallas_call | solution.py:234
  47.8 1.3 %copy-done.9 = bf16[256,4096]{1,0:T(8,128)(2,1)} copy-done((bf16[256,4096]{1,0:T(8,128)(2,1)}, bf16[256,4096]{1,0:T(8,128)(2,1)S(1)}, u32[]{:S(2)}) %copy-start.9) | copy-done | bytes 2097176
  49.2 1.1 %copy-done.11 = bf16[384,2048]{1,0:T(8,128)(2,1)} copy-done((bf16[384,2048]{1,0:T(8,128)(2,1)}, bf16[384,2048]{1,0:T(8,128)(2,1)S(1)}, u32[]{:S(2)}) %copy-start.11) | copy-done | bytes 1572888
  50.3 2.7 %collective-permute-done.10 = bf16[1024,512]{1,0:T(8,128)(2,1)S(1)} collective-permute-done((bf16[1024,512]{1,0:T(8,128)(2,1)S(1)}, bf16[1024,512]{1,0:T(8,128)(2,1)S(1)}, u32[]{:S(2)}, u32[]{:S(2)}) %collective-permute-start.10) | collective-permute-done | bytes 1048608 | tf_op jit(solution)/shard_map/ppermute | solution.py:44
  53.0 1.3 %fusion.1 = bf16[128,8,512]{2,1,0:T(8,128)(2,1)} fusion(bf16[1024,512]{1,0:T(8,128)(2,1)S(1)} %collective-permute-done.10, bf16[1024,512]{1,0:T(8,128)(2,1)S(1)} %get-tuple-element.33), kind=kLoop, calls=%fused_computation.4 | loop fusion | flops 2097152 | bytes 3145728 | tf_op jit(solution)/shard_map/all_to_all | solution.py:361
  54.3 18.5 %all-to-all-start = ((bf16[128,8,512]{2,1,0:T(8,128)(2,1)}), bf16[128,8,512]{2,1,0:T(8,128)(2,1)}, u32[]{:S(2)}, u32[]{:S(2)}) async-start(bf16[128,8,512]{2,1,0:T(8,128)(2,1)} %fusion.1), calls=%async_computation | async-start | bytes 2097152 | tf_op jit(solution)/shard_map/all_to_all | solution.py:361
  72.8 0.7 fusion
  73.6 0.8 slice_bitcast_fusion
  74.4 0.7 collective-permute-start.5
  75.1 3.4 %copy-done.3 = bf16[1024,4096]{1,0:T(8,128)(2,1)S(1)} copy-done((bf16[1024,4096]{1,0:T(8,128)(2,1)S(1)}, bf16[1024,4096]{1,0:T(8,128)(2,1)}, u32[]{:S(2)}) %copy-start.3) | copy-done | bytes 8388632
  78.4 8.8 %shard_map.79 = (f32[128,1024]{1,0:T(8,128)S(1)}, bf16[128,1024]{1,0:T(8,128)(2,1)}, bf16[128,1024]{1,0:T(8,128)(2,1)}, bf16[128,1024]{1,0:T(8,128)(2,1)}, bf16[128,1024]{1,0:T(8,128)(2,1)}) custom-call(bf16[256,4096]{1,0:T(8,128)(2,1)S(1)} %copy-done.10, bf16[384,2048]{1,0:T(8,128)(2,1)S(1)} %copy-done.12, bf16[1024,4096]{1,0:T(8,128)(2,1)S(1)} %copy-done.3), custom_call_target="tpu_custom_call" | custom-call | flops 3758096384 | bytes 10485760 | tf_op jit(solution)/shard_map/pallas_call | solution.py:280
  87.2 0.8 copy-done.6
  88.0 2.6 %collective-permute-start.6 = (bf16[128,1024]{1,0:T(8,128)(2,1)}, bf16[128,1024]{1,0:T(8,128)(2,1)S(1)}, u32[]{:S(2)}, u32[]{:S(2)}) collective-permute-start(bf16[128,1024]{1,0:T(8,128)(2,1)} %get-tuple-element.29), channel_id=1, source_target_pairs={{2,0},{4,2},{6,4},{8,6},{10,8},{12,10},{14,12},{16,14},{18,16},{20... | collective-permute-start | bytes 786440 | tf_op jit(solution)/shard_map/ppermute | solution.py:44
  90.8 3.6 %collective-permute-start.8 = (bf16[128,1024]{1,0:T(8,128)(2,1)}, bf16[128,1024]{1,0:T(8,128)(2,1)}, u32[]{:S(2)}, u32[]{:S(2)}) collective-permute-start(bf16[128,1024]{1,0:T(8,128)(2,1)} %get-tuple-element.31), channel_id=1, source_target_pairs={{2,1},{4,3},{6,5},{8,7},{10,9},{12,11},{14,13},{16,15},{18,17},{20... | collective-permute-start | bytes 786440 | tf_op jit(solution)/shard_map/ppermute | solution.py:44
  94.4 4.1 %collective-permute-start.9 = (bf16[128,1024]{1,0:T(8,128)(2,1)}, bf16[128,1024]{1,0:T(8,128)(2,1)}, u32[]{:S(2)}, u32[]{:S(2)}) collective-permute-start(bf16[128,1024]{1,0:T(8,128)(2,1)} %get-tuple-element.32), channel_id=1, source_target_pairs={{4,1},{6,3},{8,5},{10,7},{12,9},{14,11},{16,13},{18,15},{20,17},{2... | collective-permute-start | bytes 786440 | tf_op jit(solution)/shard_map/ppermute | solution.py:44
  98.4 2.9 %all-to-all-done = bf16[128,8,512]{2,1,0:T(8,128)(2,1)} async-done(((bf16[128,8,512]{2,1,0:T(8,128)(2,1)}), bf16[128,8,512]{2,1,0:T(8,128)(2,1)}, u32[]{:S(2)}, u32[]{:S(2)}) %all-to-all-start) | async-done | bytes 1048608 | tf_op jit(solution)/shard_map/all_to_all | solution.py:361
  101.3 1.5 %convert_reduce_fusion = f32[8,512]{1,0:T(8,128)S(1)} fusion(bf16[128,8,512]{2,1,0:T(8,128)(2,1)} %all-to-all-done), kind=kLoop, calls=%fused_computation | loop fusion | flops 1044480 | bytes 1064960 | tf_op jit(solution)/shard_map/reduce_sum | solution.py:365
  102.8 3.2 %collective-permute-start.11 = (f32[4,512]{1,0:T(4,128)S(1)}, f32[4,512]{1,0:T(4,128)S(1)}, u32[]{:S(2)}, u32[]{:S(2)}) collective-permute-start(f32[4,512]{1,0:T(4,128)S(1)} %get-tuple-element.42), channel_id=1, source_target_pairs={{0,1},{1,0},{2,3},{3,2},{4,5},{5,4},{6,7},{7,6},{8,9},{9,8},{10,11... | collective-permute-start | bytes 24584 | tf_op jit(solution)/shard_map/ppermute | solution.py:44
  106.1 2.2 %maximum_select_fusion = bf16[1,1,256,1024]{3,2,1,0:T(8,128)(2,1)} fusion(bf16[1,1,128,1024]{3,2,1,0:T(8,128)(2,1)} %bitcast.8, bf16[1,1,128,1024]{3,2,1,0:T(8,128)(2,1)} %get-tuple-element.35, pred[]{:T(512)S(6)} %eq.2), kind=kLoop, calls=%fused_computation.9 | loop fusion | flops 2359296 | bytes 1048577 | tf_op jit(solution)/shard_map/jit(_where)/select_n | solution.py:387
  108.3 2.7 %shard_map.80 = bf16[256,1024]{1,0:T(8,128)(2,1)} custom-call(s32[6]{0:T(128)S(1)} %pad_add_fusion.info, bf16[256,1024]{1,0:T(8,128)(2,1)S(1)} %bitcast.22, bf16[256,1024]{1,0:T(8,128)(2,1)S(1)} %bitcast.23, f32[128,1024]{1,0:T(8,128)S(1)} %copy-done.7, bf16[128,1024]{1,0:T(8,128)(2,1)S(1)} %collective-permute-done.6.even, ...), custom_call_target="tpu_custom_call" | custom-call | flops 4194304 | bytes 4194304 | tf_op jit(solution)/shard_map/pallas_call | solution.py:314
  111.0 0.6 maximum_select_fusion.1
  (38 shorter events, 0.4 us)
Async XLA Ops:
  0.6 22.9 %copy-start = (bf16[1024,1024]{1,0:T(8,128)(2,1)S(1)}, bf16[1024,1024]{1,0:T(8,128)(2,1)}, u32[]{:S(2)}) copy-start(bf16[1024,1024]{1,0:T(8,128)(2,1)} %param.8) | copy-start | bytes 6291460
  0.6 12.2 %copy-start.13 = (s32[1,4]{1,0:T(1,128)S(1)}, s32[1,4]{1,0:T(1,128)}, u32[]{:S(2)}) copy-start(s32[1,4]{1,0:T(1,128)} %param.6) | copy-start | bytes 52
  2.6 10.4 %collective-permute-start.1 = (bf16[128,1024]{1,0:T(8,128)(2,1)}, bf16[128,1024]{1,0:T(8,128)(2,1)S(1)}, u32[]{:S(2)}, u32[]{:S(2)}) collective-permute-start(bf16[128,1024]{1,0:T(8,128)(2,1)} %get-tuple-element.39), channel_id=1, source_target_pairs={{1,2},{3,4},{5,6},{7,8},{9,10},{11,12},{13,14},{15,16},{17,18},{19... | collective-permute-start | bytes 786440 | tf_op jit(solution)/shard_map/ppermute | solution.py:44
  7.1 7.2 %collective-permute-start = (bf16[128,1024]{1,0:T(8,128)(2,1)}, bf16[128,1024]{1,0:T(8,128)(2,1)S(1)}, u32[]{:S(2)}, u32[]{:S(2)}) collective-permute-start(bf16[128,1024]{1,0:T(8,128)(2,1)} %get-tuple-element.39), channel_id=1, source_target_pairs={{0,1},{1,0},{2,3},{3,2},{4,5},{5,4},{6,7},{7,6},{8,9},{9,8},{10,11... | collective-permute-start | bytes 786440 | tf_op jit(solution)/shard_map/ppermute | solution.py:44
  7.2 18.3 %collective-permute-start.3 = (bf16[128,1024]{1,0:T(8,128)(2,1)S(1)}, bf16[128,1024]{1,0:T(8,128)(2,1)S(1)}, u32[]{:S(2)}, u32[]{:S(2)}) collective-permute-start(bf16[128,1024]{1,0:T(8,128)(2,1)S(1)} %get-tuple-element.40.refs_0_), channel_id=1, source_target_pairs={{0,2},{2,4},{4,6},{6,8},{8,10},{10,12},{12,14},{14,16},{16,18},{18... | collective-permute-start | bytes 786440 | tf_op jit(solution)/shard_map/ppermute | solution.py:44
  10.3 13.3 %collective-permute-start.4 = (bf16[128,1024]{1,0:T(8,128)(2,1)}, bf16[128,1024]{1,0:T(8,128)(2,1)}, u32[]{:S(2)}, u32[]{:S(2)}) collective-permute-start(bf16[128,1024]{1,0:T(8,128)(2,1)} %get-tuple-element.38), channel_id=1, source_target_pairs={{0,1},{1,0},{2,3},{3,2},{4,5},{5,4},{6,7},{7,6},{8,9},{9,8},{10,11... | collective-permute-start | bytes 786440 | tf_op jit(solution)/shard_map/ppermute | solution.py:44
  12.9 12.6 %collective-permute-start.2 = (bf16[128,1024]{1,0:T(8,128)(2,1)S(1)}, bf16[128,1024]{1,0:T(8,128)(2,1)S(1)}, u32[]{:S(2)}, u32[]{:S(2)}) collective-permute-start(bf16[128,1024]{1,0:T(8,128)(2,1)S(1)} %collective-permute-done.1.refs_2_), channel_id=1, source_target_pairs={{2,4},{4,6},{6,8},{8,10},{10,12},{12,14},{14,16},{16,18},{18,20},{... | collective-permute-start | bytes 786440 | tf_op jit(solution)/shard_map/ppermute | solution.py:44
  14.2 3.4 %copy-start.1 = (bf16[1024,4096]{1,0:T(8,128)(2,1)S(1)}, bf16[1024,4096]{1,0:T(8,128)(2,1)}, u32[]{:S(2)}) copy-start(bf16[1024,4096]{1,0:T(8,128)(2,1)} %weight.1) | copy-start | bytes 25165828
  23.6 2.0 %copy-start.8 = (bf16[256,4096]{1,0:T(8,128)(2,1)}, bf16[256,4096]{1,0:T(8,128)(2,1)S(1)}, u32[]{:S(2)}) copy-start(bf16[256,4096]{1,0:T(8,128)(2,1)S(1)} %get-tuple-element.20.slope) | copy-start | bytes 6291460
  25.5 3.4 %copy-start.2 = (bf16[1024,4096]{1,0:T(8,128)(2,1)S(1)}, bf16[1024,4096]{1,0:T(8,128)(2,1)}, u32[]{:S(2)}) copy-start(bf16[1024,4096]{1,0:T(8,128)(2,1)} %weight.1) | copy-start | bytes 25165828
  47.8 1.4 %copy-start.9 = (bf16[256,4096]{1,0:T(8,128)(2,1)}, bf16[256,4096]{1,0:T(8,128)(2,1)S(1)}, u32[]{:S(2)}) copy-start(bf16[256,4096]{1,0:T(8,128)(2,1)S(1)} %get-tuple-element.26.d_pre) | copy-start | bytes 6291460
  49.2 1.1 %copy-start.11 = (bf16[384,2048]{1,0:T(8,128)(2,1)}, bf16[384,2048]{1,0:T(8,128)(2,1)S(1)}, u32[]{:S(2)}) copy-start(bf16[384,2048]{1,0:T(8,128)(2,1)S(1)} %get-tuple-element.27.near_d_pre) | copy-start | bytes 4718596
  50.3 2.7 %collective-permute-start.10 = (bf16[1024,512]{1,0:T(8,128)(2,1)S(1)}, bf16[1024,512]{1,0:T(8,128)(2,1)S(1)}, u32[]{:S(2)}, u32[]{:S(2)}) collective-permute-start(bf16[1024,512]{1,0:T(8,128)(2,1)S(1)} %get-tuple-element.34), channel_id=1, source_target_pairs={{0,1},{1,0},{2,3},{3,2},{4,5},{5,4},{6,7},{7,6},{8,9},{9,8},{10,11... | collective-permute-start | bytes 3145736 | tf_op jit(solution)/shard_map/ppermute | solution.py:44
  54.3 47.0 %all-to-all-start = ((bf16[128,8,512]{2,1,0:T(8,128)(2,1)}), bf16[128,8,512]{2,1,0:T(8,128)(2,1)}, u32[]{:S(2)}, u32[]{:S(2)}) async-start(bf16[128,8,512]{2,1,0:T(8,128)(2,1)} %fusion.1), calls=%async_computation | async-start | bytes 2097152 | tf_op jit(solution)/shard_map/all_to_all | solution.py:361
  72.8 2.2 %copy-start.10 = (bf16[256,4096]{1,0:T(8,128)(2,1)S(1)}, bf16[256,4096]{1,0:T(8,128)(2,1)}, u32[]{:S(2)}) copy-start(bf16[256,4096]{1,0:T(8,128)(2,1)} %copy-done.9) | copy-start | bytes 6291460
  72.8 2.2 %copy-start.12 = (bf16[384,2048]{1,0:T(8,128)(2,1)S(1)}, bf16[384,2048]{1,0:T(8,128)(2,1)}, u32[]{:S(2)}) copy-start(bf16[384,2048]{1,0:T(8,128)(2,1)} %copy-done.11) | copy-start | bytes 4718596
  74.4 28.4 %collective-permute-start.5 = (bf16[128,1024]{1,0:T(8,128)(2,1)}, bf16[128,1024]{1,0:T(8,128)(2,1)}, u32[]{:S(2)}, u32[]{:S(2)}) collective-permute-start(bf16[128,1024]{1,0:T(8,128)(2,1)} %get-tuple-element.36), channel_id=1, source_target_pairs={{0,1},{1,0},{2,3},{3,2},{4,5},{5,4},{6,7},{7,6},{8,9},{9,8},{10,11... | collective-permute-start | bytes 786440 | tf_op jit(solution)/shard_map/ppermute | solution.py:44
  75.1 3.4 %copy-start.3 = (bf16[1024,4096]{1,0:T(8,128)(2,1)S(1)}, bf16[1024,4096]{1,0:T(8,128)(2,1)}, u32[]{:S(2)}) copy-start(bf16[1024,4096]{1,0:T(8,128)(2,1)} %weight.1) | copy-start | bytes 25165828
  87.2 0.8 copy-start.6
  88.0 20.3 %copy-start.4 = (bf16[1,1,256,1024]{3,2,1,0:T(8,128)(2,1)S(1)}, bf16[1,1,256,1024]{3,2,1,0:T(8,128)(2,1)}, u32[]{:S(2)}) copy-start(bf16[1,1,256,1024]{3,2,1,0:T(8,128)(2,1)} %param.5) | copy-start | bytes 1572868
  88.0 20.3 %copy-start.5 = (bf16[1,1,256,1024]{3,2,1,0:T(8,128)(2,1)S(1)}, bf16[1,1,256,1024]{3,2,1,0:T(8,128)(2,1)}, u32[]{:S(2)}) copy-start(bf16[1,1,256,1024]{3,2,1,0:T(8,128)(2,1)} %param.9) | copy-start | bytes 1572868
  88.0 20.2 %collective-permute-start.6 = (bf16[128,1024]{1,0:T(8,128)(2,1)}, bf16[128,1024]{1,0:T(8,128)(2,1)S(1)}, u32[]{:S(2)}, u32[]{:S(2)}) collective-permute-start(bf16[128,1024]{1,0:T(8,128)(2,1)} %get-tuple-element.29), channel_id=1, source_target_pairs={{2,0},{4,2},{6,4},{8,6},{10,8},{12,10},{14,12},{16,14},{18,16},{20... | collective-permute-start | bytes 786440 | tf_op jit(solution)/shard_map/ppermute | solution.py:44
  90.7 17.6 %collective-permute-start.7 = (bf16[128,1024]{1,0:T(8,128)(2,1)}, bf16[128,1024]{1,0:T(8,128)(2,1)}, u32[]{:S(2)}, u32[]{:S(2)}) collective-permute-start(bf16[128,1024]{1,0:T(8,128)(2,1)} %get-tuple-element.30), channel_id=1, source_target_pairs={{0,1},{1,0},{2,3},{3,2},{4,5},{5,4},{6,7},{7,6},{8,9},{9,8},{10,11... | collective-permute-start | bytes 786440 | tf_op jit(solution)/shard_map/ppermute | solution.py:44
  90.8 17.5 %collective-permute-start.8 = (bf16[128,1024]{1,0:T(8,128)(2,1)}, bf16[128,1024]{1,0:T(8,128)(2,1)}, u32[]{:S(2)}, u32[]{:S(2)}) collective-permute-start(bf16[128,1024]{1,0:T(8,128)(2,1)} %get-tuple-element.31), channel_id=1, source_target_pairs={{2,1},{4,3},{6,5},{8,7},{10,9},{12,11},{14,13},{16,15},{18,17},{20... | collective-permute-start | bytes 786440 | tf_op jit(solution)/shard_map/ppermute | solution.py:44
  94.4 13.9 %collective-permute-start.9 = (bf16[128,1024]{1,0:T(8,128)(2,1)}, bf16[128,1024]{1,0:T(8,128)(2,1)}, u32[]{:S(2)}, u32[]{:S(2)}) collective-permute-start(bf16[128,1024]{1,0:T(8,128)(2,1)} %get-tuple-element.32), channel_id=1, source_target_pairs={{4,1},{6,3},{8,5},{10,7},{12,9},{14,11},{16,13},{18,15},{20,17},{2... | collective-permute-start | bytes 786440 | tf_op jit(solution)/shard_map/ppermute | solution.py:44
  101.3 7.0 %copy-start.7 = (f32[128,1024]{1,0:T(8,128)S(1)}, f32[128,1024]{1,0:T(8,128)}, u32[]{:S(2)}) copy-start(f32[128,1024]{1,0:T(8,128)} %copy-done.6) | copy-start | bytes 1572868
  102.8 8.2 %collective-permute-start.11 = (f32[4,512]{1,0:T(4,128)S(1)}, f32[4,512]{1,0:T(4,128)S(1)}, u32[]{:S(2)}, u32[]{:S(2)}) collective-permute-start(f32[4,512]{1,0:T(4,128)S(1)} %get-tuple-element.42), channel_id=1, source_target_pairs={{0,1},{1,0},{2,3},{3,2},{4,5},{5,4},{6,7},{7,6},{8,9},{9,8},{10,11... | collective-permute-start | bytes 24584 | tf_op jit(solution)/shard_map/ppermute | solution.py:44

commit v2 on v1

v2 whole, which is shorter than its diff:
```python
import jax
import jax.numpy as jnp
from jax import lax
from jax.experimental import pallas as pl
from jax.experimental.pallas import tpu as pltpu
from jax.sharding import Mesh, PartitionSpec as P

HEADS = 8
HEAD = 128
TILE = 128
MOST = 4
EPSILON = 1e-06
SCALE = HEAD ** (-0.5)
SEQ = ("y", "x", "core")
MIB = 1024 * 1024
SCOPED = 16 * MIB
TINY = pl.CostEstimate(flops=1024, bytes_accessed=1024, transcendentals=0)

F32 = jnp.float32
BF16 = jnp.bfloat16


def chain_device(block, chips):
    return 2 * block if block < chips else 2 * (2 * chips - 1 - block) + 1


def chain_block(core):
    pair = lax.axis_index(SEQ)
    return jnp.where(core == 0, pair // 2, lax.axis_size(SEQ) - 1 - pair // 2)


def tile_owner(tile, pairs):
    return tile if tile < pairs else 2 * pairs - 1 - tile


def routes(pairs):
    chips = pairs // 2
    place = [chain_device(block, chips) for block in range(pairs)]
    near_odd = [(tile_owner(2 * b - 1, pairs), place[b]) for b in range(1, pairs)]
    near_even = [(tile_owner(2 * b - 2, pairs), place[b]) for b in range(1, pairs)]
    onward = [(place[b - 1], place[b]) for b in range(2, pairs)]
    back = [(place[b], place[b - 1]) for b in range(1, pairs)]
    far_back = [(place[b], tile_owner(2 * b - 3, pairs)) for b in range(2, pairs)]
    return near_odd, near_even, onward, back, far_back


def move(block, route):
    return lax.ppermute(block, SEQ, route)


def normalize(values):
    centre = jnp.mean(values, axis=-1, keepdims=True)
    centred = values - centre
    spread = jnp.mean(centred * centred, axis=-1, keepdims=True)
    recip = lax.rsqrt(spread + EPSILON)
    return centred * recip, recip


def norm_back(upstream, normed_f, recip):
    first = jnp.mean(upstream, axis=-1, keepdims=True)
    second = jnp.mean(upstream * normed_f, axis=-1, keepdims=True)
    return recip * (upstream - first - normed_f * second)


def silu_pair(half):
    bend = jnp.tanh(half)
    silu = half + half * bend
    sigmoid = 0.5 + 0.5 * bend
    return silu, sigmoid + silu * (1.0 - sigmoid)


def dot_nn(left, right):
    return lax.dot_general(left, right, (((1,), (0,)), ((), ())), preferred_element_type=F32)


def dot_nt(left, right):
    return lax.dot_general(left, right, (((1,), (1,)), ((), ())), preferred_element_type=F32)


def dot_tn(left, right):
    return lax.dot_general(left, right, (((0,), (0,)), ((), ())), preferred_element_type=F32)


def whole():
    return pl.BlockSpec(memory_space=pltpu.VMEM)


def remote():
    return pl.BlockSpec(memory_space=pltpu.HBM)


def split_kernel(array, mine, other, sems):
    core = lax.axis_index("core")
    copies = [
        pltpu.make_async_copy(array.at[pl.ds(pl.multiple_of(at * TILE, TILE), TILE)], out, sems.at[n])
        for n, (at, out) in enumerate(((1 - core, other), (core, mine)))
    ]
    for copy in copies:
        copy.start()
    for copy in copies:
        copy.wait()


def split(array, cost):
    tile = jax.ShapeDtypeStruct((TILE, array.shape[1]), BF16)
    return pl.pallas_call(
        split_kernel,
        in_specs=[remote()],
        out_specs=[whole()] * 2,
        out_shape=[tile, tile],
        scratch_shapes=[pltpu.SemaphoreType.DMA((2,))],
        compiler_params=pltpu.CompilerParams(vmem_limit_bytes=2 * MIB),
        cost_estimate=pl.CostEstimate(flops=0, bytes_accessed=cost, transcendentals=0),
    )(array)


def project_columns(normed, weight, columns, proj, slope, copies):
    step = 512
    for n, at in enumerate(columns):
        copies[n].wait()
        silu, bent = silu_pair(0.5 * dot_nn(normed[...], weight[:, n * step : (n + 1) * step]))
        proj[:, n * step : (n + 1) * step] = silu.astype(BF16)
        slope[:, n * step : (n + 1) * step] = bent.astype(BF16)


def fetch_columns(weight, columns, held, sems):
    step = 512
    copies = [
        pltpu.make_async_copy(weight.at[:, at : at + step], held.at[:, n * step : (n + 1) * step], sems.at[n])
        for n, at in enumerate(columns)
    ]
    for copy in copies:
        copy.start()
    return copies


def project_kernel(
    mine, second, back_mine, back_second, weight, weight_out, normed, proj, slope, d_gated,
    held, held_out, sems,
):
    width = weight.shape[0]
    columns = range(0, 4 * width, 512)
    copies = fetch_columns(weight, columns, held, sems)
    last = pltpu.make_async_copy(weight_out, held_out, sems.at[len(copies)])
    last.start()
    for r, tile in enumerate((mine, second)):
        rows = slice(r * TILE, (r + 1) * TILE)
        normed[rows, :] = normalize(tile[...].astype(F32))[0].astype(BF16)
    project_columns(normed, held, columns, proj, slope, copies)
    last.wait()
    for n in range(0, width, 256):
        part = held_out[n : n + 256, :]
        d_gated[:TILE, n : n + 256] = dot_nt(back_mine[...], part)
        d_gated[TILE:, n : n + 256] = dot_nt(back_second[...], part)


def project(mine, second, back_mine, back_second, weight, weight_out):
    width, columns = weight.shape
    rows = 2 * TILE
    shapes = [((rows, width), BF16), ((rows, columns), BF16), ((rows, columns), BF16), ((rows, width), F32)]
    return pl.pallas_call(
        project_kernel,
        in_specs=[whole()] * 4 + [remote()] * 2,
        out_specs=[whole()] * 4,
        out_shape=[jax.ShapeDtypeStruct(*s) for s in shapes],
        scratch_shapes=[
            pltpu.VMEM(weight.shape, BF16),
            pltpu.VMEM(weight_out.shape, BF16),
            pltpu.SemaphoreType.DMA((columns // 512 + 1,)),
        ],
        compiler_params=pltpu.CompilerParams(vmem_limit_bytes=47 * MIB),
        cost_estimate=pl.CostEstimate(
            flops=2 * rows * width * (columns + width),
            bytes_accessed=2 * (width * columns + 2 * rows * columns),
            transcendentals=rows * columns,
        ),
    )(mine, second, back_mine, back_second, weight, weight_out)


def project_near_kernel(far, even, odd, weight, normed, proj, slope, held, sems):
    width = weight.shape[0]
    columns = [part * width + at for part in (1, 3) for at in range(0, width, 512)]
    copies = fetch_columns(weight, columns, held, sems)
    for r, tile in enumerate((far, even, odd)):
        rows = slice(r * TILE, (r + 1) * TILE)
        normed[rows, :] = normalize(tile[...].astype(F32))[0].astype(BF16)
    project_columns(normed, held, columns, proj, slope, copies)


def project_near(tiles, weight):
    rows, width = 3 * TILE, weight.shape[0]
    shapes = [((rows, width), BF16), ((rows, 2 * width), BF16), ((rows, 2 * width), BF16)]
    return pl.pallas_call(
        project_near_kernel,
        in_specs=[whole()] * 3 + [remote()],
        out_specs=[whole()] * 3,
        out_shape=[jax.ShapeDtypeStruct(*s) for s in shapes],
        scratch_shapes=[pltpu.VMEM((width, 2 * width), BF16), pltpu.SemaphoreType.DMA((4,))],
        compiler_params=pltpu.CompilerParams(vmem_limit_bytes=44 * MIB),
        cost_estimate=pl.CostEstimate(
            flops=4 * rows * width * width, bytes_accessed=8 * width * width, transcendentals=2 * rows * width
        ),
    )(*tiles, weight)


def attention_kernel(
    lengths, proj, slope, near, near_slope, d_gated,
    gated, d_pre, near_d_pre,
    factor, att_all, bent_all, attended, d_attended,
):
    width = gated.shape[1]
    halo = near.shape[0]
    core = lax.axis_index("core")
    block = chain_block(core)
    ends = [lengths[0, 0]]
    for user in range(1, lengths.shape[1]):
        ends.append(ends[-1] + lengths[0, user])
    columns = MOST * TILE
    lane = lax.broadcasted_iota(jnp.int32, (TILE, columns), 1)
    row = lax.broadcasted_iota(jnp.int32, (TILE, columns), 0)
    causal = lane - (columns - TILE) <= row
    for r in range(2):
        tile = 2 * block + r
        start, end = jnp.int32(0), ends[-1]
        for stop in ends:
            start = jnp.maximum(start, jnp.where(stop <= tile, stop, 0))
            end = jnp.minimum(end, jnp.where(stop > tile, stop, ends[-1]))
        live = (lane // TILE + (tile - (MOST - 1)) >= start) & causal
        events = jnp.full((TILE, columns), (end - start) * TILE, jnp.int32).astype(F32)
        factor[r] = jnp.where(live, 1.0 / events, 0.0)

    def head_slices(h):
        at = pl.multiple_of(h * HEAD, HEAD)
        return [pl.ds(part * width + at, HEAD) for part in range(4)]

    def forward(h, carry):
        _, at_v, at_q, at_k = head_slices(h)
        near_v, near_k = pl.ds(pl.multiple_of(h * HEAD, HEAD), HEAD), head_slices(h)[1]
        keys = jnp.concatenate([near[:, near_k], proj[:, at_k]], axis=0)
        values = jnp.concatenate([near[:, near_v], proj[:, at_v]], axis=0)
        for r in range(2):
            rows = slice(r * TILE, (r + 1) * TILE)
            window = slice(r * TILE, r * TILE + columns)
            scores = dot_nt(proj[rows, at_q], keys[window])
            silu, bent = silu_pair(scores * (0.5 * SCALE))
            att = (silu * factor[r]).astype(BF16)
            att_all[h, r] = att
            bent_all[h, r] = (bent * factor[r]).astype(BF16)
            attended[rows, near_v] = dot_nn(att, values[window])
        return carry

    lax.fori_loop(0, HEADS, forward, 0, unroll=2)

    for r in range(2):
        rows = slice(r * TILE, (r + 1) * TILE)
        gate = proj[rows, 0:width].astype(F32)
        normal, recip = normalize(attended[rows, :])
        gated[rows, :] = (normal * gate).astype(BF16)
        upstream = d_gated[rows, :]
        d_attended[rows, :] = norm_back(upstream * gate, normal, recip).astype(BF16)
        d_pre[rows, 0:width] = (upstream * normal * slope[rows, 0:width].astype(F32)).astype(BF16)

    def backward(h, carry):
        _, at_v, at_q, at_k = head_slices(h)
        near_v, near_k = pl.ds(pl.multiple_of(h * HEAD, HEAD), HEAD), head_slices(h)[1]
        keys = jnp.concatenate([near[:, near_k], proj[:, at_k]], axis=0)
        values = jnp.concatenate([near[:, near_v], proj[:, at_v]], axis=0)
        d_keys, d_values = [], []
        for r in range(2):
            rows = slice(r * TILE, (r + 1) * TILE)
            window = slice(r * TILE, r * TILE + columns)
            upstream = d_attended[rows, near_v]
            d_att = dot_nt(upstream, values[window])
            d_scores = (d_att * bent_all[h, r].astype(F32)).astype(BF16)
            d_query = dot_nn(d_scores, keys[window]) * SCALE
            d_pre[rows, at_q] = (d_query * slope[rows, at_q].astype(F32)).astype(BF16)
            d_keys.append(dot_tn(d_scores, proj[rows, at_q]))
            d_values.append(dot_tn(att_all[h, r], upstream))
        for (first, second), own_at, near_at, scaled in (
            (d_keys, at_k, near_k, SCALE),
            (d_values, at_v, near_v, 1.0),
        ):
            both = first[TILE:] + second[:-TILE]
            total = jnp.concatenate([first[:TILE], both, second[-TILE:]], axis=0) * scaled
            near_d_pre[:, near_at] = (
                total[:halo] * near_slope[:, near_at].astype(F32)
            ).astype(BF16)
            d_pre[:, own_at] = (total[halo:] * slope[:, own_at].astype(F32)).astype(BF16)
        return carry

    lax.fori_loop(0, HEADS, backward, 0, unroll=2)


def attention(lengths, proj, slope, near, near_slope, d_gated):
    rows, width = d_gated.shape
    halo = near.shape[0]
    shapes = [((rows, width), BF16), ((rows, 4 * width), BF16), ((halo, 2 * width), BF16)]
    return pl.pallas_call(
        attention_kernel,
        in_specs=[pl.BlockSpec(memory_space=pltpu.SMEM)] + [whole()] * 5,
        out_specs=[whole()] * 3,
        out_shape=[jax.ShapeDtypeStruct(*s) for s in shapes],
        scratch_shapes=[
            pltpu.VMEM((2, TILE, MOST * TILE), F32),
            pltpu.VMEM((HEADS, 2, TILE, MOST * TILE), BF16),
            pltpu.VMEM((HEADS, 2, TILE, MOST * TILE), BF16),
            pltpu.VMEM((rows, width), F32),
            pltpu.VMEM((rows, width), BF16),
        ],
        compiler_params=pltpu.CompilerParams(vmem_limit_bytes=SCOPED),
        cost_estimate=pl.CostEstimate(
            flops=2 * 800 * MIB, bytes_accessed=16 * MIB, transcendentals=MIB
        ),
    )(lengths, proj, slope, near, near_slope, d_gated)


def key_grad_kernel(near_normed, normed, near_d_pre, d_pre, send, keep):
    width = normed.shape[1]
    even = lax.axis_index("core") == 0
    half = width // 2
    side, depth = keep.shape[:2]
    d_key = jnp.concatenate([near_d_pre[:, width:], d_pre[:, 3 * width :]], axis=0)
    upper = lax.broadcasted_iota(jnp.int32, (1, 8, half), 1) < 4
    step = width // depth
    for z in range(depth):
        at = slice(z * step, (z + 1) * step)
        part = jnp.concatenate([near_normed[:, at], normed[:, at]], axis=0)
        grad = dot_tn(part, d_key).reshape(side * side, 8, width)
        left, right = grad[:, :, :half], grad[:, :, half:]
        first = jnp.where(upper, left, pltpu.roll(right, 4, 1))
        last = jnp.where(upper, pltpu.roll(left, 4, 1), right)
        kept = jnp.where(even, first, last).astype(BF16)
        sent = jnp.where(even, last, first).astype(BF16)
        for y in range(side):
            for x in range(side):
                by_row, by_column = y * side + x, x * side + y
                keep[y, z, x] = jnp.where(even, kept[by_column], kept[by_row])
                send[y, z, x] = jnp.where(even, sent[by_row], sent[by_column])


def key_grad(near_normed, normed, near_d_pre, d_pre):
    width = normed.shape[1]
    depth, side = lax.axis_size("dp"), lax.axis_size("x")
    shape = jax.ShapeDtypeStruct((side, depth, side, 8, width // 2), BF16)
    return pl.pallas_call(
        key_grad_kernel,
        in_specs=[whole()] * 4,
        out_specs=[whole()] * 2,
        out_shape=[shape, shape],
        compiler_params=pltpu.CompilerParams(vmem_limit_bytes=SCOPED),
        cost_estimate=TINY,
    )(near_normed, normed, near_d_pre, d_pre)


def ring_place():
    return jnp.where(lax.axis_index("core") == 0, lax.axis_index("x"), lax.axis_index("y"))


def ring_route(shift):
    route = []
    for pair in range(32):
        y, x, core = pair // 8, pair // 2 % 4, pair % 2
        y, x = (y, (x + shift) % 4) if core == 0 else ((y + shift) % 4, x)
        route.append((pair, y * 8 + x * 2 + core))
    return route


def ring_first_kernel(keep, received, total, up, down):
    place = ring_place()
    half = up.shape[0]
    total[...] = (keep[...].astype(F32) + received[...].astype(F32)).astype(BF16)
    opposite = total.at[lax.rem(place + 2, 4)]
    up[...] = opposite[:half]
    down[...] = opposite[half:]


def ring_second_kernel(total, from_below, from_above, up, down):
    place = ring_place()
    half = from_below.shape[0]
    above, below = total.at[lax.rem(place + 1, 4)], total.at[lax.rem(place + 3, 4)]
    up[:half] = (above[:half].astype(F32) + from_below[...].astype(F32)).astype(BF16)
    up[half:] = above[half:]
    down[:half] = below[:half]
    down[half:] = (below[half:].astype(F32) + from_above[...].astype(F32)).astype(BF16)


def ring_third_kernel(total, from_below, from_above, column):
    own = total.at[ring_place()]
    column[...] = (
        own[...].astype(F32) + from_below[...].astype(F32) + from_above[...].astype(F32)
    ).astype(BF16)


def on_device(kernel, shapes, *arrays):
    return pl.pallas_call(
        kernel,
        in_specs=[whole()] * len(arrays),
        out_specs=[whole()] * len(shapes),
        out_shape=[jax.ShapeDtypeStruct(shape, BF16) for shape in shapes],
        compiler_params=pltpu.CompilerParams(vmem_limit_bytes=SCOPED),
        cost_estimate=TINY,
    )(*arrays)


def near_through_kernel(near_d_pre, weight, far, out):
    width = weight.shape[0]
    step = 256
    for n in range(0, width, step):
        at = slice(n, n + step)
        near = dot_nt(near_d_pre[:, :width], weight[at, width : 2 * width])
        near = (near + dot_nt(near_d_pre[:, width:], weight[at, 3 * width :])).astype(BF16)
        far[:, at] = near[:TILE]
        out[:, at] = near[TILE:]


def near_through(near_d_pre, weight):
    halo, width = near_d_pre.shape[0], weight.shape[0]
    return pl.pallas_call(
        near_through_kernel,
        in_specs=[whole()] * 2,
        out_specs=[whole()] * 2,
        out_shape=[
            jax.ShapeDtypeStruct((TILE, width), BF16), jax.ShapeDtypeStruct((halo - TILE, width), BF16)
        ],
        compiler_params=pltpu.CompilerParams(vmem_limit_bytes=SCOPED),
        cost_estimate=TINY,
    )(near_d_pre, weight)


def through_kernel(d_pre, gated, mine, second, weight, weight_out, d_normed, outs):
    width = weight.shape[0]
    step = 256
    for n in range(0, width, step):
        at = slice(n, n + step)
        d_normed[:, at] = dot_nt(d_pre[...], weight[at, :])
        update = dot_nn(gated[...], weight_out[:, at])
        outs[:TILE, at] = (mine[:, at].astype(F32) + update[:TILE]).astype(BF16)
        outs[TILE:, at] = (second[:, at].astype(F32) + update[TILE:]).astype(BF16)


def through(d_pre, gated, mine, second, weight, weight_out):
    rows, width = d_pre.shape[0], weight.shape[0]
    return pl.pallas_call(
        through_kernel,
        in_specs=[whole()] * 6,
        out_specs=[whole()] * 2,
        out_shape=[
            jax.ShapeDtypeStruct((rows, width), F32), jax.ShapeDtypeStruct((rows, width), BF16)
        ],
        compiler_params=pltpu.CompilerParams(vmem_limit_bytes=SCOPED),
        cost_estimate=TINY,
    )(d_pre, gated, mine, second, weight, weight_out)


def merge_kernel(d_normed, arrived, outs, own, given):
    own[...] = d_normed[:TILE, :] + arrived[:TILE, :].astype(F32)
    given[:TILE, :] = outs[TILE:, :]
    given[TILE:, :] = (d_normed[TILE:, :] + arrived[TILE:, :].astype(F32)).astype(BF16)


def merge(d_normed, arrived, outs):
    rows, width = outs.shape
    return pl.pallas_call(
        merge_kernel,
        in_specs=[whole()] * 3,
        out_specs=[whole()] * 2,
        out_shape=[
            jax.ShapeDtypeStruct((TILE, width), F32),
            jax.ShapeDtypeStruct((rows, width), BF16),
        ],
        compiler_params=pltpu.CompilerParams(vmem_limit_bytes=SCOPED),
        cost_estimate=TINY,
    )(d_normed, arrived, outs)


def finish_kernel(
    events, back, outs, own, taken, far, layer_out, event_grads, layer, grads, sems
):
    core = lax.axis_index("core")
    kept = pl.ds(pl.multiple_of(core * TILE, TILE), TILE)
    swapped = pl.ds(pl.multiple_of((1 - core) * TILE, TILE), TILE)
    layer[0] = outs[:TILE, :]
    layer[1] = taken[:TILE, :]
    stores = [
        pltpu.make_async_copy(layer.at[r], layer_out.at[rows], sems.at[r])
        for r, rows in enumerate((kept, swapped))
    ]
    for copy in stores:
        copy.start()
    sums = (
        (kept, own[...]),
        (swapped, taken[TILE:, :].astype(F32) + far[...].astype(F32)),
    )
    for r, (rows, d_normed) in enumerate(sums):
        normed_f, recip = normalize(events[rows, :].astype(F32))
        grads[r] = (back[rows, :].astype(F32) + norm_back(d_normed, normed_f, recip)).astype(BF16)
        stores.append(pltpu.make_async_copy(grads.at[r], event_grads.at[rows], sems.at[2 + r]))
        stores[-1].start()
    for copy in stores:
        copy.wait()


def finish(events, back, outs, own, taken, far):
    rows, width = events.shape
    return pl.pallas_call(
        finish_kernel,
        in_specs=[whole()] * 6,
        out_specs=[remote()] * 2,
        out_shape=[jax.ShapeDtypeStruct((rows, width), BF16)] * 2,
        scratch_shapes=[
            pltpu.VMEM((2, TILE, width), BF16),
            pltpu.VMEM((2, TILE, width), BF16),
            pltpu.SemaphoreType.DMA((4,)),
        ],
        compiler_params=pltpu.CompilerParams(vmem_limit_bytes=SCOPED),
        cost_estimate=pl.CostEstimate(flops=4 * MIB, bytes_accessed=4 * MIB, transcendentals=0),
    )(events, back, outs, own, taken, far)


def sum_kernel(parts, out):
    total = parts[0].astype(F32)
    for n in range(1, parts.shape[0]):
        total = total + parts[n].astype(F32)
    out[:, : total.shape[1]] = total[:4]
    out[:, total.shape[1] :] = total[4:]


def sum_parts(parts):
    return pl.pallas_call(
        sum_kernel,
        in_specs=[whole()],
        out_specs=whole(),
        out_shape=jax.ShapeDtypeStruct((4, 2 * parts.shape[-1]), F32),
        compiler_params=pltpu.CompilerParams(vmem_limit_bytes=SCOPED),
        cost_estimate=TINY,
    )(parts)


def last_groups():
    place = lambda z, y, x, core: ((z * 4 + y) * 4 + x) * 2 + core
    even = [[place(z, y, x, 0) for z in range(8) for y in range(4)] for x in range(4)]
    odd = [[place(z, y, x, 1) for z in range(8) for x in range(4)] for y in range(4)]
    return even + odd


def shards(events, lengths, weight_in, weight_out, cotangent):
    pairs = lax.axis_size(SEQ)
    near_odd, near_even, onward, backward, far_back = routes(pairs)
    swap = [(i, i ^ 1) for i in range(pairs)]
    local = events.reshape(2 * TILE, -1)
    back = cotangent.reshape(2 * TILE, -1)

    mine, other = split(local, 24 * MIB)
    odd = move(other, near_odd)
    even = move(mine, near_even)
    second = move(other, swap)
    far = move(odd, onward)
    back_mine, back_other = split(back, MIB)
    back_second = move(back_other, swap)

    normed, proj, slope, d_gated = project(mine, second, back_mine, back_second, weight_in, weight_out)
    far, even, odd, proj = lax.optimization_barrier((far, even, odd, proj))
    near_normed, near, near_slope = project_near([far, even, odd], weight_in)
    gated, d_pre, near_d_pre = attention(lengths, proj, slope, near, near_slope, d_gated)

    tie = lax.optimization_barrier
    send, keep = key_grad(near_normed, normed, near_d_pre, d_pre)
    received = move(send, swap)
    near_d_pre, send = tie((near_d_pre, send))
    far_d, near_d = near_through(near_d_pre, weight_in)
    arrived = move(near_d, backward)
    received, near_d = tie((received, near_d))

    block = keep.shape[1:]
    half = (block[0] // 2,) + block[1:]
    total, up, down = on_device(ring_first_kernel, [keep.shape, half, half], keep, received)
    from_below, from_above = move(up, ring_route(1)), move(down, ring_route(-1))
    d_pre, total = tie((d_pre, total))
    d_normed, outs = through(d_pre, gated, mine, second, weight_in, weight_out)
    from_below, from_above, d_normed = tie((from_below, from_above, d_normed))
    up, down = on_device(ring_second_kernel, [block, block], total, from_below, from_above)
    from_below, from_above = move(up, ring_route(1)), move(down, ring_route(-1))
    own, given = merge(d_normed, arrived, outs)
    far_in = move(far_d, far_back)
    from_below, from_above, own, far_in = tie((from_below, from_above, own, far_in))
    (column,) = on_device(ring_third_kernel, [block], total, from_below, from_above)
    column = column.reshape((block[0] * block[1],) + block[2:])
    parts = lax.all_to_all(
        column, ("dp",) + SEQ, split_axis=0, concat_axis=0, tiled=True, axis_index_groups=last_groups()
    )
    taken = move(given, swap)
    layer_out, event_grads = finish(local, back, outs, own, taken, far_in)
    summed = sum_parts(parts)
    return (layer_out.reshape(events.shape), event_grads.reshape(events.shape), summed)


def solution(mesh):
    devices = mesh.devices
    fine = Mesh(devices.reshape(devices.shape[0], 4, 4, 2), ("dp",) + SEQ)
    every = P("dp", SEQ, None, None)
    return jax.shard_map(
        shards,
        mesh=fine,
        in_specs=(every, P("dp", None), P(), P(), every),
        out_specs=(every, every, P(("dp",) + SEQ, None)),
        check_vma=False,
    )
```

time: 112 us -> 95.2 us (0.85)
  the two profiles are of different devices: /device:TPU:1 before, /device:TPU:32 now
where the time goes in v2:
time: 95.2 us; the launch traced here: 93.4 us
  starting transfers between devices  38.7 us (41%)
  Pallas kernels  35.3 us (37%)
  waiting for transfers between devices  16.3 us (17%)
  local copies, waits for them, and re-layouts  2.11 us (2%)
    ppermute x13, starting transfers between devices, move(): return lax.ppermute(block, SEQ, route)  23.4 us
    all_to_all x1, starting transfers between devices, shards(): lax.all_to_all(column, ('dp',) + SEQ, split_axis=0, concat_axis=0, tiled=...  15.2 us
    pallas_call x1, Pallas kernels, attention(): pl.pallas_call(attention_kernel, in_specs=[pl.BlockSpec(memory_space=pltp...  11.8 us
    all_to_all x1, waiting for transfers between devices, shards(): lax.all_to_all(column, ('dp',) + SEQ, split_axis=0, concat_axis=0, tiled=...  9.15 us
    pallas_call x1, Pallas kernels, project(): pl.pallas_call(project_kernel, in_specs=[whole()] * 4 + [remote()] * 2, o...  7.44 us
    ppermute x13, waiting for transfers between devices, move(): return lax.ppermute(block, SEQ, route)  7.16 us
    pallas_call x1, Pallas kernels, project_near(): pl.pallas_call(project_near_kernel, in_specs=[whole()] * 3 + [remote()],...  4.57 us
    pallas_call x1, Pallas kernels, through(): pl.pallas_call(through_kernel, in_specs=[whole()] * 6, out_specs=[whole()...  2.9 us
  transfers between devices with their start and end apart: 14, of which 4 were waited for; matrix products, arithmetic and copies ran while one was open for 0% of the time, Pallas kernels for 17%

profile of v2, /device:TPU:32, one launch (start us, length us, event | category | flops | bytes accessed | tf_op | source)
XLA Modules:
  0.0 93.4 jit_solution(9513728226548471852)
XLA Ops:
  0.6 1.0 %copy-done.1 = bf16[1,1,256,1024]{3,2,1,0:T(8,128)(2,1)S(1)} copy-done((bf16[1,1,256,1024]{3,2,1,0:T(8,128)(2,1)S(1)}, bf16[1,1,256,1024]{3,2,1,0:T(8,128)(2,1)}, u32[]{:S(2)}) %copy-start.1) | copy-done | bytes 524312
  1.7 0.7 collective-permute-start
  2.4 2.9 %collective-permute-start.3 = (bf16[128,1024]{1,0:T(8,128)(2,1)S(1)}, bf16[128,1024]{1,0:T(8,128)(2,1)S(1)}, u32[]{:S(2)}, u32[]{:S(2)}) collective-permute-start(bf16[128,1024]{1,0:T(8,128)(2,1)S(1)} %get-tuple-element.47), channel_id=1, source_target_pairs={{0,1},{1,0},{2,3},{3,2},{4,5},{5,4},{6,7},{7,6},{8,9},{9,8},{10,11... | collective-permute-start | bytes 786440 | tf_op jit(solution)/shard_map/ppermute | solution.py:48
  5.4 1.0 %copy-done.3 = bf16[1,1,256,1024]{3,2,1,0:T(8,128)(2,1)S(1)} copy-done((bf16[1,1,256,1024]{3,2,1,0:T(8,128)(2,1)S(1)}, bf16[1,1,256,1024]{3,2,1,0:T(8,128)(2,1)}, u32[]{:S(2)}) %copy-start.3) | copy-done | bytes 524312
  6.5 0.1 collective-permute-start.4
  6.6 3.4 %collective-permute-start.2 = (bf16[128,1024]{1,0:T(8,128)(2,1)S(1)}, bf16[128,1024]{1,0:T(8,128)(2,1)S(1)}, u32[]{:S(2)}, u32[]{:S(2)}) collective-permute-start(bf16[128,1024]{1,0:T(8,128)(2,1)S(1)} %get-tuple-element.48.mine), channel_id=1, source_target_pairs={{0,2},{2,4},{4,6},{6,8},{8,10},{10,12},{12,14},{14,16},{16,18},{18... | collective-permute-start | bytes 786440 | tf_op jit(solution)/shard_map/ppermute | solution.py:48
  10.0 0.7 collective-permute-start.1
  10.7 7.4 %shard_map.78 = (bf16[256,1024]{1,0:T(8,128)(2,1)S(1)}, bf16[256,4096]{1,0:T(8,128)(2,1)S(1)}, bf16[256,4096]{1,0:T(8,128)(2,1)S(1)}, f32[256,1024]{1,0:T(8,128)S(1)}) custom-call(bf16[128,1024]{1,0:T(8,128)(2,1)S(1)} %get-tuple-element.48.mine, bf16[128,1024]{1,0:T(8,128)(2,1)S(1)} %collective-permute-done.3.second, ...), custom_call_target="tpu_custom_call" | custom-call | flops 2684354560 | bytes 12582912 | tf_op jit(solution)/shard_map/pallas_call | solution.py:161
  18.2 4.6 %shard_map.79 = (bf16[384,1024]{1,0:T(8,128)(2,1)S(1)}, bf16[384,2048]{1,0:T(8,128)(2,1)S(1)}, bf16[384,2048]{1,0:T(8,128)(2,1)S(1)}) custom-call(bf16[128,1024]{1,0:T(8,128)(2,1)S(1)} %collective-permute-done.1.far, bf16[128,1024]{1,0:T(8,128)(2,1)S(1)} %collective-permute-done.2.even, bf16[128,1024]{1,0:T(8,128)(2,1)S(1)} %collective-permute-done.odd, ...), custom_call_target="tpu_custom_call" | custom-call | flops 1610612736 | bytes 8388608 | tf_op jit(solution)/shard_map/pallas_call | solution.py:193
  22.8 11.8 %shard_map.80 = (bf16[256,1024]{1,0:T(8,128)(2,1)S(1)}, bf16[256,4096]{1,0:T(8,128)(2,1)S(1)}, bf16[384,2048]{1,0:T(8,128)(2,1)S(1)}) custom-call(s32[1,4]{1,0:T(1,128)S(1)} %copy-done.5, bf16[256,4096]{1,0:T(8,128)(2,1)S(1)} %get-tuple-element.52.proj, bf16[256,4096]{1,0:T(8,128)(2,1)S(1)} %get-tuple-element.53.slope, ...), custom_call_target="tpu_custom_call" | custom-call | flops 1677721600 | bytes 16777216 | tf_op jit(solution)/shard_map/pallas_call | solution.py:298
  34.6 2.1 %shard_map.81 = (bf16[4,8,4,8,512]{4,3,2,1,0:T(8,128)(2,1)S(1)}, bf16[4,8,4,8,512]{4,3,2,1,0:T(8,128)(2,1)S(1)}) custom-call(bf16[384,1024]{1,0:T(8,128)(2,1)S(1)} %get-tuple-element.61.near_normed, bf16[256,1024]{1,0:T(8,128)(2,1)S(1)} %get-tuple-element.62.normed, bf16[384,2048]{1,0:T(8,128)(2,1)S(1)} %get-tuple-element.66.near_d_pre, ...), custom_call_target="tpu_custom_call" | custom-call | flops 1024 | bytes 1024 | tf_op jit(solution)/shard_map/pallas_call | solution.py:345
  36.7 0.3 collective-permute-start.5
  37.0 1.8 %shard_map.82 = (bf16[128,1024]{1,0:T(8,128)(2,1)S(1)}, bf16[256,1024]{1,0:T(8,128)(2,1)S(1)}) custom-call(bf16[384,2048]{1,0:T(8,128)(2,1)S(1)} %get-tuple-element.66.near_d_pre, bf16[1024,4096]{1,0:T(8,128)(2,1)S(1)} %bitcast.6), custom_call_target="tpu_custom_call" | custom-call | flops 1024 | bytes 1024 | tf_op jit(solution)/shard_map/pallas_call | solution.py:418
  38.8 1.4 %collective-permute-start.10 = (bf16[256,1024]{1,0:T(8,128)(2,1)S(1)}, bf16[256,1024]{1,0:T(8,128)(2,1)S(1)}, u32[]{:S(2)}, u32[]{:S(2)}) collective-permute-start(bf16[256,1024]{1,0:T(8,128)(2,1)S(1)} %get-tuple-element.67), channel_id=1, source_target_pairs={{2,0},{4,2},{6,4},{8,6},{10,8},{12,10},{14,12},{16,14},{18,16},{20... | collective-permute-start | bytes 1572872 | tf_op jit(solution)/shard_map/ppermute | solution.py:48
  40.3 0.6 shard_map.83
  40.9 4.6 %collective-permute-start.6 = (bf16[4,4,8,512]{3,2,1,0:T(8,128)(2,1)S(1)}, bf16[4,4,8,512]{3,2,1,0:T(8,128)(2,1)S(1)}, u32[]{:S(2)}, u32[]{:S(2)}) collective-permute-start(bf16[4,4,8,512]{3,2,1,0:T(8,128)(2,1)S(1)} %get-tuple-element.74), channel_id=1, source_target_pairs={{0,2},{1,9},{2,4},{3,11},{4,6},{5,13},{6,0},{7,15},{8,10},{9,17},{... | collective-permute-start | bytes 393224 | tf_op jit(solution)/shard_map/ppermute | solution.py:48
  45.5 3.2 %collective-permute-start.7 = (bf16[4,4,8,512]{3,2,1,0:T(8,128)(2,1)S(1)}, bf16[4,4,8,512]{3,2,1,0:T(8,128)(2,1)S(1)}, u32[]{:S(2)}, u32[]{:S(2)}) collective-permute-start(bf16[4,4,8,512]{3,2,1,0:T(8,128)(2,1)S(1)} %get-tuple-element.75), channel_id=1, source_target_pairs={{0,6},{1,25},{2,0},{3,27},{4,2},{5,29},{6,4},{7,31},{8,14},{9,1},{... | collective-permute-start | bytes 393224 | tf_op jit(solution)/shard_map/ppermute | solution.py:48
  48.7 0.7 collective-permute-start.11
  49.4 2.9 %shard_map.84 = (f32[256,1024]{1,0:T(8,128)S(1)}, bf16[256,1024]{1,0:T(8,128)(2,1)S(1)}) custom-call(bf16[256,4096]{1,0:T(8,128)(2,1)S(1)} %get-tuple-element.70.d_pre, bf16[256,1024]{1,0:T(8,128)(2,1)S(1)} %get-tuple-element.71.gated, bf16[128,1024]{1,0:T(8,128)(2,1)S(1)} %get-tuple-element.48.mine, bf16[128,1024]{1,0:T(8,128)(2,1)S(1)} %collective-permute-done.3.second, ...), custom_call_target="tpu_custom_call" | custom-call | flops 1024 | bytes 1024 | tf_op jit(solution)/shard_map/pallas_call | solution.py:443
  52.3 0.2 collective-permute-done.6.from_below
  52.5 0.9 collective-permute-done.7.from_above
  53.4 0.1 shard_map.85
  53.4 2.5 %collective-permute-start.8 = (bf16[8,4,8,512]{3,2,1,0:T(8,128)(2,1)S(1)}, bf16[8,4,8,512]{3,2,1,0:T(8,128)(2,1)S(1)}, u32[]{:S(2)}, u32[]{:S(2)}) collective-permute-start(bf16[8,4,8,512]{3,2,1,0:T(8,128)(2,1)S(1)} %get-tuple-element.79), channel_id=1, source_target_pairs={{0,2},{1,9},{2,4},{3,11},{4,6},{5,13},{6,0},{7,15},{8,10},{9,17},{... | collective-permute-start | bytes 786440 | tf_op jit(solution)/shard_map/ppermute | solution.py:48
  56.0 2.2 %collective-permute-start.9 = (bf16[8,4,8,512]{3,2,1,0:T(8,128)(2,1)S(1)}, bf16[8,4,8,512]{3,2,1,0:T(8,128)(2,1)S(1)}, u32[]{:S(2)}, u32[]{:S(2)}) collective-permute-start(bf16[8,4,8,512]{3,2,1,0:T(8,128)(2,1)S(1)} %get-tuple-element.80), channel_id=1, source_target_pairs={{0,6},{1,25},{2,0},{3,27},{4,2},{5,29},{6,4},{7,31},{8,14},{9,1},{... | collective-permute-start | bytes 786440 | tf_op jit(solution)/shard_map/ppermute | solution.py:48
  58.2 0.9 shard_map.86
  59.0 0.8 collective-permute-start.12
  59.8 6.0 %collective-permute-done.8.from_below = bf16[8,4,8,512]{3,2,1,0:T(8,128)(2,1)S(1)} collective-permute-done((bf16[8,4,8,512]{3,2,1,0:T(8,128)(2,1)S(1)}, bf16[8,4,8,512]{3,2,1,0:T(8,128)(2,1)S(1)}, u32[]{:S(2)}, u32[]{:S(2)}) %collective-permute-start.8) | collective-permute-done | bytes 262176 | tf_op jit(solution)/shard_map/ppermute | solution.py:48
  65.9 0.8 shard_map.88
  66.7 15.2 %all-to-all-start = ((bf16[32,8,512]{2,1,0:T(8,128)(2,1)}), bf16[32,8,512]{2,1,0:T(8,128)(2,1)S(1)}, u32[]{:S(2)}, u32[]{:S(2)}) async-start(bf16[32,8,512]{2,1,0:T(8,128)(2,1)} %bitcast.4), calls=%async_computation | async-start | bytes 524288 | tf_op jit(solution)/shard_map/all_to_all | solution.py:588
  81.9 1.6 %shard_map.87 = (bf16[256,1024]{1,0:T(8,128)(2,1)}, bf16[256,1024]{1,0:T(8,128)(2,1)}) custom-call(bf16[256,1024]{1,0:T(8,128)(2,1)S(1)} %bitcast.8, bf16[256,1024]{1,0:T(8,128)(2,1)S(1)} %bitcast.10, bf16[256,1024]{1,0:T(8,128)(2,1)S(1)} %get-tuple-element.72.outs, f32[128,1024]{1,0:T(8,128)S(1)} %get-tuple-element.84.own, ...), custom_call_target="tpu_custom_call" | custom-call | flops 4194304 | bytes 4194304 | tf_op jit(solution)/shard_map/pallas_call | solution.py:505
  83.6 9.1 %all-to-all-done.parts = bf16[32,8,512]{2,1,0:T(8,128)(2,1)S(1)} async-done(((bf16[32,8,512]{2,1,0:T(8,128)(2,1)}), bf16[32,8,512]{2,1,0:T(8,128)(2,1)S(1)}, u32[]{:S(2)}, u32[]{:S(2)}) %all-to-all-start) | async-done | bytes 262176 | tf_op jit(solution)/shard_map/all_to_all | solution.py:588
  92.7 0.7 shard_map.89
  (27 shorter events, 0.2 us)
Async XLA Ops:
  0.6 1.0 %copy-start.1 = (bf16[1,1,256,1024]{3,2,1,0:T(8,128)(2,1)S(1)}, bf16[1,1,256,1024]{3,2,1,0:T(8,128)(2,1)}, u32[]{:S(2)}) copy-start(bf16[1,1,256,1024]{3,2,1,0:T(8,128)(2,1)} %param.5) | copy-start | bytes 1572868
  1.7 8.2 %collective-permute-start = (bf16[128,1024]{1,0:T(8,128)(2,1)S(1)}, bf16[128,1024]{1,0:T(8,128)(2,1)S(1)}, u32[]{:S(2)}, u32[]{:S(2)}) collective-permute-start(bf16[128,1024]{1,0:T(8,128)(2,1)S(1)} %get-tuple-element.47), channel_id=1, source_target_pairs={{1,2},{3,4},{5,6},{7,8},{9,10},{11,12},{13,14},{15,16},{17,18},{19... | collective-permute-start | bytes 786440 | tf_op jit(solution)/shard_map/ppermute | solution.py:48
  2.4 8.2 %collective-permute-start.3 = (bf16[128,1024]{1,0:T(8,128)(2,1)S(1)}, bf16[128,1024]{1,0:T(8,128)(2,1)S(1)}, u32[]{:S(2)}, u32[]{:S(2)}) collective-permute-start(bf16[128,1024]{1,0:T(8,128)(2,1)S(1)} %get-tuple-element.47), channel_id=1, source_target_pairs={{0,1},{1,0},{2,3},{3,2},{4,5},{5,4},{6,7},{7,6},{8,9},{9,8},{10,11... | collective-permute-start | bytes 786440 | tf_op jit(solution)/shard_map/ppermute | solution.py:48
  5.3 1.0 %copy-start.3 = (bf16[1,1,256,1024]{3,2,1,0:T(8,128)(2,1)S(1)}, bf16[1,1,256,1024]{3,2,1,0:T(8,128)(2,1)}, u32[]{:S(2)}) copy-start(bf16[1,1,256,1024]{3,2,1,0:T(8,128)(2,1)} %param.9) | copy-start | bytes 1572868
  6.5 4.2 %collective-permute-start.4 = (bf16[128,1024]{1,0:T(8,128)(2,1)S(1)}, bf16[128,1024]{1,0:T(8,128)(2,1)S(1)}, u32[]{:S(2)}, u32[]{:S(2)}) collective-permute-start(bf16[128,1024]{1,0:T(8,128)(2,1)S(1)} %get-tuple-element.50), channel_id=1, source_target_pairs={{0,1},{1,0},{2,3},{3,2},{4,5},{5,4},{6,7},{7,6},{8,9},{9,8},{10,11... | collective-permute-start | bytes 786440 | tf_op jit(solution)/shard_map/ppermute | solution.py:48
  6.6 11.6 %collective-permute-start.2 = (bf16[128,1024]{1,0:T(8,128)(2,1)S(1)}, bf16[128,1024]{1,0:T(8,128)(2,1)S(1)}, u32[]{:S(2)}, u32[]{:S(2)}) collective-permute-start(bf16[128,1024]{1,0:T(8,128)(2,1)S(1)} %get-tuple-element.48.mine), channel_id=1, source_target_pairs={{0,2},{2,4},{4,6},{6,8},{8,10},{10,12},{12,14},{14,16},{16,18},{18... | collective-permute-start | bytes 786440 | tf_op jit(solution)/shard_map/ppermute | solution.py:48
  10.0 8.2 %collective-permute-start.1 = (bf16[128,1024]{1,0:T(8,128)(2,1)S(1)}, bf16[128,1024]{1,0:T(8,128)(2,1)S(1)}, u32[]{:S(2)}, u32[]{:S(2)}) collective-permute-start(bf16[128,1024]{1,0:T(8,128)(2,1)S(1)} %collective-permute-done.odd), channel_id=1, source_target_pairs={{2,4},{4,6},{6,8},{8,10},{10,12},{12,14},{14,16},{16,18},{18,20},{... | collective-permute-start | bytes 786440 | tf_op jit(solution)/shard_map/ppermute | solution.py:48
  18.2 4.6 %copy-start.5 = (s32[1,4]{1,0:T(1,128)S(1)}, s32[1,4]{1,0:T(1,128)}, u32[]{:S(2)}) copy-start(s32[1,4]{1,0:T(1,128)} %lengths.1) | copy-start | bytes 52
  18.2 18.8 %slice-start = ((s8[8388608]{0:T(1024)(128)(4,1)}), s8[4194304]{0:T(1024)(128)(4,1)S(1)}, s32[]{:S(2)}) async-start(s8[8388608]{0:T(1024)(128)(4,1)} %bitcast.5), calls=%async_computation.1 | async-start | bytes 8388608
  22.8 14.2 %slice-start.1 = ((s8[8388608]{0:T(1024)(128)(4,1)}), s8[4194304]{0:T(1024)(128)(4,1)S(1)}, s32[]{:S(2)}) async-start(s8[8388608]{0:T(1024)(128)(4,1)} %bitcast.5), calls=%async_computation.2 | async-start | bytes 8388608
  36.7 3.6 %collective-permute-start.5 = (bf16[4,8,4,8,512]{4,3,2,1,0:T(8,128)(2,1)S(1)}, bf16[4,8,4,8,512]{4,3,2,1,0:T(8,128)(2,1)S(1)}, u32[]{:S(2)}, u32[]{:S(2)}) collective-permute-start(bf16[4,8,4,8,512]{4,3,2,1,0:T(8,128)(2,1)S(1)} %get-tuple-element.65), channel_id=1, source_target_pairs={{0,1},{1,0},{2,3},{3,2},{4,5},{5,4},{6,7},{7,6},{8,9},{9,8},{10,11... | collective-permute-start | bytes 3145736 | tf_op jit(solution)/shard_map/ppermute | solution.py:48
  38.8 10.5 %copy-start = (bf16[1024,1024]{1,0:T(8,128)(2,1)S(1)}, bf16[1024,1024]{1,0:T(8,128)(2,1)}, u32[]{:S(2)}) copy-start(bf16[1024,1024]{1,0:T(8,128)(2,1)} %weight_out.3) | copy-start | bytes 6291460
  38.8 19.3 %collective-permute-start.10 = (bf16[256,1024]{1,0:T(8,128)(2,1)S(1)}, bf16[256,1024]{1,0:T(8,128)(2,1)S(1)}, u32[]{:S(2)}, u32[]{:S(2)}) collective-permute-start(bf16[256,1024]{1,0:T(8,128)(2,1)S(1)} %get-tuple-element.67), channel_id=1, source_target_pairs={{2,0},{4,2},{6,4},{8,6},{10,8},{12,10},{14,12},{16,14},{18,16},{20... | collective-permute-start | bytes 1572872 | tf_op jit(solution)/shard_map/ppermute | solution.py:48
  40.9 11.6 %collective-permute-start.6 = (bf16[4,4,8,512]{3,2,1,0:T(8,128)(2,1)S(1)}, bf16[4,4,8,512]{3,2,1,0:T(8,128)(2,1)S(1)}, u32[]{:S(2)}, u32[]{:S(2)}) collective-permute-start(bf16[4,4,8,512]{3,2,1,0:T(8,128)(2,1)S(1)} %get-tuple-element.74), channel_id=1, source_target_pairs={{0,2},{1,9},{2,4},{3,11},{4,6},{5,13},{6,0},{7,15},{8,10},{9,17},{... | collective-permute-start | bytes 393224 | tf_op jit(solution)/shard_map/ppermute | solution.py:48
  45.5 7.9 %collective-permute-start.7 = (bf16[4,4,8,512]{3,2,1,0:T(8,128)(2,1)S(1)}, bf16[4,4,8,512]{3,2,1,0:T(8,128)(2,1)S(1)}, u32[]{:S(2)}, u32[]{:S(2)}) collective-permute-start(bf16[4,4,8,512]{3,2,1,0:T(8,128)(2,1)S(1)} %get-tuple-element.75), channel_id=1, source_target_pairs={{0,6},{1,25},{2,0},{3,27},{4,2},{5,29},{6,4},{7,31},{8,14},{9,1},{... | collective-permute-start | bytes 393224 | tf_op jit(solution)/shard_map/ppermute | solution.py:48
  48.7 11.1 %collective-permute-start.11 = (bf16[128,1024]{1,0:T(8,128)(2,1)S(1)}, bf16[128,1024]{1,0:T(8,128)(2,1)S(1)}, u32[]{:S(2)}, u32[]{:S(2)}) collective-permute-start(bf16[128,1024]{1,0:T(8,128)(2,1)S(1)} %get-tuple-element.83), channel_id=1, source_target_pairs={{4,1},{6,3},{8,5},{10,7},{12,9},{14,11},{16,13},{18,15},{20,17},{2... | collective-permute-start | bytes 786440 | tf_op jit(solution)/shard_map/ppermute | solution.py:48
  53.4 12.4 %collective-permute-start.8 = (bf16[8,4,8,512]{3,2,1,0:T(8,128)(2,1)S(1)}, bf16[8,4,8,512]{3,2,1,0:T(8,128)(2,1)S(1)}, u32[]{:S(2)}, u32[]{:S(2)}) collective-permute-start(bf16[8,4,8,512]{3,2,1,0:T(8,128)(2,1)S(1)} %get-tuple-element.79), channel_id=1, source_target_pairs={{0,2},{1,9},{2,4},{3,11},{4,6},{5,13},{6,0},{7,15},{8,10},{9,17},{... | collective-permute-start | bytes 786440 | tf_op jit(solution)/shard_map/ppermute | solution.py:48
  56.0 9.9 %collective-permute-start.9 = (bf16[8,4,8,512]{3,2,1,0:T(8,128)(2,1)S(1)}, bf16[8,4,8,512]{3,2,1,0:T(8,128)(2,1)S(1)}, u32[]{:S(2)}, u32[]{:S(2)}) collective-permute-start(bf16[8,4,8,512]{3,2,1,0:T(8,128)(2,1)S(1)} %get-tuple-element.80), channel_id=1, source_target_pairs={{0,6},{1,25},{2,0},{3,27},{4,2},{5,29},{6,4},{7,31},{8,14},{9,1},{... | collective-permute-start | bytes 786440 | tf_op jit(solution)/shard_map/ppermute | solution.py:48
  58.2 23.8 %copy-start.2 = (bf16[1,1,256,1024]{3,2,1,0:T(8,128)(2,1)S(1)}, bf16[1,1,256,1024]{3,2,1,0:T(8,128)(2,1)}, u32[]{:S(2)}) copy-start(bf16[1,1,256,1024]{3,2,1,0:T(8,128)(2,1)} %param.5) | copy-start | bytes 1572868
  58.2 23.8 %copy-start.4 = (bf16[1,1,256,1024]{3,2,1,0:T(8,128)(2,1)S(1)}, bf16[1,1,256,1024]{3,2,1,0:T(8,128)(2,1)}, u32[]{:S(2)}) copy-start(bf16[1,1,256,1024]{3,2,1,0:T(8,128)(2,1)} %param.9) | copy-start | bytes 1572868
  59.0 22.9 %collective-permute-start.12 = (bf16[256,1024]{1,0:T(8,128)(2,1)}, bf16[256,1024]{1,0:T(8,128)(2,1)S(1)}, u32[]{:S(2)}, u32[]{:S(2)}) collective-permute-start(bf16[256,1024]{1,0:T(8,128)(2,1)} %get-tuple-element.85), channel_id=1, source_target_pairs={{0,1},{1,0},{2,3},{3,2},{4,5},{5,4},{6,7},{7,6},{8,9},{9,8},{10,11... | collective-permute-start | bytes 1572872 | tf_op jit(solution)/shard_map/ppermute | solution.py:48
  66.7 26.1 %all-to-all-start = ((bf16[32,8,512]{2,1,0:T(8,128)(2,1)}), bf16[32,8,512]{2,1,0:T(8,128)(2,1)S(1)}, u32[]{:S(2)}, u32[]{:S(2)}) async-start(bf16[32,8,512]{2,1,0:T(8,128)(2,1)} %bitcast.4), calls=%async_computation | async-start | bytes 524288 | tf_op jit(solution)/shard_map/all_to_all | solution.py:588

commit v3 on v2

--- a/solution.py
+++ b/solution.py
@@ -36,12 +36,11 @@
 def routes(pairs):
     chips = pairs // 2
     place = [chain_device(block, chips) for block in range(pairs)]
-    near_odd = [(tile_owner(2 * b - 1, pairs), place[b]) for b in range(1, pairs)]
-    near_even = [(tile_owner(2 * b - 2, pairs), place[b]) for b in range(1, pairs)]
-    onward = [(place[b - 1], place[b]) for b in range(2, pairs)]
+    onward = [(place[b - 1], place[b]) for b in range(1, pairs)]
+    far = [(tile_owner(2 * b - 3, pairs), place[b]) for b in range(2, pairs)]
     back = [(place[b], place[b - 1]) for b in range(1, pairs)]
     far_back = [(place[b], tile_owner(2 * b - 3, pairs)) for b in range(2, pairs)]
-    return near_odd, near_even, onward, back, far_back
+    return onward, far, back, far_back
 
 
 def move(block, route):
@@ -63,10 +62,9 @@
 
 
 def silu_pair(half):
-    bend = jnp.tanh(half)
-    silu = half + half * bend
-    sigmoid = 0.5 + 0.5 * bend
-    return silu, sigmoid + silu * (1.0 - sigmoid)
+    rise = 1.0 + jnp.tanh(half)
+    silu = half * rise
+    return silu, rise * ((0.5 + half) - 0.5 * silu)
 
 
 def dot_nn(left, right):
@@ -101,7 +99,7 @@
         copy.wait()
 
 
-def split(array, cost):
+def split(array):
     tile = jax.ShapeDtypeStruct((TILE, array.shape[1]), BF16)
     return pl.pallas_call(
         split_kernel,
@@ -110,97 +108,85 @@
         out_shape=[tile, tile],
         scratch_shapes=[pltpu.SemaphoreType.DMA((2,))],
         compiler_params=pltpu.CompilerParams(vmem_limit_bytes=2 * MIB),
-        cost_estimate=pl.CostEstimate(flops=0, bytes_accessed=cost, transcendentals=0),
+        cost_estimate=pl.CostEstimate(flops=8 * 1024 * MIB, bytes_accessed=24 * MIB, transcendentals=0),
     )(array)
 
 
-def project_columns(normed, weight, columns, proj, slope, copies):
+def project_columns(normed, weight, columns, proj, slope):
     step = 512
     for n, at in enumerate(columns):
-        copies[n].wait()
-        silu, bent = silu_pair(0.5 * dot_nn(normed[...], weight[:, n * step : (n + 1) * step]))
+        pre = dot_nn(normed[...], weight[:, at : at + step])
+        silu, bent = silu_pair(0.5 * pre)
         proj[:, n * step : (n + 1) * step] = silu.astype(BF16)
         slope[:, n * step : (n + 1) * step] = bent.astype(BF16)
 
 
-def fetch_columns(weight, columns, held, sems):
-    step = 512
-    copies = [
-        pltpu.make_async_copy(weight.at[:, at : at + step], held.at[:, n * step : (n + 1) * step], sems.at[n])
-        for n, at in enumerate(columns)
-    ]
-    for copy in copies:
-        copy.start()
-    return copies
-
-
-def project_kernel(
-    mine, second, back_mine, back_second, weight, weight_out, normed, proj, slope, d_gated,
-    held, held_out, sems,
-):
-    width = weight.shape[0]
-    columns = range(0, 4 * width, 512)
-    copies = fetch_columns(weight, columns, held, sems)
-    last = pltpu.make_async_copy(weight_out, held_out, sems.at[len(copies)])
-    last.start()
+def normalize_kernel(mine, second, normed):
     for r, tile in enumerate((mine, second)):
         rows = slice(r * TILE, (r + 1) * TILE)
         normed[rows, :] = normalize(tile[...].astype(F32))[0].astype(BF16)
-    project_columns(normed, held, columns, proj, slope, copies)
-    last.wait()
+
+
+def normalize_block(mine, second):
+    rows, width = mine.shape
+    return pl.pallas_call(
+        normalize_kernel,
+        in_specs=[whole()] * 2,
+        out_specs=whole(),
+        out_shape=jax.ShapeDtypeStruct((2 * rows, width), BF16),
+        compiler_params=pltpu.CompilerParams(vmem_limit_bytes=2 * MIB),
+        cost_estimate=pl.CostEstimate(flops=1024 * MIB, bytes_accessed=MIB, transcendentals=0),
+    )(mine, second)
+
+
+def project_kernel(normed, back_mine, back_second, weight_in, weight_out, proj, slope, d_gated):
+    width = weight_in.shape[0]
+    project_columns(normed, weight_in, range(0, 4 * width, 512), proj, slope)
     for n in range(0, width, 256):
-        part = held_out[n : n + 256, :]
+        part = weight_out[n : n + 256, :]
         d_gated[:TILE, n : n + 256] = dot_nt(back_mine[...], part)
         d_gated[TILE:, n : n + 256] = dot_nt(back_second[...], part)
 
 
-def project(mine, second, back_mine, back_second, weight, weight_out):
+def project(normed, back_mine, back_second, weight, weight_out):
     width, columns = weight.shape
     rows = 2 * TILE
-    shapes = [((rows, width), BF16), ((rows, columns), BF16), ((rows, columns), BF16), ((rows, width), F32)]
+    shapes = [((rows, columns), BF16), ((rows, columns), BF16), ((rows, width), F32)]
     return pl.pallas_call(
         project_kernel,
-        in_specs=[whole()] * 4 + [remote()] * 2,
-        out_specs=[whole()] * 4,
+        in_specs=[whole()] * 5,
+        out_specs=[whole()] * 3,
         out_shape=[jax.ShapeDtypeStruct(*s) for s in shapes],
-        scratch_shapes=[
-            pltpu.VMEM(weight.shape, BF16),
-            pltpu.VMEM(weight_out.shape, BF16),
-            pltpu.SemaphoreType.DMA((columns // 512 + 1,)),
-        ],
-        compiler_params=pltpu.CompilerParams(vmem_limit_bytes=47 * MIB),
+        compiler_params=pltpu.CompilerParams(vmem_limit_bytes=SCOPED),
         cost_estimate=pl.CostEstimate(
             flops=2 * rows * width * (columns + width),
             bytes_accessed=2 * (width * columns + 2 * rows * columns),
             transcendentals=rows * columns,
         ),
-    )(mine, second, back_mine, back_second, weight, weight_out)
-
-
-def project_near_kernel(far, even, odd, weight, normed, proj, slope, held, sems):
+    )(normed, back_mine, back_second, weight, weight_out)
+
+
+def project_near_kernel(far, near, weight, normed, proj, slope):
     width = weight.shape[0]
+    normed[:TILE, :] = normalize(far[...].astype(F32))[0].astype(BF16)
+    normed[TILE:, :] = near[...]
     columns = [part * width + at for part in (1, 3) for at in range(0, width, 512)]
-    copies = fetch_columns(weight, columns, held, sems)
-    for r, tile in enumerate((far, even, odd)):
-        rows = slice(r * TILE, (r + 1) * TILE)
-        normed[rows, :] = normalize(tile[...].astype(F32))[0].astype(BF16)
-    project_columns(normed, held, columns, proj, slope, copies)
-
-
-def project_near(tiles, weight):
+    project_columns(normed, weight, columns, proj, slope)
+
+
+def project_near(far, near, weight):
     rows, width = 3 * TILE, weight.shape[0]
     shapes = [((rows, width), BF16), ((rows, 2 * width), BF16), ((rows, 2 * width), BF16)]
     return pl.pallas_call(
         project_near_kernel,
-        in_specs=[whole()] * 3 + [remote()],
+        in_specs=[whole()] * 3,
         out_specs=[whole()] * 3,
         out_shape=[jax.ShapeDtypeStruct(*s) for s in shapes],
-        scratch_shapes=[pltpu.VMEM((width, 2 * width), BF16), pltpu.SemaphoreType.DMA((4,))],
-        compiler_params=pltpu.CompilerParams(vmem_limit_bytes=44 * MIB),
+        compiler_params=pltpu.CompilerParams(vmem_limit_bytes=SCOPED),
         cost_estimate=pl.CostEstimate(
             flops=4 * rows * width * width, bytes_accessed=8 * width * width, transcendentals=2 * rows * width
         ),
-    )(*tiles, weight)
+    )(far, near, weight)
 
 
 def attention_kernel(
@@ -238,10 +224,11 @@
         near_v, near_k = pl.ds(pl.multiple_of(h * HEAD, HEAD), HEAD), head_slices(h)[1]
         keys = jnp.concatenate([near[:, near_k], proj[:, at_k]], axis=0)
         values = jnp.concatenate([near[:, near_v], proj[:, at_v]], axis=0)
+        all_scores = dot_nt(proj[:, at_q], keys)
         for r in range(2):
             rows = slice(r * TILE, (r + 1) * TILE)
             window = slice(r * TILE, r * TILE + columns)
-            scores = dot_nt(proj[rows, at_q], keys[window])
+            scores = all_scores[rows, window]
             silu, bent = silu_pair(scores * (0.5 * SCALE))
             att = (silu * factor[r]).astype(BF16)
             att_all[h, r] = att
@@ -249,7 +236,7 @@
             attended[rows, near_v] = dot_nn(att, values[window])
         return carry
 
-    lax.fori_loop(0, HEADS, forward, 0, unroll=2)
+    lax.fori_loop(0, HEADS, forward, 0, unroll=8)
 
     for r in range(2):
         rows = slice(r * TILE, (r + 1) * TILE)
@@ -265,30 +252,34 @@
         near_v, near_k = pl.ds(pl.multiple_of(h * HEAD, HEAD), HEAD), head_slices(h)[1]
         keys = jnp.concatenate([near[:, near_k], proj[:, at_k]], axis=0)
         values = jnp.concatenate([near[:, near_v], proj[:, at_v]], axis=0)
-        d_keys, d_values = [], []
+        blank = jnp.zeros((TILE, TILE), BF16)
+
+        def spread(parts):
+            return jnp.concatenate(
+                [jnp.concatenate([parts[0], blank], axis=1), jnp.concatenate([blank, parts[1]], axis=1)], axis=0
+            )
+
+        queries, upstream = proj[:, at_q], d_attended[:, near_v]
+        d_scores = []
+        d_all = dot_nt(upstream, values)
         for r in range(2):
             rows = slice(r * TILE, (r + 1) * TILE)
             window = slice(r * TILE, r * TILE + columns)
-            upstream = d_attended[rows, near_v]
-            d_att = dot_nt(upstream, values[window])
-            d_scores = (d_att * bent_all[h, r].astype(F32)).astype(BF16)
-            d_query = dot_nn(d_scores, keys[window]) * SCALE
-            d_pre[rows, at_q] = (d_query * slope[rows, at_q].astype(F32)).astype(BF16)
-            d_keys.append(dot_tn(d_scores, proj[rows, at_q]))
-            d_values.append(dot_tn(att_all[h, r], upstream))
-        for (first, second), own_at, near_at, scaled in (
-            (d_keys, at_k, near_k, SCALE),
-            (d_values, at_v, near_v, 1.0),
-        ):
-            both = first[TILE:] + second[:-TILE]
-            total = jnp.concatenate([first[:TILE], both, second[-TILE:]], axis=0) * scaled
+            d_att = d_all[rows, window]
+            d_scores.append((d_att * bent_all[h, r].astype(F32)).astype(BF16))
+        d_scores = spread(d_scores)
+        d_query = dot_nn(d_scores, keys) * SCALE
+        d_pre[:, at_q] = (d_query * slope[:, at_q].astype(F32)).astype(BF16)
+        d_key = dot_tn(d_scores, queries) * SCALE
+        d_value = dot_tn(spread([att_all[h, 0], att_all[h, 1]]), upstream)
+        for total, own_at, near_at in ((d_key, at_k, near_k), (d_value, at_v, near_v)):
             near_d_pre[:, near_at] = (
                 total[:halo] * near_slope[:, near_at].astype(F32)
             ).astype(BF16)
             d_pre[:, own_at] = (total[halo:] * slope[:, own_at].astype(F32)).astype(BF16)
         return carry
 
-    lax.fori_loop(0, HEADS, backward, 0, unroll=2)
+    lax.fori_loop(0, HEADS, backward, 0, unroll=8)
 
 
 def attention(lengths, proj, slope, near, near_slope, d_gated):
@@ -332,10 +323,8 @@
         kept = jnp.where(even, first, last).astype(BF16)
         sent = jnp.where(even, last, first).astype(BF16)
         for y in range(side):
-            for x in range(side):
-                by_row, by_column = y * side + x, x * side + y
-                keep[y, z, x] = jnp.where(even, kept[by_column], kept[by_row])
-                send[y, z, x] = jnp.where(even, sent[by_row], sent[by_column])
+            keep[y, z] = kept[y * side : (y + 1) * side]
+            send[y, z] = sent[y * side : (y + 1) * side]
 
 
 def key_grad(near_normed, normed, near_d_pre, d_pre):
@@ -352,21 +341,8 @@
     )(near_normed, normed, near_d_pre, d_pre)
 
 
-def ring_place():
-    return jnp.where(lax.axis_index("core") == 0, lax.axis_index("x"), lax.axis_index("y"))
-
-
-def ring_route(shift):
-    route = []
-    for pair in range(32):
-        y, x, core = pair // 8, pair // 2 % 4, pair % 2
-        y, x = (y, (x + shift) % 4) if core == 0 else ((y + shift) % 4, x)
-        route.append((pair, y * 8 + x * 2 + core))
-    return route
-
-
 def ring_first_kernel(keep, received, total, up, down):
-    place = ring_place()
+    place = lax.axis_index("y")
     half = up.shape[0]
     total[...] = (keep[...].astype(F32) + received[...].astype(F32)).astype(BF16)
     opposite = total.at[lax.rem(place + 2, 4)]
@@ -375,7 +351,7 @@
 
 
 def ring_second_kernel(total, from_below, from_above, up, down):
-    place = ring_place()
+    place = lax.axis_index("y")
     half = from_below.shape[0]
     above, below = total.at[lax.rem(place + 1, 4)], total.at[lax.rem(place + 3, 4)]
     up[:half] = (above[:half].astype(F32) + from_below[...].astype(F32)).astype(BF16)
@@ -385,7 +361,7 @@
 
 
 def ring_third_kernel(total, from_below, from_above, column):
-    own = total.at[ring_place()]
+    own = total.at[lax.axis_index("y")]
     column[...] = (
         own[...].astype(F32) + from_below[...].astype(F32) + from_above[...].astype(F32)
     ).astype(BF16)
@@ -536,59 +512,55 @@
     )(parts)
 
 
-def last_groups():
-    place = lambda z, y, x, core: ((z * 4 + y) * 4 + x) * 2 + core
-    even = [[place(z, y, x, 0) for z in range(8) for y in range(4)] for x in range(4)]
-    odd = [[place(z, y, x, 1) for z in range(8) for x in range(4)] for y in range(4)]
-    return even + odd
+def around(block, shift):
+    return lax.ppermute(block, "y", [(i, (i + shift) % 4) for i in range(4)])
 
 
 def shards(events, lengths, weight_in, weight_out, cotangent):
     pairs = lax.axis_size(SEQ)
-    near_odd, near_even, onward, backward, far_back = routes(pairs)
+    onward, far_on, backward, far_back = routes(pairs)
     swap = [(i, i ^ 1) for i in range(pairs)]
     local = events.reshape(2 * TILE, -1)
     back = cotangent.reshape(2 * TILE, -1)
 
-    mine, other = split(local, 24 * MIB)
-    odd = move(other, near_odd)
-    even = move(mine, near_even)
+    mine, other = split(local)
+    far = move(other, far_on)
     second = move(other, swap)
-    far = move(odd, onward)
-    back_mine, back_other = split(back, MIB)
+    back_mine, back_other = split(back)
     back_second = move(back_other, swap)
-
-    normed, proj, slope, d_gated = project(mine, second, back_mine, back_second, weight_in, weight_out)
-    far, even, odd, proj = lax.optimization_barrier((far, even, odd, proj))
-    near_normed, near, near_slope = project_near([far, even, odd], weight_in)
+    normed = normalize_block(mine, second)
+    near = move(normed, onward)
+
+    far, normed = lax.optimization_barrier((far, normed))
+    proj, slope, d_gated = project(normed, back_mine, back_second, weight_in, weight_out)
+    far, near, proj = lax.optimization_barrier((far, near, proj))
+    near_normed, near, near_slope = project_near(far, near, weight_in)
     gated, d_pre, near_d_pre = attention(lengths, proj, slope, near, near_slope, d_gated)
 
     tie = lax.optimization_barrier
+    far_d, near_d = near_through(near_d_pre, weight_in)
+    arrived = move(near_d, backward)
+    near_d_pre, near_d = tie((near_d_pre, near_d))
     send, keep = key_grad(near_normed, normed, near_d_pre, d_pre)
     received = move(send, swap)
-    near_d_pre, send = tie((near_d_pre, send))
-    far_d, near_d = near_through(near_d_pre, weight_in)
-    arrived = move(near_d, backward)
-    received, near_d = tie((received, near_d))
 
     block = keep.shape[1:]
     half = (block[0] // 2,) + block[1:]
     total, up, down = on_device(ring_first_kernel, [keep.shape, half, half], keep, received)
-    from_below, from_above = move(up, ring_route(1)), move(down, ring_route(-1))
-    d_pre, total = tie((d_pre, total))
+    from_below, from_above = around(up, 1), around(down, -1)
+    far_d, d_pre, total = tie((far_d, d_pre, total))
+    far_in = move(far_d, far_back)
     d_normed, outs = through(d_pre, gated, mine, second, weight_in, weight_out)
-    from_below, from_above, d_normed = tie((from_below, from_above, d_normed))
+    from_below, from_above, d_normed, far_in = tie((from_below, from_above, d_normed, far_in))
     up, down = on_device(ring_second_kernel, [block, block], total, from_below, from_above)
-    from_below, from_above = move(up, ring_route(1)), move(down, ring_route(-1))
+    from_below, from_above = around(up, 1), around(down, -1)
+    d_normed, up = tie((d_normed, up))
     own, given = merge(d_normed, arrived, outs)
-    far_in = move(far_d, far_back)
-    from_below, from_above, own, far_in = tie((from_below, from_above, own, far_in))
+    taken = move(given, swap)
+    from_below, from_above, taken = tie((from_below, from_above, taken))
     (column,) = on_device(ring_third_kernel, [block], total, from_below, from_above)
     column = column.reshape((block[0] * block[1],) + block[2:])
-    parts = lax.all_to_all(
-        column, ("dp",) + SEQ, split_axis=0, concat_axis=0, tiled=True, axis_index_groups=last_groups()
-    )
-    taken = move(given, swap)
+    parts = lax.all_to_all(column, ("dp", "x"), split_axis=0, concat_axis=0, tiled=True)
     layer_out, event_grads = finish(local, back, outs, own, taken, far_in)
     summed = sum_parts(parts)
     return (layer_out.reshape(events.shape), event_grads.reshape(events.shape), summed)

time: 95.2 us -> 88.8 us (0.933); the launches traced: 93.4 us -> 88.5 us
  waiting for transfers between devices: 16.3 us -> 26.9 us
  Pallas kernels: 35.3 us -> 25.5 us
  starting transfers between devices: 38.7 us -> 34.2 us
  local copies, waits for them, and re-layouts: 2.11 us -> 1.07 us
    ppermute x0 -> x4, waiting for transfers between devices: none -> 13.1 us  [around(): return lax.ppermute(block, 'y', [(i, (i + shift) % 4) for i in range(4)])]
    ppermute x0 -> x4, starting transfers between devices: none -> 13 us  [around(): return lax.ppermute(block, 'y', [(i, (i + shift) % 4) for i in range(4)])]
    ppermute x13 -> x8, starting transfers between devices: 23.4 us -> 11.1 us  [move(): return lax.ppermute(block, SEQ, route)]
    all_to_all x1, starting transfers between devices: 15.2 us -> 10 us  [shards(): lax.all_to_all(column, ('dp', 'x'), split_axis=0, concat_axis=0, tiled=True)]
    pallas_call x2 -> x3, Pallas kernels: 12 us -> 7.55 us  [the longest x1 4.57 us: project(): pl.pallas_call(project_kernel, in_specs=[whole()] * 5, out_specs=[whole()...]
    pallas_call x1, Pallas kernels: 11.8 us -> 7.37 us  [attention(): pl.pallas_call(attention_kernel, in_specs=[pl.BlockSpec(memory_space=pltp...]
    ppermute x13 -> x8, waiting for transfers between devices: 7.16 us -> 3.79 us  [move(): return lax.ppermute(block, SEQ, route)]
    unnamed x16 -> x14, local copies, waits for them, and re-layouts: 2.11 us -> 1.07 us
  transfers between devices with their start and end apart: 14 -> 13, of which waited for: 4 -> 8; matrix products, arithmetic and copies ran while one was open for 0% -> 0% of each run, Pallas kernels for 17% -> 11%
where the time goes in v3:
time: 88.8 us; the launch traced here: 88.5 us
  starting transfers between devices  34.2 us (39%)
  waiting for transfers between devices  26.9 us (30%)
  Pallas kernels  25.5 us (29%)
  local copies, waits for them, and re-layouts  1.07 us (1%)
    ppermute x4, waiting for transfers between devices, around(): return lax.ppermute(block, 'y', [(i, (i + shift) % 4) for i in range(4)])  13.1 us
    ppermute x4, starting transfers between devices, around(): return lax.ppermute(block, 'y', [(i, (i + shift) % 4) for i in range(4)])  13 us
    ppermute x8, starting transfers between devices, move(): return lax.ppermute(block, SEQ, route)  11.1 us
    all_to_all x1, starting transfers between devices, shards(): lax.all_to_all(column, ('dp', 'x'), split_axis=0, concat_axis=0, tiled=True)  10 us
    all_to_all x1, waiting for transfers between devices, shards(): lax.all_to_all(column, ('dp', 'x'), split_axis=0, concat_axis=0, tiled=True)  9.97 us
    pallas_call x1, Pallas kernels, attention(): pl.pallas_call(attention_kernel, in_specs=[pl.BlockSpec(memory_space=pltp...  7.37 us
    pallas_call x1, Pallas kernels, project(): pl.pallas_call(project_kernel, in_specs=[whole()] * 5, out_specs=[whole()...  4.57 us
    ppermute x8, waiting for transfers between devices, move(): return lax.ppermute(block, SEQ, route)  3.79 us
  transfers between devices with their start and end apart: 13, of which 8 were waited for; matrix products, arithmetic and copies ran while one was open for 0% of the time, Pallas kernels for 11%

profile of v3, /device:TPU:32, one launch (start us, length us, event | category | flops | bytes accessed | tf_op | source)
XLA Modules:
  0.0 88.5 jit_solution(12942926136719793567)
XLA Ops:
  0.6 1.0 %copy-done.1 = bf16[1,1,256,1024]{3,2,1,0:T(8,128)(2,1)S(1)} copy-done((bf16[1,1,256,1024]{3,2,1,0:T(8,128)(2,1)S(1)}, bf16[1,1,256,1024]{3,2,1,0:T(8,128)(2,1)}, u32[]{:S(2)}) %copy-start.1) | copy-done | bytes 524312
  1.8 0.1 collective-permute-start.1
  1.9 0.8 collective-permute-start
  2.7 0.7 collective-permute-done.1.second
  3.4 0.3 shard_map.77.normed
  3.7 3.7 %collective-permute-start.2 = (bf16[256,1024]{1,0:T(8,128)(2,1)S(1)}, bf16[256,1024]{1,0:T(8,128)(2,1)S(1)}, u32[]{:S(2)}, u32[]{:S(2)}) collective-permute-start(bf16[256,1024]{1,0:T(8,128)(2,1)S(1)} %shard_map.77.normed), channel_id=1, source_target_pairs={{0,2},{2,4},{4,6},{6,8},{8,10},{10,12},{12,14},{14,16},{16,18},{18... | collective-permute-start | bytes 1572872 | tf_op jit(solution)/shard_map/ppermute | solution.py:47
  7.5 1.6 %collective-permute-start.3 = (bf16[128,1024]{1,0:T(8,128)(2,1)S(1)}, bf16[128,1024]{1,0:T(8,128)(2,1)S(1)}, u32[]{:S(2)}, u32[]{:S(2)}) collective-permute-start(bf16[128,1024]{1,0:T(8,128)(2,1)S(1)} %get-tuple-element.53), channel_id=1, source_target_pairs={{0,1},{1,0},{2,3},{3,2},{4,5},{5,4},{6,7},{7,6},{8,9},{9,8},{10,11... | collective-permute-start | bytes 786440 | tf_op jit(solution)/shard_map/ppermute | solution.py:47
  9.2 1.2 %collective-permute-done.3.back_second = bf16[128,1024]{1,0:T(8,128)(2,1)S(1)} collective-permute-done((bf16[128,1024]{1,0:T(8,128)(2,1)S(1)}, bf16[128,1024]{1,0:T(8,128)(2,1)S(1)}, u32[]{:S(2)}, u32[]{:S(2)}) %collective-permute-start.3) | collective-permute-done | bytes 262176 | tf_op jit(solution)/shard_map/ppermute | solution.py:47
  10.3 4.6 %shard_map.79 = (bf16[256,4096]{1,0:T(8,128)(2,1)S(1)}, bf16[256,4096]{1,0:T(8,128)(2,1)S(1)}, f32[256,1024]{1,0:T(8,128)S(1)}) custom-call(bf16[256,1024]{1,0:T(8,128)(2,1)S(1)} %shard_map.77.normed, bf16[128,1024]{1,0:T(8,128)(2,1)S(1)} %get-tuple-element.52.back_mine, bf16[128,1024]{1,0:T(8,128)(2,1)S(1)} %collective-permute-done.3.back_second, ...), custom_call_target="tpu_custom_call" | custom-call | flops 2684354560 | bytes 12582912 | tf_op jit(solution)/shard_map/pallas_call | solution.py:155
  14.9 0.9 %collective-permute-done.2.near = bf16[256,1024]{1,0:T(8,128)(2,1)S(1)} collective-permute-done((bf16[256,1024]{1,0:T(8,128)(2,1)S(1)}, bf16[256,1024]{1,0:T(8,128)(2,1)S(1)}, u32[]{:S(2)}, u32[]{:S(2)}) %collective-permute-start.2) | collective-permute-done | bytes 524320 | tf_op jit(solution)/shard_map/ppermute | solution.py:47
  15.8 2.7 %shard_map.80 = (bf16[384,1024]{1,0:T(8,128)(2,1)S(1)}, bf16[384,2048]{1,0:T(8,128)(2,1)S(1)}, bf16[384,2048]{1,0:T(8,128)(2,1)S(1)}) custom-call(bf16[128,1024]{1,0:T(8,128)(2,1)S(1)} %collective-permute-done.far, bf16[256,1024]{1,0:T(8,128)(2,1)S(1)} %collective-permute-done.2.near, bf16[1024,4096]{1,0:T(8,128)(2,1)S(1)} %bitcast.6), custom_call_target="tpu_custom_call" | custom-call | flops 1610612736 | bytes 8388608 | tf_op jit(solution)/shard_map/pallas_call | solution.py:180
  18.5 7.4 %shard_map.81 = (bf16[256,1024]{1,0:T(8,128)(2,1)S(1)}, bf16[256,4096]{1,0:T(8,128)(2,1)S(1)}, bf16[384,2048]{1,0:T(8,128)(2,1)S(1)}) custom-call(s32[1,4]{1,0:T(1,128)S(1)} %copy-done.4, bf16[256,4096]{1,0:T(8,128)(2,1)S(1)} %get-tuple-element.55.proj, bf16[256,4096]{1,0:T(8,128)(2,1)S(1)} %get-tuple-element.56.slope, ...), custom_call_target="tpu_custom_call" | custom-call | flops 1677721600 | bytes 16777216 | tf_op jit(solution)/shard_map/pallas_call | solution.py:289
  25.9 1.8 %shard_map.82 = (bf16[128,1024]{1,0:T(8,128)(2,1)S(1)}, bf16[256,1024]{1,0:T(8,128)(2,1)S(1)}) custom-call(bf16[384,2048]{1,0:T(8,128)(2,1)S(1)} %get-tuple-element.67.near_d_pre, bf16[1024,4096]{1,0:T(8,128)(2,1)S(1)} %bitcast.6), custom_call_target="tpu_custom_call" | custom-call | flops 1024 | bytes 1024 | tf_op jit(solution)/shard_map/pallas_call | solution.py:394
  27.7 2.0 %shard_map.83 = (bf16[4,8,4,8,512]{4,3,2,1,0:T(8,128)(2,1)S(1)}, bf16[4,8,4,8,512]{4,3,2,1,0:T(8,128)(2,1)S(1)}) custom-call(bf16[384,1024]{1,0:T(8,128)(2,1)S(1)} %get-tuple-element.65.near_normed, bf16[256,1024]{1,0:T(8,128)(2,1)S(1)} %shard_map.77.normed, bf16[384,2048]{1,0:T(8,128)(2,1)S(1)} %get-tuple-element.67.near_d_pre, ...), custom_call_target="tpu_custom_call" | custom-call | flops 1024 | bytes 1024 | tf_op jit(solution)/shard_map/pallas_call | solution.py:334
  29.7 2.8 %collective-permute-start.4 = (bf16[4,8,4,8,512]{4,3,2,1,0:T(8,128)(2,1)S(1)}, bf16[4,8,4,8,512]{4,3,2,1,0:T(8,128)(2,1)S(1)}, u32[]{:S(2)}, u32[]{:S(2)}) collective-permute-start(bf16[4,8,4,8,512]{4,3,2,1,0:T(8,128)(2,1)S(1)} %get-tuple-element.69), channel_id=1, source_target_pairs={{0,1},{1,0},{2,3},{3,2},{4,5},{5,4},{6,7},{7,6},{8,9},{9,8},{10,11... | collective-permute-start | bytes 3145736 | tf_op jit(solution)/shard_map/ppermute | solution.py:47
  32.5 1.3 %collective-permute-start.8 = (bf16[256,1024]{1,0:T(8,128)(2,1)S(1)}, bf16[256,1024]{1,0:T(8,128)(2,1)S(1)}, u32[]{:S(2)}, u32[]{:S(2)}) collective-permute-start(bf16[256,1024]{1,0:T(8,128)(2,1)S(1)} %get-tuple-element.66), channel_id=1, source_target_pairs={{2,0},{4,2},{6,4},{8,6},{10,8},{12,10},{14,12},{16,14},{18,16},{20... | collective-permute-start | bytes 1572872 | tf_op jit(solution)/shard_map/ppermute | solution.py:47
  33.8 1.0 %collective-permute-done.4.received = bf16[4,8,4,8,512]{4,3,2,1,0:T(8,128)(2,1)S(1)} collective-permute-done((bf16[4,8,4,8,512]{4,3,2,1,0:T(8,128)(2,1)S(1)}, bf16[4,8,4,8,512]{4,3,2,1,0:T(8,128)(2,1)S(1)}, u32[]{:S(2)}, u32[]{:S(2)}) %collective-permute-start.4) | collective-permute-done | bytes 1048608 | tf_op jit(solution)/shard_map/ppermute | solution.py:47
  34.8 0.6 shard_map.84
  35.4 0.7 collective-permute-start.7
  36.0 7.9 %collective-permute-start.5 = (bf16[4,4,8,512]{3,2,1,0:T(8,128)(2,1)S(1)}, bf16[4,4,8,512]{3,2,1,0:T(8,128)(2,1)S(1)}, u32[]{:S(2)}, u32[]{:S(2)}) collective-permute-start(bf16[4,4,8,512]{3,2,1,0:T(8,128)(2,1)S(1)} %get-tuple-element.74), channel_id=1, source_target_pairs={{0,8},{8,16},{16,24},{24,0},{1,9},{9,17},{17,25},{25,1},{2,10},{10... | collective-permute-start | bytes 393224 | tf_op jit(solution)/shard_map/ppermute | solution.py:516
  43.9 1.5 %collective-permute-start.6 = (bf16[4,4,8,512]{3,2,1,0:T(8,128)(2,1)S(1)}, bf16[4,4,8,512]{3,2,1,0:T(8,128)(2,1)S(1)}, u32[]{:S(2)}, u32[]{:S(2)}) collective-permute-start(bf16[4,4,8,512]{3,2,1,0:T(8,128)(2,1)S(1)} %get-tuple-element.75), channel_id=1, source_target_pairs={{0,24},{8,0},{16,8},{24,16},{1,25},{9,1},{17,9},{25,17},{2,26},{10... | collective-permute-start | bytes 393224 | tf_op jit(solution)/shard_map/ppermute | solution.py:516
  45.4 2.9 %shard_map.85 = (f32[256,1024]{1,0:T(8,128)S(1)}, bf16[256,1024]{1,0:T(8,128)(2,1)S(1)}) custom-call(bf16[256,4096]{1,0:T(8,128)(2,1)S(1)} %get-tuple-element.71.d_pre, bf16[256,1024]{1,0:T(8,128)(2,1)S(1)} %get-tuple-element.72.gated, bf16[128,1024]{1,0:T(8,128)(2,1)S(1)} %get-tuple-element.49.mine, bf16[128,1024]{1,0:T(8,128)(2,1)S(1)} %collective-permute-done.1.second, ...), custom_call_target="tpu_custom_call" | custom-call | flops 1024 | bytes 1024 | tf_op jit(solution)/shard_map/pallas_call | solution.py:419
  48.3 3.9 %collective-permute-done.5.from_below = bf16[4,4,8,512]{3,2,1,0:T(8,128)(2,1)S(1)} collective-permute-done((bf16[4,4,8,512]{3,2,1,0:T(8,128)(2,1)S(1)}, bf16[4,4,8,512]{3,2,1,0:T(8,128)(2,1)S(1)}, u32[]{:S(2)}, u32[]{:S(2)}) %collective-permute-start.5) | collective-permute-done | bytes 131104 | tf_op jit(solution)/shard_map/ppermute | solution.py:516
  52.3 0.1 shard_map.87
  52.5 3.6 %collective-permute-start.10 = (bf16[8,4,8,512]{3,2,1,0:T(8,128)(2,1)S(1)}, bf16[8,4,8,512]{3,2,1,0:T(8,128)(2,1)S(1)}, u32[]{:S(2)}, u32[]{:S(2)}) collective-permute-start(bf16[8,4,8,512]{3,2,1,0:T(8,128)(2,1)S(1)} %get-tuple-element.85), channel_id=1, source_target_pairs={{0,24},{8,0},{16,8},{24,16},{1,25},{9,1},{17,9},{25,17},{2,26},{10... | collective-permute-start | bytes 786440 | tf_op jit(solution)/shard_map/ppermute | solution.py:516
  56.2 5.8 %collective-permute-done.10.from_above = bf16[8,4,8,512]{3,2,1,0:T(8,128)(2,1)S(1)} collective-permute-done((bf16[8,4,8,512]{3,2,1,0:T(8,128)(2,1)S(1)}, bf16[8,4,8,512]{3,2,1,0:T(8,128)(2,1)S(1)}, u32[]{:S(2)}, u32[]{:S(2)}) %collective-permute-start.10) | collective-permute-done | bytes 262176 | tf_op jit(solution)/shard_map/ppermute | solution.py:516
  62.0 3.4 %collective-permute-done.9.from_below = bf16[8,4,8,512]{3,2,1,0:T(8,128)(2,1)S(1)} collective-permute-done((bf16[8,4,8,512]{3,2,1,0:T(8,128)(2,1)S(1)}, bf16[8,4,8,512]{3,2,1,0:T(8,128)(2,1)S(1)}, u32[]{:S(2)}, u32[]{:S(2)}) %collective-permute-start.9) | collective-permute-done | bytes 262176 | tf_op jit(solution)/shard_map/ppermute | solution.py:516
  65.4 0.8 shard_map.89
  66.2 10.0 %all-to-all-start = ((bf16[32,8,512]{2,1,0:T(8,128)(2,1)}), bf16[32,8,512]{2,1,0:T(8,128)(2,1)S(1)}, u32[]{:S(2)}, u32[]{:S(2)}) async-start(bf16[32,8,512]{2,1,0:T(8,128)(2,1)} %bitcast.4), calls=%async_computation | async-start | bytes 524288 | tf_op jit(solution)/shard_map/all_to_all | solution.py:563
  76.3 1.6 %shard_map.88 = (bf16[256,1024]{1,0:T(8,128)(2,1)}, bf16[256,1024]{1,0:T(8,128)(2,1)}) custom-call(bf16[256,1024]{1,0:T(8,128)(2,1)S(1)} %bitcast.8, bf16[256,1024]{1,0:T(8,128)(2,1)S(1)} %bitcast.10, bf16[256,1024]{1,0:T(8,128)(2,1)S(1)} %get-tuple-element.73.outs, f32[128,1024]{1,0:T(8,128)S(1)} %get-tuple-element.84.own, ...), custom_call_target="tpu_custom_call" | custom-call | flops 4194304 | bytes 4194304 | tf_op jit(solution)/shard_map/pallas_call | solution.py:481
  77.9 10.0 %all-to-all-done.parts = bf16[32,8,512]{2,1,0:T(8,128)(2,1)S(1)} async-done(((bf16[32,8,512]{2,1,0:T(8,128)(2,1)}), bf16[32,8,512]{2,1,0:T(8,128)(2,1)S(1)}, u32[]{:S(2)}, u32[]{:S(2)}) %all-to-all-start) | async-done | bytes 262176 | tf_op jit(solution)/shard_map/all_to_all | solution.py:563
  87.8 0.7 shard_map.90
  (24 shorter events, 0.3 us)
Async XLA Ops:
  0.6 1.0 %copy-start.1 = (bf16[1,1,256,1024]{3,2,1,0:T(8,128)(2,1)S(1)}, bf16[1,1,256,1024]{3,2,1,0:T(8,128)(2,1)}, u32[]{:S(2)}) copy-start(bf16[1,1,256,1024]{3,2,1,0:T(8,128)(2,1)} %param.5) | copy-start | bytes 1572868
  1.7 5.7 %copy-start.3 = (bf16[1,1,256,1024]{3,2,1,0:T(8,128)(2,1)S(1)}, bf16[1,1,256,1024]{3,2,1,0:T(8,128)(2,1)}, u32[]{:S(2)}) copy-start(bf16[1,1,256,1024]{3,2,1,0:T(8,128)(2,1)} %param.9) | copy-start | bytes 1572868
  1.8 1.6 %collective-permute-start.1 = (bf16[128,1024]{1,0:T(8,128)(2,1)S(1)}, bf16[128,1024]{1,0:T(8,128)(2,1)S(1)}, u32[]{:S(2)}, u32[]{:S(2)}) collective-permute-start(bf16[128,1024]{1,0:T(8,128)(2,1)S(1)} %get-tuple-element.48), channel_id=1, source_target_pairs={{0,1},{1,0},{2,3},{3,2},{4,5},{5,4},{6,7},{7,6},{8,9},{9,8},{10,11... | collective-permute-start | bytes 786440 | tf_op jit(solution)/shard_map/ppermute | solution.py:47
  1.9 7.3 %collective-permute-start = (bf16[128,1024]{1,0:T(8,128)(2,1)S(1)}, bf16[128,1024]{1,0:T(8,128)(2,1)S(1)}, u32[]{:S(2)}, u32[]{:S(2)}) collective-permute-start(bf16[128,1024]{1,0:T(8,128)(2,1)S(1)} %get-tuple-element.48), channel_id=1, source_target_pairs={{1,4},{3,6},{5,8},{7,10},{9,12},{11,14},{13,16},{15,18},{17,20},{1... | collective-permute-start | bytes 786440 | tf_op jit(solution)/shard_map/ppermute | solution.py:47
  3.4 7.0 %slice-start = ((s8[8388608]{0:T(1024)(128)(4,1)}), s8[4194304]{0:T(1024)(128)(4,1)S(1)}, s32[]{:S(2)}) async-start(s8[8388608]{0:T(1024)(128)(4,1)} %bitcast.5), calls=%async_computation.1 | async-start | bytes 8388608
  3.7 12.1 %collective-permute-start.2 = (bf16[256,1024]{1,0:T(8,128)(2,1)S(1)}, bf16[256,1024]{1,0:T(8,128)(2,1)S(1)}, u32[]{:S(2)}, u32[]{:S(2)}) collective-permute-start(bf16[256,1024]{1,0:T(8,128)(2,1)S(1)} %shard_map.77.normed), channel_id=1, source_target_pairs={{0,2},{2,4},{4,6},{6,8},{8,10},{10,12},{12,14},{14,16},{16,18},{18... | collective-permute-start | bytes 1572872 | tf_op jit(solution)/shard_map/ppermute | solution.py:47
  7.4 2.9 %slice-start.1 = ((s8[8388608]{0:T(1024)(128)(4,1)}), s8[4194304]{0:T(1024)(128)(4,1)S(1)}, s32[]{:S(2)}) async-start(s8[8388608]{0:T(1024)(128)(4,1)} %bitcast.5), calls=%async_computation.2 | async-start | bytes 8388608
  7.4 2.9 %copy-start = (bf16[1024,1024]{1,0:T(8,128)(2,1)S(1)}, bf16[1024,1024]{1,0:T(8,128)(2,1)}, u32[]{:S(2)}) copy-start(bf16[1024,1024]{1,0:T(8,128)(2,1)} %weight_out.3) | copy-start | bytes 6291460
  7.5 2.8 %collective-permute-start.3 = (bf16[128,1024]{1,0:T(8,128)(2,1)S(1)}, bf16[128,1024]{1,0:T(8,128)(2,1)S(1)}, u32[]{:S(2)}, u32[]{:S(2)}) collective-permute-start(bf16[128,1024]{1,0:T(8,128)(2,1)S(1)} %get-tuple-element.53), channel_id=1, source_target_pairs={{0,1},{1,0},{2,3},{3,2},{4,5},{5,4},{6,7},{7,6},{8,9},{9,8},{10,11... | collective-permute-start | bytes 786440 | tf_op jit(solution)/shard_map/ppermute | solution.py:47
  15.8 2.7 %copy-start.4 = (s32[1,4]{1,0:T(1,128)S(1)}, s32[1,4]{1,0:T(1,128)}, u32[]{:S(2)}) copy-start(s32[1,4]{1,0:T(1,128)} %lengths.1) | copy-start | bytes 52
  29.7 5.1 %collective-permute-start.4 = (bf16[4,8,4,8,512]{4,3,2,1,0:T(8,128)(2,1)S(1)}, bf16[4,8,4,8,512]{4,3,2,1,0:T(8,128)(2,1)S(1)}, u32[]{:S(2)}, u32[]{:S(2)}) collective-permute-start(bf16[4,8,4,8,512]{4,3,2,1,0:T(8,128)(2,1)S(1)} %get-tuple-element.69), channel_id=1, source_target_pairs={{0,1},{1,0},{2,3},{3,2},{4,5},{5,4},{6,7},{7,6},{8,9},{9,8},{10,11... | collective-permute-start | bytes 3145736 | tf_op jit(solution)/shard_map/ppermute | solution.py:47
  32.5 19.8 %collective-permute-start.8 = (bf16[256,1024]{1,0:T(8,128)(2,1)S(1)}, bf16[256,1024]{1,0:T(8,128)(2,1)S(1)}, u32[]{:S(2)}, u32[]{:S(2)}) collective-permute-start(bf16[256,1024]{1,0:T(8,128)(2,1)S(1)} %get-tuple-element.66), channel_id=1, source_target_pairs={{2,0},{4,2},{6,4},{8,6},{10,8},{12,10},{14,12},{16,14},{18,16},{20... | collective-permute-start | bytes 1572872 | tf_op jit(solution)/shard_map/ppermute | solution.py:47
  35.4 16.9 %collective-permute-start.7 = (bf16[128,1024]{1,0:T(8,128)(2,1)S(1)}, bf16[128,1024]{1,0:T(8,128)(2,1)S(1)}, u32[]{:S(2)}, u32[]{:S(2)}) collective-permute-start(bf16[128,1024]{1,0:T(8,128)(2,1)S(1)} %get-tuple-element.77), channel_id=1, source_target_pairs={{4,1},{6,3},{8,5},{10,7},{12,9},{14,11},{16,13},{18,15},{20,17},{2... | collective-permute-start | bytes 786440 | tf_op jit(solution)/shard_map/ppermute | solution.py:47
  36.0 16.2 %collective-permute-start.5 = (bf16[4,4,8,512]{3,2,1,0:T(8,128)(2,1)S(1)}, bf16[4,4,8,512]{3,2,1,0:T(8,128)(2,1)S(1)}, u32[]{:S(2)}, u32[]{:S(2)}) collective-permute-start(bf16[4,4,8,512]{3,2,1,0:T(8,128)(2,1)S(1)} %get-tuple-element.74), channel_id=1, source_target_pairs={{0,8},{8,16},{16,24},{24,0},{1,9},{9,17},{17,25},{25,1},{2,10},{10... | collective-permute-start | bytes 393224 | tf_op jit(solution)/shard_map/ppermute | solution.py:516
  43.9 8.3 %collective-permute-start.6 = (bf16[4,4,8,512]{3,2,1,0:T(8,128)(2,1)S(1)}, bf16[4,4,8,512]{3,2,1,0:T(8,128)(2,1)S(1)}, u32[]{:S(2)}, u32[]{:S(2)}) collective-permute-start(bf16[4,4,8,512]{3,2,1,0:T(8,128)(2,1)S(1)} %get-tuple-element.75), channel_id=1, source_target_pairs={{0,24},{8,0},{16,8},{24,16},{1,25},{9,1},{17,9},{25,17},{2,26},{10... | collective-permute-start | bytes 393224 | tf_op jit(solution)/shard_map/ppermute | solution.py:516
  52.3 23.9 %copy-start.2 = (bf16[1,1,256,1024]{3,2,1,0:T(8,128)(2,1)S(1)}, bf16[1,1,256,1024]{3,2,1,0:T(8,128)(2,1)}, u32[]{:S(2)}) copy-start(bf16[1,1,256,1024]{3,2,1,0:T(8,128)(2,1)} %param.5) | copy-start | bytes 1572868
  52.4 13.0 %collective-permute-start.11 = (bf16[256,1024]{1,0:T(8,128)(2,1)S(1)}, bf16[256,1024]{1,0:T(8,128)(2,1)S(1)}, u32[]{:S(2)}, u32[]{:S(2)}) collective-permute-start(bf16[256,1024]{1,0:T(8,128)(2,1)S(1)} %get-tuple-element.86), channel_id=1, source_target_pairs={{0,1},{1,0},{2,3},{3,2},{4,5},{5,4},{6,7},{7,6},{8,9},{9,8},{10,11... | collective-permute-start | bytes 1572872 | tf_op jit(solution)/shard_map/ppermute | solution.py:47
  52.5 9.5 %collective-permute-start.10 = (bf16[8,4,8,512]{3,2,1,0:T(8,128)(2,1)S(1)}, bf16[8,4,8,512]{3,2,1,0:T(8,128)(2,1)S(1)}, u32[]{:S(2)}, u32[]{:S(2)}) collective-permute-start(bf16[8,4,8,512]{3,2,1,0:T(8,128)(2,1)S(1)} %get-tuple-element.85), channel_id=1, source_target_pairs={{0,24},{8,0},{16,8},{24,16},{1,25},{9,1},{17,9},{25,17},{2,26},{10... | collective-permute-start | bytes 786440 | tf_op jit(solution)/shard_map/ppermute | solution.py:516
  56.2 9.2 %collective-permute-start.9 = (bf16[8,4,8,512]{3,2,1,0:T(8,128)(2,1)S(1)}, bf16[8,4,8,512]{3,2,1,0:T(8,128)(2,1)S(1)}, u32[]{:S(2)}, u32[]{:S(2)}) collective-permute-start(bf16[8,4,8,512]{3,2,1,0:T(8,128)(2,1)S(1)} %get-tuple-element.82), channel_id=1, source_target_pairs={{0,8},{8,16},{16,24},{24,0},{1,9},{9,17},{17,25},{25,1},{2,10},{10... | collective-permute-start | bytes 786440 | tf_op jit(solution)/shard_map/ppermute | solution.py:516
  66.2 21.6 %all-to-all-start = ((bf16[32,8,512]{2,1,0:T(8,128)(2,1)}), bf16[32,8,512]{2,1,0:T(8,128)(2,1)S(1)}, u32[]{:S(2)}, u32[]{:S(2)}) async-start(bf16[32,8,512]{2,1,0:T(8,128)(2,1)} %bitcast.4), calls=%async_computation | async-start | bytes 524288 | tf_op jit(solution)/shard_map/all_to_all | solution.py:563

commit v4 on v3

--- a/solution.py
+++ b/solution.py
@@ -538,27 +538,29 @@
     gated, d_pre, near_d_pre = attention(lengths, proj, slope, near, near_slope, d_gated)
 
     tie = lax.optimization_barrier
-    far_d, near_d = near_through(near_d_pre, weight_in)
-    arrived = move(near_d, backward)
-    near_d_pre, near_d = tie((near_d_pre, near_d))
     send, keep = key_grad(near_normed, normed, near_d_pre, d_pre)
     received = move(send, swap)
+    near_d_pre, send = tie((near_d_pre, send))
+    far_d, near_d = near_through(near_d_pre, weight_in)
+    received, near_d = tie((received, near_d))
 
     block = keep.shape[1:]
     half = (block[0] // 2,) + block[1:]
     total, up, down = on_device(ring_first_kernel, [keep.shape, half, half], keep, received)
     from_below, from_above = around(up, 1), around(down, -1)
-    far_d, d_pre, total = tie((far_d, d_pre, total))
+    d_pre, total = tie((d_pre, total))
+    d_normed, outs = through(d_pre, gated, mine, second, weight_in, weight_out)
+    from_below, from_above, d_normed, near_d, far_d = tie((from_below, from_above, d_normed, near_d, far_d))
+    arrived = move(near_d, backward)
     far_in = move(far_d, far_back)
-    d_normed, outs = through(d_pre, gated, mine, second, weight_in, weight_out)
-    from_below, from_above, d_normed, far_in = tie((from_below, from_above, d_normed, far_in))
     up, down = on_device(ring_second_kernel, [block, block], total, from_below, from_above)
     from_below, from_above = around(up, 1), around(down, -1)
-    d_normed, up = tie((d_normed, up))
+    from_below, from_above, arrived, far_in = tie((from_below, from_above, arrived, far_in))
     own, given = merge(d_normed, arrived, outs)
     taken = move(given, swap)
-    from_below, from_above, taken = tie((from_below, from_above, taken))
+    from_below, own = tie((from_below, own))
     (column,) = on_device(ring_third_kernel, [block], total, from_below, from_above)
+    column, taken = tie((column, taken))
     column = column.reshape((block[0] * block[1],) + block[2:])
     parts = lax.all_to_all(column, ("dp", "x"), split_axis=0, concat_axis=0, tiled=True)
     layer_out, event_grads = finish(local, back, outs, own, taken, far_in)

time: 88.8 us -> 90.7 us (1.021); the launches traced: 88.5 us -> 89.4 us
  starting transfers between devices: 34.2 us -> 35.5 us
    all_to_all x1, starting transfers between devices: 10 us -> 13.9 us  [shards(): lax.all_to_all(column, ('dp', 'x'), split_axis=0, concat_axis=0, tiled=True)]
    ppermute x4, starting transfers between devices: 13 us -> 10.6 us  [around(): return lax.ppermute(block, 'y', [(i, (i + shift) % 4) for i in range(4)])]
    ppermute x4, waiting for transfers between devices: 13.1 us -> 11.2 us  [around(): return lax.ppermute(block, 'y', [(i, (i + shift) % 4) for i in range(4)])]
  transfers between devices with their start and end apart: 13 -> 13, of which waited for: 8 -> 8; matrix products, arithmetic and copies ran while one was open for 0% -> 0% of each run, Pallas kernels for 11% -> 14%
where the time goes in v4:
time: 90.7 us; the launch traced here: 89.4 us
  starting transfers between devices  35.5 us (39%)
  waiting for transfers between devices  26.4 us (29%)
  Pallas kernels  25.5 us (28%)
  local copies, waits for them, and re-layouts  1.07 us (1%)
    all_to_all x1, starting transfers between devices, shards(): lax.all_to_all(column, ('dp', 'x'), split_axis=0, concat_axis=0, tiled=True)  13.9 us
    ppermute x4, waiting for transfers between devices, around(): return lax.ppermute(block, 'y', [(i, (i + shift) % 4) for i in range(4)])  11.2 us
    ppermute x8, starting transfers between devices, move(): return lax.ppermute(block, SEQ, route)  11.1 us
    all_to_all x1, waiting for transfers between devices, shards(): lax.all_to_all(column, ('dp', 'x'), split_axis=0, concat_axis=0, tiled=True)  10.8 us
    ppermute x4, starting transfers between devices, around(): return lax.ppermute(block, 'y', [(i, (i + shift) % 4) for i in range(4)])  10.6 us
    pallas_call x1, Pallas kernels, attention(): pl.pallas_call(attention_kernel, in_specs=[pl.BlockSpec(memory_space=pltp...  7.37 us
    pallas_call x1, Pallas kernels, project(): pl.pallas_call(project_kernel, in_specs=[whole()] * 5, out_specs=[whole()...  4.57 us
    ppermute x8, waiting for transfers between devices, move(): return lax.ppermute(block, SEQ, route)  4.35 us
  transfers between devices with their start and end apart: 13, of which 8 were waited for; matrix products, arithmetic and copies ran while one was open for 0% of the time, Pallas kernels for 14%

profile of v4, /device:TPU:32, one launch (start us, length us, event | category | flops | bytes accessed | tf_op | source)
XLA Modules:
  0.0 89.4 jit_solution(4470802153705960396)
XLA Ops:
  0.6 1.0 %copy-done.1 = bf16[1,1,256,1024]{3,2,1,0:T(8,128)(2,1)S(1)} copy-done((bf16[1,1,256,1024]{3,2,1,0:T(8,128)(2,1)S(1)}, bf16[1,1,256,1024]{3,2,1,0:T(8,128)(2,1)}, u32[]{:S(2)}) %copy-start.1) | copy-done | bytes 524312
  1.9 0.8 collective-permute-start
  2.7 0.7 collective-permute-done.1.second
  3.4 0.3 shard_map.77.normed
  3.7 3.7 %collective-permute-start.2 = (bf16[256,1024]{1,0:T(8,128)(2,1)S(1)}, bf16[256,1024]{1,0:T(8,128)(2,1)S(1)}, u32[]{:S(2)}, u32[]{:S(2)}) collective-permute-start(bf16[256,1024]{1,0:T(8,128)(2,1)S(1)} %shard_map.77.normed), channel_id=1, source_target_pairs={{0,2},{2,4},{4,6},{6,8},{8,10},{10,12},{12,14},{14,16},{16,18},{18... | collective-permute-start | bytes 1572872 | tf_op jit(solution)/shard_map/ppermute | solution.py:47
  7.5 1.6 %collective-permute-start.3 = (bf16[128,1024]{1,0:T(8,128)(2,1)S(1)}, bf16[128,1024]{1,0:T(8,128)(2,1)S(1)}, u32[]{:S(2)}, u32[]{:S(2)}) collective-permute-start(bf16[128,1024]{1,0:T(8,128)(2,1)S(1)} %get-tuple-element.59), channel_id=1, source_target_pairs={{0,1},{1,0},{2,3},{3,2},{4,5},{5,4},{6,7},{7,6},{8,9},{9,8},{10,11... | collective-permute-start | bytes 786440 | tf_op jit(solution)/shard_map/ppermute | solution.py:47
  9.2 1.2 %collective-permute-done.3.back_second = bf16[128,1024]{1,0:T(8,128)(2,1)S(1)} collective-permute-done((bf16[128,1024]{1,0:T(8,128)(2,1)S(1)}, bf16[128,1024]{1,0:T(8,128)(2,1)S(1)}, u32[]{:S(2)}, u32[]{:S(2)}) %collective-permute-start.3) | collective-permute-done | bytes 262176 | tf_op jit(solution)/shard_map/ppermute | solution.py:47
  10.3 4.6 %shard_map.79 = (bf16[256,4096]{1,0:T(8,128)(2,1)S(1)}, bf16[256,4096]{1,0:T(8,128)(2,1)S(1)}, f32[256,1024]{1,0:T(8,128)S(1)}) custom-call(bf16[256,1024]{1,0:T(8,128)(2,1)S(1)} %shard_map.77.normed, bf16[128,1024]{1,0:T(8,128)(2,1)S(1)} %get-tuple-element.58.back_mine, bf16[128,1024]{1,0:T(8,128)(2,1)S(1)} %collective-permute-done.3.back_second, ...), custom_call_target="tpu_custom_call" | custom-call | flops 2684354560 | bytes 12582912 | tf_op jit(solution)/shard_map/pallas_call | solution.py:155
  14.9 0.9 %collective-permute-done.2.near = bf16[256,1024]{1,0:T(8,128)(2,1)S(1)} collective-permute-done((bf16[256,1024]{1,0:T(8,128)(2,1)S(1)}, bf16[256,1024]{1,0:T(8,128)(2,1)S(1)}, u32[]{:S(2)}, u32[]{:S(2)}) %collective-permute-start.2) | collective-permute-done | bytes 524320 | tf_op jit(solution)/shard_map/ppermute | solution.py:47
  15.8 2.7 %shard_map.80 = (bf16[384,1024]{1,0:T(8,128)(2,1)S(1)}, bf16[384,2048]{1,0:T(8,128)(2,1)S(1)}, bf16[384,2048]{1,0:T(8,128)(2,1)S(1)}) custom-call(bf16[128,1024]{1,0:T(8,128)(2,1)S(1)} %collective-permute-done.far, bf16[256,1024]{1,0:T(8,128)(2,1)S(1)} %collective-permute-done.2.near, bf16[1024,4096]{1,0:T(8,128)(2,1)S(1)} %bitcast.6), custom_call_target="tpu_custom_call" | custom-call | flops 1610612736 | bytes 8388608 | tf_op jit(solution)/shard_map/pallas_call | solution.py:180
  18.5 7.4 %shard_map.81 = (bf16[256,1024]{1,0:T(8,128)(2,1)S(1)}, bf16[256,4096]{1,0:T(8,128)(2,1)S(1)}, bf16[384,2048]{1,0:T(8,128)(2,1)S(1)}) custom-call(s32[1,4]{1,0:T(1,128)S(1)} %copy-done.4, bf16[256,4096]{1,0:T(8,128)(2,1)S(1)} %get-tuple-element.61.proj, bf16[256,4096]{1,0:T(8,128)(2,1)S(1)} %get-tuple-element.62.slope, ...), custom_call_target="tpu_custom_call" | custom-call | flops 1677721600 | bytes 16777216 | tf_op jit(solution)/shard_map/pallas_call | solution.py:289
  25.9 2.0 %shard_map.82 = (bf16[4,8,4,8,512]{4,3,2,1,0:T(8,128)(2,1)S(1)}, bf16[4,8,4,8,512]{4,3,2,1,0:T(8,128)(2,1)S(1)}) custom-call(bf16[384,1024]{1,0:T(8,128)(2,1)S(1)} %get-tuple-element.69.near_normed, bf16[256,1024]{1,0:T(8,128)(2,1)S(1)} %shard_map.77.normed, bf16[384,2048]{1,0:T(8,128)(2,1)S(1)} %get-tuple-element.73.near_d_pre, ...), custom_call_target="tpu_custom_call" | custom-call | flops 1024 | bytes 1024 | tf_op jit(solution)/shard_map/pallas_call | solution.py:334
  27.9 2.8 %collective-permute-start.4 = (bf16[4,8,4,8,512]{4,3,2,1,0:T(8,128)(2,1)S(1)}, bf16[4,8,4,8,512]{4,3,2,1,0:T(8,128)(2,1)S(1)}, u32[]{:S(2)}, u32[]{:S(2)}) collective-permute-start(bf16[4,8,4,8,512]{4,3,2,1,0:T(8,128)(2,1)S(1)} %get-tuple-element.72), channel_id=1, source_target_pairs={{0,1},{1,0},{2,3},{3,2},{4,5},{5,4},{6,7},{7,6},{8,9},{9,8},{10,11... | collective-permute-start | bytes 3145736 | tf_op jit(solution)/shard_map/ppermute | solution.py:47
  30.7 1.8 %shard_map.83 = (bf16[128,1024]{1,0:T(8,128)(2,1)S(1)}, bf16[256,1024]{1,0:T(8,128)(2,1)S(1)}) custom-call(bf16[384,2048]{1,0:T(8,128)(2,1)S(1)} %get-tuple-element.73.near_d_pre, bf16[1024,4096]{1,0:T(8,128)(2,1)S(1)} %bitcast.6), custom_call_target="tpu_custom_call" | custom-call | flops 1024 | bytes 1024 | tf_op jit(solution)/shard_map/pallas_call | solution.py:394
  32.5 0.5 collective-permute-done.4.received
  33.0 0.6 shard_map.84
  33.5 4.0 %collective-permute-start.5 = (bf16[4,4,8,512]{3,2,1,0:T(8,128)(2,1)S(1)}, bf16[4,4,8,512]{3,2,1,0:T(8,128)(2,1)S(1)}, u32[]{:S(2)}, u32[]{:S(2)}) collective-permute-start(bf16[4,4,8,512]{3,2,1,0:T(8,128)(2,1)S(1)} %get-tuple-element.81), channel_id=1, source_target_pairs={{0,8},{8,16},{16,24},{24,0},{1,9},{9,17},{17,25},{25,1},{2,10},{10... | collective-permute-start | bytes 393224 | tf_op jit(solution)/shard_map/ppermute | solution.py:516
  37.6 1.8 %collective-permute-start.6 = (bf16[4,4,8,512]{3,2,1,0:T(8,128)(2,1)S(1)}, bf16[4,4,8,512]{3,2,1,0:T(8,128)(2,1)S(1)}, u32[]{:S(2)}, u32[]{:S(2)}) collective-permute-start(bf16[4,4,8,512]{3,2,1,0:T(8,128)(2,1)S(1)} %get-tuple-element.82), channel_id=1, source_target_pairs={{0,24},{8,0},{16,8},{24,16},{1,25},{9,1},{17,9},{25,17},{2,26},{10... | collective-permute-start | bytes 393224 | tf_op jit(solution)/shard_map/ppermute | solution.py:516
  39.4 2.9 %shard_map.85 = (f32[256,1024]{1,0:T(8,128)S(1)}, bf16[256,1024]{1,0:T(8,128)(2,1)S(1)}) custom-call(bf16[256,4096]{1,0:T(8,128)(2,1)S(1)} %get-tuple-element.77.d_pre, bf16[256,1024]{1,0:T(8,128)(2,1)S(1)} %get-tuple-element.78.gated, bf16[128,1024]{1,0:T(8,128)(2,1)S(1)} %get-tuple-element.55.mine, bf16[128,1024]{1,0:T(8,128)(2,1)S(1)} %collective-permute-done.1.second, ...), custom_call_target="tpu_custom_call" | custom-call | flops 1024 | bytes 1024 | tf_op jit(solution)/shard_map/pallas_call | solution.py:419
  42.3 0.8 collective-permute-done.5.from_below
  43.1 1.3 %collective-permute-start.9 = (bf16[256,1024]{1,0:T(8,128)(2,1)S(1)}, bf16[256,1024]{1,0:T(8,128)(2,1)S(1)}, u32[]{:S(2)}, u32[]{:S(2)}) collective-permute-start(bf16[256,1024]{1,0:T(8,128)(2,1)S(1)} %get-tuple-element.90), channel_id=1, source_target_pairs={{2,0},{4,2},{6,4},{8,6},{10,8},{12,10},{14,12},{16,14},{18,16},{20... | collective-permute-start | bytes 1572872 | tf_op jit(solution)/shard_map/ppermute | solution.py:47
  44.5 4.4 %collective-permute-start.7 = (bf16[8,4,8,512]{3,2,1,0:T(8,128)(2,1)S(1)}, bf16[8,4,8,512]{3,2,1,0:T(8,128)(2,1)S(1)}, u32[]{:S(2)}, u32[]{:S(2)}) collective-permute-start(bf16[8,4,8,512]{3,2,1,0:T(8,128)(2,1)S(1)} %get-tuple-element.88), channel_id=1, source_target_pairs={{0,8},{8,16},{16,24},{24,0},{1,9},{9,17},{17,25},{25,1},{2,10},{10... | collective-permute-start | bytes 786440 | tf_op jit(solution)/shard_map/ppermute | solution.py:516
  48.9 0.3 collective-permute-start.8
  49.2 0.7 collective-permute-start.10
  49.9 10.4 %collective-permute-done.7.from_below = bf16[8,4,8,512]{3,2,1,0:T(8,128)(2,1)S(1)} collective-permute-done((bf16[8,4,8,512]{3,2,1,0:T(8,128)(2,1)S(1)}, bf16[8,4,8,512]{3,2,1,0:T(8,128)(2,1)S(1)}, u32[]{:S(2)}, u32[]{:S(2)}) %collective-permute-start.7) | collective-permute-done | bytes 262176 | tf_op jit(solution)/shard_map/ppermute | solution.py:516
  60.3 0.1 shard_map.87
  60.5 0.8 shard_map.88
  61.3 1.1 %collective-permute-done.11.taken = bf16[256,1024]{1,0:T(8,128)(2,1)S(1)} collective-permute-done((bf16[256,1024]{1,0:T(8,128)(2,1)S(1)}, bf16[256,1024]{1,0:T(8,128)(2,1)S(1)}, u32[]{:S(2)}, u32[]{:S(2)}) %collective-permute-start.11) | collective-permute-done | bytes 524320 | tf_op jit(solution)/shard_map/ppermute | solution.py:47
  62.4 13.9 %all-to-all-start = ((bf16[32,8,512]{2,1,0:T(8,128)(2,1)}), bf16[32,8,512]{2,1,0:T(8,128)(2,1)S(1)}, u32[]{:S(2)}, u32[]{:S(2)}) async-start(bf16[32,8,512]{2,1,0:T(8,128)(2,1)} %bitcast.4), calls=%async_computation | async-start | bytes 524288 | tf_op jit(solution)/shard_map/all_to_all | solution.py:565
  76.3 1.6 %shard_map.89 = (bf16[256,1024]{1,0:T(8,128)(2,1)}, bf16[256,1024]{1,0:T(8,128)(2,1)}) custom-call(bf16[256,1024]{1,0:T(8,128)(2,1)S(1)} %bitcast.8, bf16[256,1024]{1,0:T(8,128)(2,1)S(1)} %bitcast.10, bf16[256,1024]{1,0:T(8,128)(2,1)S(1)} %get-tuple-element.79.outs, f32[128,1024]{1,0:T(8,128)S(1)} %get-tuple-element.96.own, ...), custom_call_target="tpu_custom_call" | custom-call | flops 4194304 | bytes 4194304 | tf_op jit(solution)/shard_map/pallas_call | solution.py:481
  77.9 10.8 %all-to-all-done.parts = bf16[32,8,512]{2,1,0:T(8,128)(2,1)S(1)} async-done(((bf16[32,8,512]{2,1,0:T(8,128)(2,1)}), bf16[32,8,512]{2,1,0:T(8,128)(2,1)S(1)}, u32[]{:S(2)}, u32[]{:S(2)}) %all-to-all-start) | async-done | bytes 262176 | tf_op jit(solution)/shard_map/all_to_all | solution.py:565
  88.7 0.7 shard_map.90
  (24 shorter events, 0.4 us)
Async XLA Ops:
  0.6 1.0 %copy-start.1 = (bf16[1,1,256,1024]{3,2,1,0:T(8,128)(2,1)S(1)}, bf16[1,1,256,1024]{3,2,1,0:T(8,128)(2,1)}, u32[]{:S(2)}) copy-start(bf16[1,1,256,1024]{3,2,1,0:T(8,128)(2,1)} %param.5) | copy-start | bytes 1572868
  1.7 5.7 %copy-start.3 = (bf16[1,1,256,1024]{3,2,1,0:T(8,128)(2,1)S(1)}, bf16[1,1,256,1024]{3,2,1,0:T(8,128)(2,1)}, u32[]{:S(2)}) copy-start(bf16[1,1,256,1024]{3,2,1,0:T(8,128)(2,1)} %param.9) | copy-start | bytes 1572868
  1.8 1.6 %collective-permute-start.1 = (bf16[128,1024]{1,0:T(8,128)(2,1)S(1)}, bf16[128,1024]{1,0:T(8,128)(2,1)S(1)}, u32[]{:S(2)}, u32[]{:S(2)}) collective-permute-start(bf16[128,1024]{1,0:T(8,128)(2,1)S(1)} %get-tuple-element.54), channel_id=1, source_target_pairs={{0,1},{1,0},{2,3},{3,2},{4,5},{5,4},{6,7},{7,6},{8,9},{9,8},{10,11... | collective-permute-start | bytes 786440 | tf_op jit(solution)/shard_map/ppermute | solution.py:47
  1.9 7.3 %collective-permute-start = (bf16[128,1024]{1,0:T(8,128)(2,1)S(1)}, bf16[128,1024]{1,0:T(8,128)(2,1)S(1)}, u32[]{:S(2)}, u32[]{:S(2)}) collective-permute-start(bf16[128,1024]{1,0:T(8,128)(2,1)S(1)} %get-tuple-element.54), channel_id=1, source_target_pairs={{1,4},{3,6},{5,8},{7,10},{9,12},{11,14},{13,16},{15,18},{17,20},{1... | collective-permute-start | bytes 786440 | tf_op jit(solution)/shard_map/ppermute | solution.py:47
  3.4 7.0 %slice-start = ((s8[8388608]{0:T(1024)(128)(4,1)}), s8[4194304]{0:T(1024)(128)(4,1)S(1)}, s32[]{:S(2)}) async-start(s8[8388608]{0:T(1024)(128)(4,1)} %bitcast.5), calls=%async_computation.1 | async-start | bytes 8388608
  3.7 12.1 %collective-permute-start.2 = (bf16[256,1024]{1,0:T(8,128)(2,1)S(1)}, bf16[256,1024]{1,0:T(8,128)(2,1)S(1)}, u32[]{:S(2)}, u32[]{:S(2)}) collective-permute-start(bf16[256,1024]{1,0:T(8,128)(2,1)S(1)} %shard_map.77.normed), channel_id=1, source_target_pairs={{0,2},{2,4},{4,6},{6,8},{8,10},{10,12},{12,14},{14,16},{16,18},{18... | collective-permute-start | bytes 1572872 | tf_op jit(solution)/shard_map/ppermute | solution.py:47
  7.4 2.9 %slice-start.1 = ((s8[8388608]{0:T(1024)(128)(4,1)}), s8[4194304]{0:T(1024)(128)(4,1)S(1)}, s32[]{:S(2)}) async-start(s8[8388608]{0:T(1024)(128)(4,1)} %bitcast.5), calls=%async_computation.2 | async-start | bytes 8388608
  7.4 2.9 %copy-start = (bf16[1024,1024]{1,0:T(8,128)(2,1)S(1)}, bf16[1024,1024]{1,0:T(8,128)(2,1)}, u32[]{:S(2)}) copy-start(bf16[1024,1024]{1,0:T(8,128)(2,1)} %weight_out.3) | copy-start | bytes 6291460
  7.5 2.8 %collective-permute-start.3 = (bf16[128,1024]{1,0:T(8,128)(2,1)S(1)}, bf16[128,1024]{1,0:T(8,128)(2,1)S(1)}, u32[]{:S(2)}, u32[]{:S(2)}) collective-permute-start(bf16[128,1024]{1,0:T(8,128)(2,1)S(1)} %get-tuple-element.59), channel_id=1, source_target_pairs={{0,1},{1,0},{2,3},{3,2},{4,5},{5,4},{6,7},{7,6},{8,9},{9,8},{10,11... | collective-permute-start | bytes 786440 | tf_op jit(solution)/shard_map/ppermute | solution.py:47
  15.8 2.7 %copy-start.4 = (s32[1,4]{1,0:T(1,128)S(1)}, s32[1,4]{1,0:T(1,128)}, u32[]{:S(2)}) copy-start(s32[1,4]{1,0:T(1,128)} %lengths.1) | copy-start | bytes 52
  27.9 5.1 %collective-permute-start.4 = (bf16[4,8,4,8,512]{4,3,2,1,0:T(8,128)(2,1)S(1)}, bf16[4,8,4,8,512]{4,3,2,1,0:T(8,128)(2,1)S(1)}, u32[]{:S(2)}, u32[]{:S(2)}) collective-permute-start(bf16[4,8,4,8,512]{4,3,2,1,0:T(8,128)(2,1)S(1)} %get-tuple-element.72), channel_id=1, source_target_pairs={{0,1},{1,0},{2,3},{3,2},{4,5},{5,4},{6,7},{7,6},{8,9},{9,8},{10,11... | collective-permute-start | bytes 3145736 | tf_op jit(solution)/shard_map/ppermute | solution.py:47
  33.5 9.6 %collective-permute-start.5 = (bf16[4,4,8,512]{3,2,1,0:T(8,128)(2,1)S(1)}, bf16[4,4,8,512]{3,2,1,0:T(8,128)(2,1)S(1)}, u32[]{:S(2)}, u32[]{:S(2)}) collective-permute-start(bf16[4,4,8,512]{3,2,1,0:T(8,128)(2,1)S(1)} %get-tuple-element.81), channel_id=1, source_target_pairs={{0,8},{8,16},{16,24},{24,0},{1,9},{9,17},{17,25},{25,1},{2,10},{10... | collective-permute-start | bytes 393224 | tf_op jit(solution)/shard_map/ppermute | solution.py:516
  37.6 5.5 %collective-permute-start.6 = (bf16[4,4,8,512]{3,2,1,0:T(8,128)(2,1)S(1)}, bf16[4,4,8,512]{3,2,1,0:T(8,128)(2,1)S(1)}, u32[]{:S(2)}, u32[]{:S(2)}) collective-permute-start(bf16[4,4,8,512]{3,2,1,0:T(8,128)(2,1)S(1)} %get-tuple-element.82), channel_id=1, source_target_pairs={{0,24},{8,0},{16,8},{24,16},{1,25},{9,1},{17,9},{25,17},{2,26},{10... | collective-permute-start | bytes 393224 | tf_op jit(solution)/shard_map/ppermute | solution.py:516
  43.1 17.1 %collective-permute-start.9 = (bf16[256,1024]{1,0:T(8,128)(2,1)S(1)}, bf16[256,1024]{1,0:T(8,128)(2,1)S(1)}, u32[]{:S(2)}, u32[]{:S(2)}) collective-permute-start(bf16[256,1024]{1,0:T(8,128)(2,1)S(1)} %get-tuple-element.90), channel_id=1, source_target_pairs={{2,0},{4,2},{6,4},{8,6},{10,8},{12,10},{14,12},{16,14},{18,16},{20... | collective-permute-start | bytes 1572872 | tf_op jit(solution)/shard_map/ppermute | solution.py:47
  44.5 15.7 %collective-permute-start.7 = (bf16[8,4,8,512]{3,2,1,0:T(8,128)(2,1)S(1)}, bf16[8,4,8,512]{3,2,1,0:T(8,128)(2,1)S(1)}, u32[]{:S(2)}, u32[]{:S(2)}) collective-permute-start(bf16[8,4,8,512]{3,2,1,0:T(8,128)(2,1)S(1)} %get-tuple-element.88), channel_id=1, source_target_pairs={{0,8},{8,16},{16,24},{24,0},{1,9},{9,17},{17,25},{25,1},{2,10},{10... | collective-permute-start | bytes 786440 | tf_op jit(solution)/shard_map/ppermute | solution.py:516
  48.9 11.4 %collective-permute-start.8 = (bf16[8,4,8,512]{3,2,1,0:T(8,128)(2,1)S(1)}, bf16[8,4,8,512]{3,2,1,0:T(8,128)(2,1)S(1)}, u32[]{:S(2)}, u32[]{:S(2)}) collective-permute-start(bf16[8,4,8,512]{3,2,1,0:T(8,128)(2,1)S(1)} %get-tuple-element.89), channel_id=1, source_target_pairs={{0,24},{8,0},{16,8},{24,16},{1,25},{9,1},{17,9},{25,17},{2,26},{10... | collective-permute-start | bytes 786440 | tf_op jit(solution)/shard_map/ppermute | solution.py:516
  49.2 11.1 %collective-permute-start.10 = (bf16[128,1024]{1,0:T(8,128)(2,1)S(1)}, bf16[128,1024]{1,0:T(8,128)(2,1)S(1)}, u32[]{:S(2)}, u32[]{:S(2)}) collective-permute-start(bf16[128,1024]{1,0:T(8,128)(2,1)S(1)} %get-tuple-element.91), channel_id=1, source_target_pairs={{4,1},{6,3},{8,5},{10,7},{12,9},{14,11},{16,13},{18,15},{20,17},{2... | collective-permute-start | bytes 786440 | tf_op jit(solution)/shard_map/ppermute | solution.py:47
  60.2 16.0 %copy-start.2 = (bf16[1,1,256,1024]{3,2,1,0:T(8,128)(2,1)S(1)}, bf16[1,1,256,1024]{3,2,1,0:T(8,128)(2,1)}, u32[]{:S(2)}) copy-start(bf16[1,1,256,1024]{3,2,1,0:T(8,128)(2,1)} %param.5) | copy-start | bytes 1572868
  60.4 2.0 %collective-permute-start.11 = (bf16[256,1024]{1,0:T(8,128)(2,1)S(1)}, bf16[256,1024]{1,0:T(8,128)(2,1)S(1)}, u32[]{:S(2)}, u32[]{:S(2)}) collective-permute-start(bf16[256,1024]{1,0:T(8,128)(2,1)S(1)} %get-tuple-element.99), channel_id=1, source_target_pairs={{0,1},{1,0},{2,3},{3,2},{4,5},{5,4},{6,7},{7,6},{8,9},{9,8},{10,11... | collective-permute-start | bytes 1572872 | tf_op jit(solution)/shard_map/ppermute | solution.py:47
  62.4 26.4 %all-to-all-start = ((bf16[32,8,512]{2,1,0:T(8,128)(2,1)}), bf16[32,8,512]{2,1,0:T(8,128)(2,1)S(1)}, u32[]{:S(2)}, u32[]{:S(2)}) async-start(bf16[32,8,512]{2,1,0:T(8,128)(2,1)} %bitcast.4), calls=%async_computation | async-start | bytes 524288 | tf_op jit(solution)/shard_map/all_to_all | solution.py:565

commit v5 on v3

--- a/solution.py
+++ b/solution.py
@@ -548,13 +548,13 @@
     half = (block[0] // 2,) + block[1:]
     total, up, down = on_device(ring_first_kernel, [keep.shape, half, half], keep, received)
     from_below, from_above = around(up, 1), around(down, -1)
-    far_d, d_pre, total = tie((far_d, d_pre, total))
+    d_pre, total = tie((d_pre, total))
     far_in = move(far_d, far_back)
     d_normed, outs = through(d_pre, gated, mine, second, weight_in, weight_out)
-    from_below, from_above, d_normed, far_in = tie((from_below, from_above, d_normed, far_in))
+    from_below, from_above, d_normed = tie((from_below, from_above, d_normed))
     up, down = on_device(ring_second_kernel, [block, block], total, from_below, from_above)
     from_below, from_above = around(up, 1), around(down, -1)
-    d_normed, up = tie((d_normed, up))
+    d_normed, up, far_in = tie((d_normed, up, far_in))
     own, given = merge(d_normed, arrived, outs)
     taken = move(given, swap)
     from_below, from_above, taken = tie((from_below, from_above, taken))

time: 88.8 us -> 89.1 us (level)
    ppermute x4, starting transfers between devices: 13 us -> 14 us  [around(): return lax.ppermute(block, 'y', [(i, (i + shift) % 4) for i in range(4)])]
where the time goes in v5:
time: 89.1 us; the launch traced here: 88.8 us
  starting transfers between devices  34.5 us (39%)
  waiting for transfers between devices  26.8 us (30%)
  Pallas kernels  25.5 us (29%)
  local copies, waits for them, and re-layouts  1.07 us (1%)
    ppermute x4, starting transfers between devices, around(): return lax.ppermute(block, 'y', [(i, (i + shift) % 4) for i in range(4)])  14 us
    ppermute x4, waiting for transfers between devices, around(): return lax.ppermute(block, 'y', [(i, (i + shift) % 4) for i in range(4)])  13.7 us
    ppermute x8, starting transfers between devices, move(): return lax.ppermute(block, SEQ, route)  11.1 us
    all_to_all x1, waiting for transfers between devices, shards(): lax.all_to_all(column, ('dp', 'x'), split_axis=0, concat_axis=0, tiled=True)  9.97 us
    all_to_all x1, starting transfers between devices, shards(): lax.all_to_all(column, ('dp', 'x'), split_axis=0, concat_axis=0, tiled=True)  9.43 us
    pallas_call x1, Pallas kernels, attention(): pl.pallas_call(attention_kernel, in_specs=[pl.BlockSpec(memory_space=pltp...  7.37 us
    pallas_call x1, Pallas kernels, project(): pl.pallas_call(project_kernel, in_specs=[whole()] * 5, out_specs=[whole()...  4.57 us
    ppermute x8, waiting for transfers between devices, move(): return lax.ppermute(block, SEQ, route)  3.11 us
  transfers between devices with their start and end apart: 13, of which 8 were waited for; matrix products, arithmetic and copies ran while one was open for 0% of the time, Pallas kernels for 11%

profile of v5, /device:TPU:32, one launch (start us, length us, event | category | flops | bytes accessed | tf_op | source)
XLA Modules:
  0.0 88.8 jit_solution(9228575533988291091)
XLA Ops:
  0.6 1.0 %copy-done.1 = bf16[1,1,256,1024]{3,2,1,0:T(8,128)(2,1)S(1)} copy-done((bf16[1,1,256,1024]{3,2,1,0:T(8,128)(2,1)S(1)}, bf16[1,1,256,1024]{3,2,1,0:T(8,128)(2,1)}, u32[]{:S(2)}) %copy-start.1) | copy-done | bytes 524312
  1.9 0.8 collective-permute-start
  2.7 0.7 collective-permute-done.1.second
  3.4 0.3 shard_map.77.normed
  3.7 3.7 %collective-permute-start.2 = (bf16[256,1024]{1,0:T(8,128)(2,1)S(1)}, bf16[256,1024]{1,0:T(8,128)(2,1)S(1)}, u32[]{:S(2)}, u32[]{:S(2)}) collective-permute-start(bf16[256,1024]{1,0:T(8,128)(2,1)S(1)} %shard_map.77.normed), channel_id=1, source_target_pairs={{0,2},{2,4},{4,6},{6,8},{8,10},{10,12},{12,14},{14,16},{16,18},{18... | collective-permute-start | bytes 1572872 | tf_op jit(solution)/shard_map/ppermute | solution.py:47
  7.5 1.6 %collective-permute-start.3 = (bf16[128,1024]{1,0:T(8,128)(2,1)S(1)}, bf16[128,1024]{1,0:T(8,128)(2,1)S(1)}, u32[]{:S(2)}, u32[]{:S(2)}) collective-permute-start(bf16[128,1024]{1,0:T(8,128)(2,1)S(1)} %get-tuple-element.52), channel_id=1, source_target_pairs={{0,1},{1,0},{2,3},{3,2},{4,5},{5,4},{6,7},{7,6},{8,9},{9,8},{10,11... | collective-permute-start | bytes 786440 | tf_op jit(solution)/shard_map/ppermute | solution.py:47
  9.2 1.2 %collective-permute-done.3.back_second = bf16[128,1024]{1,0:T(8,128)(2,1)S(1)} collective-permute-done((bf16[128,1024]{1,0:T(8,128)(2,1)S(1)}, bf16[128,1024]{1,0:T(8,128)(2,1)S(1)}, u32[]{:S(2)}, u32[]{:S(2)}) %collective-permute-start.3) | collective-permute-done | bytes 262176 | tf_op jit(solution)/shard_map/ppermute | solution.py:47
  10.3 4.6 %shard_map.79 = (bf16[256,4096]{1,0:T(8,128)(2,1)S(1)}, bf16[256,4096]{1,0:T(8,128)(2,1)S(1)}, f32[256,1024]{1,0:T(8,128)S(1)}) custom-call(bf16[256,1024]{1,0:T(8,128)(2,1)S(1)} %shard_map.77.normed, bf16[128,1024]{1,0:T(8,128)(2,1)S(1)} %get-tuple-element.51.back_mine, bf16[128,1024]{1,0:T(8,128)(2,1)S(1)} %collective-permute-done.3.back_second, ...), custom_call_target="tpu_custom_call" | custom-call | flops 2684354560 | bytes 12582912 | tf_op jit(solution)/shard_map/pallas_call | solution.py:155
  14.9 0.9 %collective-permute-done.2.near = bf16[256,1024]{1,0:T(8,128)(2,1)S(1)} collective-permute-done((bf16[256,1024]{1,0:T(8,128)(2,1)S(1)}, bf16[256,1024]{1,0:T(8,128)(2,1)S(1)}, u32[]{:S(2)}, u32[]{:S(2)}) %collective-permute-start.2) | collective-permute-done | bytes 524320 | tf_op jit(solution)/shard_map/ppermute | solution.py:47
  15.8 2.7 %shard_map.80 = (bf16[384,1024]{1,0:T(8,128)(2,1)S(1)}, bf16[384,2048]{1,0:T(8,128)(2,1)S(1)}, bf16[384,2048]{1,0:T(8,128)(2,1)S(1)}) custom-call(bf16[128,1024]{1,0:T(8,128)(2,1)S(1)} %collective-permute-done.far, bf16[256,1024]{1,0:T(8,128)(2,1)S(1)} %collective-permute-done.2.near, bf16[1024,4096]{1,0:T(8,128)(2,1)S(1)} %bitcast.6), custom_call_target="tpu_custom_call" | custom-call | flops 1610612736 | bytes 8388608 | tf_op jit(solution)/shard_map/pallas_call | solution.py:180
  18.5 7.4 %shard_map.81 = (bf16[256,1024]{1,0:T(8,128)(2,1)S(1)}, bf16[256,4096]{1,0:T(8,128)(2,1)S(1)}, bf16[384,2048]{1,0:T(8,128)(2,1)S(1)}) custom-call(s32[1,4]{1,0:T(1,128)S(1)} %copy-done.4, bf16[256,4096]{1,0:T(8,128)(2,1)S(1)} %get-tuple-element.54.proj, bf16[256,4096]{1,0:T(8,128)(2,1)S(1)} %get-tuple-element.55.slope, ...), custom_call_target="tpu_custom_call" | custom-call | flops 1677721600 | bytes 16777216 | tf_op jit(solution)/shard_map/pallas_call | solution.py:289
  25.9 1.8 %shard_map.82 = (bf16[128,1024]{1,0:T(8,128)(2,1)S(1)}, bf16[256,1024]{1,0:T(8,128)(2,1)S(1)}) custom-call(bf16[384,2048]{1,0:T(8,128)(2,1)S(1)} %get-tuple-element.65.near_d_pre, bf16[1024,4096]{1,0:T(8,128)(2,1)S(1)} %bitcast.6), custom_call_target="tpu_custom_call" | custom-call | flops 1024 | bytes 1024 | tf_op jit(solution)/shard_map/pallas_call | solution.py:394
  27.7 2.0 %shard_map.83 = (bf16[4,8,4,8,512]{4,3,2,1,0:T(8,128)(2,1)S(1)}, bf16[4,8,4,8,512]{4,3,2,1,0:T(8,128)(2,1)S(1)}) custom-call(bf16[384,1024]{1,0:T(8,128)(2,1)S(1)} %get-tuple-element.62.near_normed, bf16[256,1024]{1,0:T(8,128)(2,1)S(1)} %shard_map.77.normed, bf16[384,2048]{1,0:T(8,128)(2,1)S(1)} %get-tuple-element.65.near_d_pre, ...), custom_call_target="tpu_custom_call" | custom-call | flops 1024 | bytes 1024 | tf_op jit(solution)/shard_map/pallas_call | solution.py:334
  29.7 2.8 %collective-permute-start.4 = (bf16[4,8,4,8,512]{4,3,2,1,0:T(8,128)(2,1)S(1)}, bf16[4,8,4,8,512]{4,3,2,1,0:T(8,128)(2,1)S(1)}, u32[]{:S(2)}, u32[]{:S(2)}) collective-permute-start(bf16[4,8,4,8,512]{4,3,2,1,0:T(8,128)(2,1)S(1)} %get-tuple-element.67), channel_id=1, source_target_pairs={{0,1},{1,0},{2,3},{3,2},{4,5},{5,4},{6,7},{7,6},{8,9},{9,8},{10,11... | collective-permute-start | bytes 3145736 | tf_op jit(solution)/shard_map/ppermute | solution.py:47
  32.5 1.3 %collective-permute-start.8 = (bf16[256,1024]{1,0:T(8,128)(2,1)S(1)}, bf16[256,1024]{1,0:T(8,128)(2,1)S(1)}, u32[]{:S(2)}, u32[]{:S(2)}) collective-permute-start(bf16[256,1024]{1,0:T(8,128)(2,1)S(1)} %get-tuple-element.64), channel_id=1, source_target_pairs={{2,0},{4,2},{6,4},{8,6},{10,8},{12,10},{14,12},{16,14},{18,16},{20... | collective-permute-start | bytes 1572872 | tf_op jit(solution)/shard_map/ppermute | solution.py:47
  33.8 0.7 collective-permute-start.7
  34.5 0.3 collective-permute-done.4.received
  34.8 0.6 shard_map.84
  35.4 8.5 %collective-permute-start.5 = (bf16[4,4,8,512]{3,2,1,0:T(8,128)(2,1)S(1)}, bf16[4,4,8,512]{3,2,1,0:T(8,128)(2,1)S(1)}, u32[]{:S(2)}, u32[]{:S(2)}) collective-permute-start(bf16[4,4,8,512]{3,2,1,0:T(8,128)(2,1)S(1)} %get-tuple-element.72), channel_id=1, source_target_pairs={{0,8},{8,16},{16,24},{24,0},{1,9},{9,17},{17,25},{25,1},{2,10},{10... | collective-permute-start | bytes 393224 | tf_op jit(solution)/shard_map/ppermute | solution.py:516
  43.9 1.5 %collective-permute-start.6 = (bf16[4,4,8,512]{3,2,1,0:T(8,128)(2,1)S(1)}, bf16[4,4,8,512]{3,2,1,0:T(8,128)(2,1)S(1)}, u32[]{:S(2)}, u32[]{:S(2)}) collective-permute-start(bf16[4,4,8,512]{3,2,1,0:T(8,128)(2,1)S(1)} %get-tuple-element.73), channel_id=1, source_target_pairs={{0,24},{8,0},{16,8},{24,16},{1,25},{9,1},{17,9},{25,17},{2,26},{10... | collective-permute-start | bytes 393224 | tf_op jit(solution)/shard_map/ppermute | solution.py:516
  45.4 2.9 %shard_map.85 = (f32[256,1024]{1,0:T(8,128)S(1)}, bf16[256,1024]{1,0:T(8,128)(2,1)S(1)}) custom-call(bf16[256,4096]{1,0:T(8,128)(2,1)S(1)} %get-tuple-element.69.d_pre, bf16[256,1024]{1,0:T(8,128)(2,1)S(1)} %get-tuple-element.70.gated, bf16[128,1024]{1,0:T(8,128)(2,1)S(1)} %get-tuple-element.48.mine, bf16[128,1024]{1,0:T(8,128)(2,1)S(1)} %collective-permute-done.1.second, ...), custom_call_target="tpu_custom_call" | custom-call | flops 1024 | bytes 1024 | tf_op jit(solution)/shard_map/pallas_call | solution.py:419
  48.3 4.2 %collective-permute-done.5.from_below = bf16[4,4,8,512]{3,2,1,0:T(8,128)(2,1)S(1)} collective-permute-done((bf16[4,4,8,512]{3,2,1,0:T(8,128)(2,1)S(1)}, bf16[4,4,8,512]{3,2,1,0:T(8,128)(2,1)S(1)}, u32[]{:S(2)}, u32[]{:S(2)}) %collective-permute-start.5) | collective-permute-done | bytes 131104 | tf_op jit(solution)/shard_map/ppermute | solution.py:516
  52.6 0.1 shard_map.87
  52.7 0.1 collective-permute-start.11
  52.8 3.9 %collective-permute-start.10 = (bf16[8,4,8,512]{3,2,1,0:T(8,128)(2,1)S(1)}, bf16[8,4,8,512]{3,2,1,0:T(8,128)(2,1)S(1)}, u32[]{:S(2)}, u32[]{:S(2)}) collective-permute-start(bf16[8,4,8,512]{3,2,1,0:T(8,128)(2,1)S(1)} %get-tuple-element.83), channel_id=1, source_target_pairs={{0,24},{8,0},{16,8},{24,16},{1,25},{9,1},{17,9},{25,17},{2,26},{10... | collective-permute-start | bytes 786440 | tf_op jit(solution)/shard_map/ppermute | solution.py:516
  56.7 6.2 %collective-permute-done.10.from_above = bf16[8,4,8,512]{3,2,1,0:T(8,128)(2,1)S(1)} collective-permute-done((bf16[8,4,8,512]{3,2,1,0:T(8,128)(2,1)S(1)}, bf16[8,4,8,512]{3,2,1,0:T(8,128)(2,1)S(1)}, u32[]{:S(2)}, u32[]{:S(2)}) %collective-permute-start.10) | collective-permute-done | bytes 262176 | tf_op jit(solution)/shard_map/ppermute | solution.py:516
  62.9 3.4 %collective-permute-done.9.from_below = bf16[8,4,8,512]{3,2,1,0:T(8,128)(2,1)S(1)} collective-permute-done((bf16[8,4,8,512]{3,2,1,0:T(8,128)(2,1)S(1)}, bf16[8,4,8,512]{3,2,1,0:T(8,128)(2,1)S(1)}, u32[]{:S(2)}, u32[]{:S(2)}) %collective-permute-start.9) | collective-permute-done | bytes 262176 | tf_op jit(solution)/shard_map/ppermute | solution.py:516
  66.3 0.8 shard_map.89
  67.1 9.4 %all-to-all-start = ((bf16[32,8,512]{2,1,0:T(8,128)(2,1)}), bf16[32,8,512]{2,1,0:T(8,128)(2,1)S(1)}, u32[]{:S(2)}, u32[]{:S(2)}) async-start(bf16[32,8,512]{2,1,0:T(8,128)(2,1)} %bitcast.4), calls=%async_computation | async-start | bytes 524288 | tf_op jit(solution)/shard_map/all_to_all | solution.py:563
  76.6 1.6 %shard_map.88 = (bf16[256,1024]{1,0:T(8,128)(2,1)}, bf16[256,1024]{1,0:T(8,128)(2,1)}) custom-call(bf16[256,1024]{1,0:T(8,128)(2,1)S(1)} %bitcast.8, bf16[256,1024]{1,0:T(8,128)(2,1)S(1)} %bitcast.10, bf16[256,1024]{1,0:T(8,128)(2,1)S(1)} %get-tuple-element.71.outs, f32[128,1024]{1,0:T(8,128)S(1)} %get-tuple-element.82.own, ...), custom_call_target="tpu_custom_call" | custom-call | flops 4194304 | bytes 4194304 | tf_op jit(solution)/shard_map/pallas_call | solution.py:481
  78.2 10.0 %all-to-all-done.parts = bf16[32,8,512]{2,1,0:T(8,128)(2,1)S(1)} async-done(((bf16[32,8,512]{2,1,0:T(8,128)(2,1)}), bf16[32,8,512]{2,1,0:T(8,128)(2,1)S(1)}, u32[]{:S(2)}, u32[]{:S(2)}) %all-to-all-start) | async-done | bytes 262176 | tf_op jit(solution)/shard_map/all_to_all | solution.py:563
  88.1 0.7 shard_map.90
  (24 shorter events, 0.3 us)
Async XLA Ops:
  0.6 1.0 %copy-start.1 = (bf16[1,1,256,1024]{3,2,1,0:T(8,128)(2,1)S(1)}, bf16[1,1,256,1024]{3,2,1,0:T(8,128)(2,1)}, u32[]{:S(2)}) copy-start(bf16[1,1,256,1024]{3,2,1,0:T(8,128)(2,1)} %param.5) | copy-start | bytes 1572868
  1.7 5.7 %copy-start.3 = (bf16[1,1,256,1024]{3,2,1,0:T(8,128)(2,1)S(1)}, bf16[1,1,256,1024]{3,2,1,0:T(8,128)(2,1)}, u32[]{:S(2)}) copy-start(bf16[1,1,256,1024]{3,2,1,0:T(8,128)(2,1)} %param.9) | copy-start | bytes 1572868
  1.8 1.6 %collective-permute-start.1 = (bf16[128,1024]{1,0:T(8,128)(2,1)S(1)}, bf16[128,1024]{1,0:T(8,128)(2,1)S(1)}, u32[]{:S(2)}, u32[]{:S(2)}) collective-permute-start(bf16[128,1024]{1,0:T(8,128)(2,1)S(1)} %get-tuple-element.47), channel_id=1, source_target_pairs={{0,1},{1,0},{2,3},{3,2},{4,5},{5,4},{6,7},{7,6},{8,9},{9,8},{10,11... | collective-permute-start | bytes 786440 | tf_op jit(solution)/shard_map/ppermute | solution.py:47
  1.9 7.3 %collective-permute-start = (bf16[128,1024]{1,0:T(8,128)(2,1)S(1)}, bf16[128,1024]{1,0:T(8,128)(2,1)S(1)}, u32[]{:S(2)}, u32[]{:S(2)}) collective-permute-start(bf16[128,1024]{1,0:T(8,128)(2,1)S(1)} %get-tuple-element.47), channel_id=1, source_target_pairs={{1,4},{3,6},{5,8},{7,10},{9,12},{11,14},{13,16},{15,18},{17,20},{1... | collective-permute-start | bytes 786440 | tf_op jit(solution)/shard_map/ppermute | solution.py:47
  3.4 7.0 %slice-start = ((s8[8388608]{0:T(1024)(128)(4,1)}), s8[4194304]{0:T(1024)(128)(4,1)S(1)}, s32[]{:S(2)}) async-start(s8[8388608]{0:T(1024)(128)(4,1)} %bitcast.5), calls=%async_computation.1 | async-start | bytes 8388608
  3.7 12.1 %collective-permute-start.2 = (bf16[256,1024]{1,0:T(8,128)(2,1)S(1)}, bf16[256,1024]{1,0:T(8,128)(2,1)S(1)}, u32[]{:S(2)}, u32[]{:S(2)}) collective-permute-start(bf16[256,1024]{1,0:T(8,128)(2,1)S(1)} %shard_map.77.normed), channel_id=1, source_target_pairs={{0,2},{2,4},{4,6},{6,8},{8,10},{10,12},{12,14},{14,16},{16,18},{18... | collective-permute-start | bytes 1572872 | tf_op jit(solution)/shard_map/ppermute | solution.py:47
  7.4 2.9 %slice-start.1 = ((s8[8388608]{0:T(1024)(128)(4,1)}), s8[4194304]{0:T(1024)(128)(4,1)S(1)}, s32[]{:S(2)}) async-start(s8[8388608]{0:T(1024)(128)(4,1)} %bitcast.5), calls=%async_computation.2 | async-start | bytes 8388608
  7.4 2.9 %copy-start = (bf16[1024,1024]{1,0:T(8,128)(2,1)S(1)}, bf16[1024,1024]{1,0:T(8,128)(2,1)}, u32[]{:S(2)}) copy-start(bf16[1024,1024]{1,0:T(8,128)(2,1)} %weight_out.3) | copy-start | bytes 6291460
  7.5 2.8 %collective-permute-start.3 = (bf16[128,1024]{1,0:T(8,128)(2,1)S(1)}, bf16[128,1024]{1,0:T(8,128)(2,1)S(1)}, u32[]{:S(2)}, u32[]{:S(2)}) collective-permute-start(bf16[128,1024]{1,0:T(8,128)(2,1)S(1)} %get-tuple-element.52), channel_id=1, source_target_pairs={{0,1},{1,0},{2,3},{3,2},{4,5},{5,4},{6,7},{7,6},{8,9},{9,8},{10,11... | collective-permute-start | bytes 786440 | tf_op jit(solution)/shard_map/ppermute | solution.py:47
  15.8 2.7 %copy-start.4 = (s32[1,4]{1,0:T(1,128)S(1)}, s32[1,4]{1,0:T(1,128)}, u32[]{:S(2)}) copy-start(s32[1,4]{1,0:T(1,128)} %lengths.1) | copy-start | bytes 52
  29.7 5.1 %collective-permute-start.4 = (bf16[4,8,4,8,512]{4,3,2,1,0:T(8,128)(2,1)S(1)}, bf16[4,8,4,8,512]{4,3,2,1,0:T(8,128)(2,1)S(1)}, u32[]{:S(2)}, u32[]{:S(2)}) collective-permute-start(bf16[4,8,4,8,512]{4,3,2,1,0:T(8,128)(2,1)S(1)} %get-tuple-element.67), channel_id=1, source_target_pairs={{0,1},{1,0},{2,3},{3,2},{4,5},{5,4},{6,7},{7,6},{8,9},{9,8},{10,11... | collective-permute-start | bytes 3145736 | tf_op jit(solution)/shard_map/ppermute | solution.py:47
  32.5 20.1 %collective-permute-start.8 = (bf16[256,1024]{1,0:T(8,128)(2,1)S(1)}, bf16[256,1024]{1,0:T(8,128)(2,1)S(1)}, u32[]{:S(2)}, u32[]{:S(2)}) collective-permute-start(bf16[256,1024]{1,0:T(8,128)(2,1)S(1)} %get-tuple-element.64), channel_id=1, source_target_pairs={{2,0},{4,2},{6,4},{8,6},{10,8},{12,10},{14,12},{16,14},{18,16},{20... | collective-permute-start | bytes 1572872 | tf_op jit(solution)/shard_map/ppermute | solution.py:47
  33.8 18.8 %collective-permute-start.7 = (bf16[128,1024]{1,0:T(8,128)(2,1)S(1)}, bf16[128,1024]{1,0:T(8,128)(2,1)S(1)}, u32[]{:S(2)}, u32[]{:S(2)}) collective-permute-start(bf16[128,1024]{1,0:T(8,128)(2,1)S(1)} %get-tuple-element.80), channel_id=1, source_target_pairs={{4,1},{6,3},{8,5},{10,7},{12,9},{14,11},{16,13},{18,15},{20,17},{2... | collective-permute-start | bytes 786440 | tf_op jit(solution)/shard_map/ppermute | solution.py:47
  35.4 17.1 %collective-permute-start.5 = (bf16[4,4,8,512]{3,2,1,0:T(8,128)(2,1)S(1)}, bf16[4,4,8,512]{3,2,1,0:T(8,128)(2,1)S(1)}, u32[]{:S(2)}, u32[]{:S(2)}) collective-permute-start(bf16[4,4,8,512]{3,2,1,0:T(8,128)(2,1)S(1)} %get-tuple-element.72), channel_id=1, source_target_pairs={{0,8},{8,16},{16,24},{24,0},{1,9},{9,17},{17,25},{25,1},{2,10},{10... | collective-permute-start | bytes 393224 | tf_op jit(solution)/shard_map/ppermute | solution.py:516
  43.9 8.6 %collective-permute-start.6 = (bf16[4,4,8,512]{3,2,1,0:T(8,128)(2,1)S(1)}, bf16[4,4,8,512]{3,2,1,0:T(8,128)(2,1)S(1)}, u32[]{:S(2)}, u32[]{:S(2)}) collective-permute-start(bf16[4,4,8,512]{3,2,1,0:T(8,128)(2,1)S(1)} %get-tuple-element.73), channel_id=1, source_target_pairs={{0,24},{8,0},{16,8},{24,16},{1,25},{9,1},{17,9},{25,17},{2,26},{10... | collective-permute-start | bytes 393224 | tf_op jit(solution)/shard_map/ppermute | solution.py:516
  52.6 23.9 %copy-start.2 = (bf16[1,1,256,1024]{3,2,1,0:T(8,128)(2,1)S(1)}, bf16[1,1,256,1024]{3,2,1,0:T(8,128)(2,1)}, u32[]{:S(2)}) copy-start(bf16[1,1,256,1024]{3,2,1,0:T(8,128)(2,1)} %param.5) | copy-start | bytes 1572868
  52.7 13.6 %collective-permute-start.11 = (bf16[256,1024]{1,0:T(8,128)(2,1)S(1)}, bf16[256,1024]{1,0:T(8,128)(2,1)S(1)}, u32[]{:S(2)}, u32[]{:S(2)}) collective-permute-start(bf16[256,1024]{1,0:T(8,128)(2,1)S(1)} %get-tuple-element.84), channel_id=1, source_target_pairs={{0,1},{1,0},{2,3},{3,2},{4,5},{5,4},{6,7},{7,6},{8,9},{9,8},{10,11... | collective-permute-start | bytes 1572872 | tf_op jit(solution)/shard_map/ppermute | solution.py:47
  52.8 10.1 %collective-permute-start.10 = (bf16[8,4,8,512]{3,2,1,0:T(8,128)(2,1)S(1)}, bf16[8,4,8,512]{3,2,1,0:T(8,128)(2,1)S(1)}, u32[]{:S(2)}, u32[]{:S(2)}) collective-permute-start(bf16[8,4,8,512]{3,2,1,0:T(8,128)(2,1)S(1)} %get-tuple-element.83), channel_id=1, source_target_pairs={{0,24},{8,0},{16,8},{24,16},{1,25},{9,1},{17,9},{25,17},{2,26},{10... | collective-permute-start | bytes 786440 | tf_op jit(solution)/shard_map/ppermute | solution.py:516
  56.7 9.6 %collective-permute-start.9 = (bf16[8,4,8,512]{3,2,1,0:T(8,128)(2,1)S(1)}, bf16[8,4,8,512]{3,2,1,0:T(8,128)(2,1)S(1)}, u32[]{:S(2)}, u32[]{:S(2)}) collective-permute-start(bf16[8,4,8,512]{3,2,1,0:T(8,128)(2,1)S(1)} %get-tuple-element.79), channel_id=1, source_target_pairs={{0,8},{8,16},{16,24},{24,0},{1,9},{9,17},{17,25},{25,1},{2,10},{10... | collective-permute-start | bytes 786440 | tf_op jit(solution)/shard_map/ppermute | solution.py:516
  67.1 21.0 %all-to-all-start = ((bf16[32,8,512]{2,1,0:T(8,128)(2,1)}), bf16[32,8,512]{2,1,0:T(8,128)(2,1)S(1)}, u32[]{:S(2)}, u32[]{:S(2)}) async-start(bf16[32,8,512]{2,1,0:T(8,128)(2,1)} %bitcast.4), calls=%async_computation | async-start | bytes 524288 | tf_op jit(solution)/shard_map/all_to_all | solution.py:563
